TPU v7x, 32 devices: a whole 2x2x4 slice. The times are simulated.
32 devices in a mesh: row: 4 (over y, x), col: 8 (over z, core).
Axes of the slice: x: 2, y: 2, z: 4, core: 2. Of those that a mesh axis runs over, the one named last changes fastest.
Arguments:
- elevation: float32 [2048, 8192], P('row', 'col'), may hold values from -6 to 6
- ocean: int32 [2048, 8192], P('row', 'col'), may hold values from 0 to 1, as said below
- outlet: int32 [2048, 8192], P('row', 'col'), may hold values from 0 to 1, as said below
Outputs:
- surface: float32 [2048, 8192], P('row', 'col')
Inputs may be any that keep to these rules, and one draw needn't show every extreme that they name: ocean cells are scattered; no bound on their count in any region may be assumed. outlet cells are scattered; no bound on their count in any region may be assumed.
All inputs are finite; a program needn't handle non-finite values.
Results may differ from a plain program's by a relative error of at most 0.00002.
Values sent between devices are 32-bit elements; how exact they have to be, the bound alone decides.
No kernel may reach another device: no remote copies, remote signals or barrier semaphores. Data moves between devices by JAX's collectives and lax.ppermute only.
A program may use at most 128 MiB of HBM per device.

v0:
```python
import jax
import jax.numpy as jnp
from jax import lax
from jax.sharding import PartitionSpec as P

BLK = 16
COARSE = 4
FINE = 8


huge_level = 1e30
fine_step = 2.0 ** (-10)
coarse_step = 2.0 ** (-6)


def extended_2(block, sides, width):
    for axis, dim in sides:
        count = lax.axis_size(axis)
        forward = [(i, i + 1) for i in range(count - 1)]
        forward.append((count - 1, 0))
        backward = [(target, source) for source, target in forward]
        low = lax.ppermute(
            lax.slice_in_dim(block, block.shape[dim] - width, None, axis=dim), axis, forward
        )
        high = lax.ppermute(lax.slice_in_dim(block, 0, width, axis=dim), axis, backward)
        block = jnp.concatenate([low, block, high], axis=dim)
    return block


def neighbour_min(extended):
    height = extended.shape[0] - 2
    width = extended.shape[1] - 2
    result = None
    for down in range(3):
        for across in range(3):
            if down == 1 and across == 1:
                continue
            piece = extended[down : down + height, across : across + width]
            result = piece if result is None else jnp.minimum(result, piece)
    return result


def update(extended, ground, lock, step_size):
    center = extended[1:-1, 1:-1]
    lowered = jnp.minimum(center, neighbour_min(extended) + step_size)
    return jnp.minimum(jnp.maximum(ground, lowered), lock)


def seal(extended, margin):
    row_pos = lax.axis_index("row")
    row_count = lax.axis_size("row")
    row_dim = extended.ndim - 2
    row_iota = lax.broadcasted_iota(jnp.int32, extended.shape, row_dim)
    north_edge = (row_iota < margin) & (row_pos == 0)
    south_edge = (row_iota >= extended.shape[row_dim] - margin) & (row_pos == row_count - 1)
    return jnp.where(north_edge | south_edge, jnp.float32(huge_level), extended)


def coarse_sweep(coarse, ground_c, lock_c):
    extended = extended_2(coarse, (("row", 0), ("col", 1)), 1)
    return update(seal(extended, 1), ground_c, lock_c, coarse_step)


def shrink_sweeps(banded, count, step_size):
    current = banded[0]
    band_ground = banded[1]
    band_lock = banded[2]
    full_rows = band_ground.shape[0]
    full_cols = band_ground.shape[1]
    for sweep in range(count):
        inset = sweep + 1
        inner_ground = band_ground[inset : full_rows - inset, inset : full_cols - inset]
        inner_lock = band_lock[inset : full_rows - inset, inset : full_cols - inset]
        current = update(current, inner_ground, inner_lock, step_size)
    return current


def shards(elevation, ocean, outlet):
    ground = jnp.where(ocean == 1, jnp.float32(0.0), elevation)
    drains = (ocean == 1) | (outlet == 1)
    lock = jnp.where(drains, ground, jnp.float32(huge_level))
    tile_rows, tile_cols = elevation.shape
    coarse_rows = tile_rows // BLK
    coarse_cols = tile_cols // BLK
    shape_blocks = (coarse_rows, BLK, coarse_cols, BLK)
    ground_c = ground.reshape(shape_blocks).min(axis=(1, 3))
    lock_c = lock.reshape(shape_blocks).min(axis=(1, 3))
    coarse = ground.reshape(shape_blocks).max(axis=(1, 3))
    for sweep in range(COARSE):
        coarse = coarse_sweep(coarse, ground_c, lock_c)
    lifted = jnp.broadcast_to(coarse[:, None, :, None], shape_blocks).reshape(tile_rows, tile_cols)
    surface = jnp.minimum(jnp.maximum(ground, lifted), lock)
    stacked = jnp.stack([surface, ground, lock])
    banded = extended_2(stacked, (("row", 1), ("col", 2)), FINE)
    surface = shrink_sweeps(seal(banded, FINE), FINE, fine_step)
    return surface


def solution(mesh):
    return jax.shard_map(
        shards,
        mesh=mesh,
        in_specs=(P("row", "col"), P("row", "col"), P("row", "col")),
        out_specs=P("row", "col"),
        check_vma=False,
    )
```

profile of v0, /device:TPU:0, one launch (start us, length us, event | category | flops | bytes accessed | tf_op | source)
XLA Modules:
  0.0 179.0 jit_solution(3976363296850570579)
XLA Ops:
  0.0 5.4 %or_select_fusion = (f32[512,1024]{1,0:T(8,128)S(1)}, f32[512,1024]{1,0:T(8,128)}) fusion(s32[512,1024]{1,0:T(8,128)} %param.5, f32[512,1024]{1,0:T(8,128)} %param.3, s32[512,1024]{1,0:T(8,128)} %param.4), kind=kLoop, calls=%fused_computation.94 | loop fusion | flops 2621440 | bytes 10485760 | tf_op jit(solution)/shard_map/jit(_where)/select_n | solution.py:81
  5.4 10.4 %reshape.11 = f32[32,16,64,16]{3,2,1,0:T(8,128)} reshape(f32[512,1024]{1,0:T(8,128)} %get-tuple-element.8) | data formatting | bytes 4194304 | tf_op jit(solution)/shard_map/reshape | solution.py:86
  15.8 8.3 %fusion.43 = (f32[32,64]{1,0:T(8,128)S(1)}, f32[32,64]{1,0:T(8,128)S(1)}) fusion(f32[32,16,64,16]{3,2,1,0:T(8,128)} %reshape.11), kind=kLoop, calls=%fused_computation.158 | loop fusion | flops 1044480 | bytes 2113536 | tf_op jit(solution)/shard_map/reduce_max | solution.py:88
  24.1 3.0 %collective-permute-start = (f32[1,64]{1,0:T(1,128)S(1)}, f32[1,64]{1,0:T(1,128)S(1)}, u32[]{:S(2)}, u32[]{:S(2)}) collective-permute-start(f32[1,64]{1,0:T(1,128)S(1)} %get-tuple-element.30), channel_id=1, source_target_pairs={{0,8},{8,16},{16,24},{24,0},{1,9},{9,17},{17,25},{25,1},{2,10},{10... | collective-permute-start | bytes 776 | tf_op jit(solution)/shard_map/ppermute | solution.py:22
  27.1 1.0 collective-permute-start.1
  28.1 9.0 %reshape.12 = f32[32,16,64,16]{3,2,1,0:T(8,128)} reshape(f32[512,1024]{1,0:T(8,128)S(1)} %get-tuple-element.7) | data formatting | bytes 4194304 | tf_op jit(solution)/shard_map/reshape | solution.py:87
  37.2 3.5 %collective-permute-start.3 = (f32[34,1]{1,0:T(8,128)S(1)}, f32[34,1]{1,0:T(8,128)S(1)}, u32[]{:S(2)}, u32[]{:S(2)}) collective-permute-start(f32[34,1]{1,0:T(8,128)S(1)} %get-tuple-element.23), channel_id=1, source_target_pairs={{1,0},{2,1},{3,2},{4,3},{5,4},{6,5},{7,6},{0,7},{9,8},{10,9},{11,1... | collective-permute-start | bytes 416 | tf_op jit(solution)/shard_map/ppermute | solution.py:25
  40.8 7.0 %reduce_min.19 = f32[32,64]{1,0:T(8,128)S(1)} reduce(f32[32,16,64,16]{3,2,1,0:T(8,128)} %reshape.12, f32[]{:T(128)} %constant.21.clone.1), dimensions={1,3}, to_apply=%region_2.3 | reduce | flops 522240 | bytes 2105348 | tf_op jit(solution)/shard_map/reduce_min | solution.py:87
  48.0 1.1 collective-permute-start.4
  49.1 1.9 %collective-permute-start.5 = (f32[1,64]{1,0:T(1,128)S(1)}, f32[1,64]{1,0:T(1,128)S(1)}, u32[]{:S(2)}, u32[]{:S(2)}) collective-permute-start(f32[1,64]{1,0:T(1,128)S(1)} %get-tuple-element.29), channel_id=1, source_target_pairs={{8,0},{16,8},{24,16},{0,24},{9,1},{17,9},{25,17},{1,25},{10,2},{18... | collective-permute-start | bytes 776 | tf_op jit(solution)/shard_map/ppermute | solution.py:25
  51.0 1.5 collective-permute-done.4
  52.5 0.5 collective-permute-done.5
  53.1 3.5 %collective-permute-start.7 = (f32[34,1]{1,0:T(8,128)S(1)}, f32[34,1]{1,0:T(8,128)S(1)}, u32[]{:S(2)}, u32[]{:S(2)}) collective-permute-start(f32[34,1]{1,0:T(8,128)S(1)} %get-tuple-element.21), channel_id=1, source_target_pairs={{1,0},{2,1},{3,2},{4,3},{5,4},{6,5},{7,6},{0,7},{9,8},{10,9},{11,1... | collective-permute-start | bytes 416 | tf_op jit(solution)/shard_map/ppermute | solution.py:25
  56.6 1.5 collective-permute-done.6
  58.3 3.0 %collective-permute-start.8 = (f32[1,64]{1,0:T(1,128)S(1)}, f32[1,64]{1,0:T(1,128)S(1)}, u32[]{:S(2)}, u32[]{:S(2)}) collective-permute-start(f32[1,64]{1,0:T(1,128)S(1)} %get-tuple-element.26), channel_id=1, source_target_pairs={{0,8},{8,16},{16,24},{24,0},{1,9},{9,17},{17,25},{25,1},{2,10},{10... | collective-permute-start | bytes 776 | tf_op jit(solution)/shard_map/ppermute | solution.py:22
  61.3 1.5 collective-permute-done.8
  62.8 2.0 %collective-permute-done.9 = f32[1,64]{1,0:T(1,128)S(1)} collective-permute-done((f32[1,64]{1,0:T(1,128)S(1)}, f32[1,64]{1,0:T(1,128)S(1)}, u32[]{:S(2)}, u32[]{:S(2)}) %collective-permute-start.9) | collective-permute-done | bytes 288 | tf_op jit(solution)/shard_map/ppermute | solution.py:25
  64.9 3.5 %collective-permute-start.11 = (f32[34,1]{1,0:T(8,128)S(1)}, f32[34,1]{1,0:T(8,128)S(1)}, u32[]{:S(2)}, u32[]{:S(2)}) collective-permute-start(f32[34,1]{1,0:T(8,128)S(1)} %get-tuple-element.19), channel_id=1, source_target_pairs={{1,0},{2,1},{3,2},{4,3},{5,4},{6,5},{7,6},{0,7},{9,8},{10,9},{11,1... | collective-permute-start | bytes 416 | tf_op jit(solution)/shard_map/ppermute | solution.py:25
  68.5 1.5 collective-permute-done.10
  70.1 1.0 collective-permute-start.12
  71.2 2.0 %collective-permute-start.13 = (f32[1,64]{1,0:T(1,128)S(1)}, f32[1,64]{1,0:T(1,128)S(1)}, u32[]{:S(2)}, u32[]{:S(2)}) collective-permute-start(f32[1,64]{1,0:T(1,128)S(1)} %get-tuple-element.25), channel_id=1, source_target_pairs={{8,0},{16,8},{24,16},{0,24},{9,1},{17,9},{25,17},{1,25},{10,2},{18... | collective-permute-start | bytes 776 | tf_op jit(solution)/shard_map/ppermute | solution.py:25
  73.1 1.5 collective-permute-done.12
  74.8 3.5 %collective-permute-start.15 = (f32[34,1]{1,0:T(8,128)S(1)}, f32[34,1]{1,0:T(8,128)S(1)}, u32[]{:S(2)}, u32[]{:S(2)}) collective-permute-start(f32[34,1]{1,0:T(8,128)S(1)} %get-tuple-element.17), channel_id=1, source_target_pairs={{1,0},{2,1},{3,2},{4,3},{5,4},{6,5},{7,6},{0,7},{9,8},{10,9},{11,1... | collective-permute-start | bytes 416 | tf_op jit(solution)/shard_map/ppermute | solution.py:25
  78.3 1.5 collective-permute-done.14
  80.0 7.9 %broadcast_in_dim.29 = f32[32,16,64,16]{3,2,1,0:T(8,128)} broadcast(f32[32,64]{1,0:T(8,128)S(1)} %fusion.27), dimensions={0,2} | broadcast | bytes 2105344 | tf_op jit(solution)/shard_map/broadcast_in_dim | solution.py:91
  87.9 15.2 %reshape.13 = f32[512,1024]{1,0:T(8,128)} reshape(f32[32,16,64,16]{3,2,1,0:T(8,128)} %broadcast_in_dim.29) | data formatting | bytes 4194304 | tf_op jit(solution)/shard_map/reshape | solution.py:91
  103.2 3.0 %minimum_bitcast_fusion = f32[1,512,1024]{2,1,0:T(8,128)S(1)} fusion(f32[512,1024]{1,0:T(8,128)S(1)} %get-tuple-element.7, f32[512,1024]{1,0:T(8,128)} %get-tuple-element.8, f32[512,1024]{1,0:T(8,128)} %reshape.13), kind=kLoop, calls=%fused_computation.93 | loop fusion | flops 1048576 | bytes 8388608 | tf_op jit(solution)/shard_map/stack | solution.py:93
  106.2 1.5 collective-permute-start.16
  107.8 1.6 collective-permute-start.17
  109.4 2.4 %collective-permute-done.16 = f32[3,8,1024]{2,1,0:T(8,128)S(1)} collective-permute-done((f32[3,8,1024]{2,1,0:T(8,128)S(1)}, f32[3,8,1024]{2,1,0:T(8,128)S(1)}, u32[]{:S(2)}, u32[]{:S(2)}) %collective-permute-start.16) | collective-permute-done | bytes 98336 | tf_op jit(solution)/shard_map/ppermute | solution.py:22
  111.8 0.6 collective-permute-done.17
  112.4 1.0 pad_maximum_fusion
  113.5 2.8 %copy-done.1 = f32[3,528,1024]{2,1,0:T(8,128)} copy-done((f32[3,528,1024]{2,1,0:T(8,128)}, f32[3,528,1024]{2,1,0:T(8,128)S(1)}, u32[]{:S(2)}) %copy-start.1) | copy-done | bytes 6488088
  116.2 0.3 fusion.44
  116.8 0.3 copy.4
  117.2 3.5 %collective-permute-start.19 = (f32[3,528,8]{1,2,0:T(8,128)S(1)}, f32[3,528,8]{1,2,0:T(8,128)S(1)}, u32[]{:S(2)}, u32[]{:S(2)}) collective-permute-start(f32[3,528,8]{1,2,0:T(8,128)S(1)} %copy.5), channel_id=1, source_target_pairs={{1,0},{2,1},{3,2},{4,3},{5,4},{6,5},{7,6},{0,7},{9,8},{10,9},{11,1... | collective-permute-start | bytes 152072 | tf_op jit(solution)/shard_map/ppermute | solution.py:25
  120.7 1.9 %collective-permute-done.19 = f32[3,528,8]{1,2,0:T(8,128)S(1)} collective-permute-done((f32[3,528,8]{1,2,0:T(8,128)S(1)}, f32[3,528,8]{1,2,0:T(8,128)S(1)}, u32[]{:S(2)}, u32[]{:S(2)}) %collective-permute-start.19) | collective-permute-done | bytes 50720 | tf_op jit(solution)/shard_map/ppermute | solution.py:25
  123.1 9.1 %concatenate.39 = f32[3,528,1040]{2,1,0:T(8,128)} concatenate(f32[3,528,8]{2,1,0:T(8,128)S(1)} %copy.6, f32[3,528,1024]{2,1,0:T(8,128)} %copy-done.1, f32[3,528,8]{2,1,0:T(8,128)S(1)} %copy.7), dimensions={2} | concatenate | bytes 13178880 | tf_op jit(solution)/shard_map/concatenate | solution.py:26
  132.3 3.8 %broadcast_select_fusion = f32[3,528,1040]{2,1,0:T(8,128)S(1)} fusion(f32[3,528,1040]{2,1,0:T(8,128)} %concatenate.39, pred[528]{0:T(1024)(128)(4,1)S(1)} %fusion.41), kind=kLoop, calls=%fused_computation.1 | loop fusion | flops 1647360 | bytes 13179408 | tf_op jit(solution)/shard_map/jit(_where)/select_n | solution.py:56
  136.1 0.5 slice_bitcast_fusion.2
  136.6 5.2 %slice_minimum_fusion.16 = f32[526,1038]{1,0:T(8,128)S(1)} fusion(f32[528,1040]{1,0:T(8,128)S(1)} %get-tuple-element.10, f32[528,1040]{1,0:T(8,128)S(1)} %get-tuple-element.11, f32[528,1040]{1,0:T(8,128)S(1)} %get-tuple-element.9), kind=kLoop, calls=%fused_computation.24 | loop fusion | flops 6005868 | bytes 26207424 | tf_op jit(solution)/shard_map/min | solution.py:46
  141.8 5.3 %slice_minimum_fusion.8 = f32[524,1036]{1,0:T(8,128)S(1)} fusion(f32[528,1040]{1,0:T(8,128)S(1)} %get-tuple-element.10, f32[526,1038]{1,0:T(8,128)S(1)} %slice_minimum_fusion.16, f32[528,1040]{1,0:T(8,128)S(1)} %get-tuple-element.9), kind=kLoop, calls=%fused_computation.13 | loop fusion | flops 5971504 | bytes 26057472 | tf_op jit(solution)/shard_map/min | solution.py:46
  147.1 5.2 %slice_minimum_fusion = f32[522,1034]{1,0:T(8,128)S(1)} fusion(f32[528,1040]{1,0:T(8,128)S(1)} %get-tuple-element.10, f32[524,1036]{1,0:T(8,128)S(1)} %slice_minimum_fusion.8, f32[528,1040]{1,0:T(8,128)S(1)} %get-tuple-element.9), kind=kLoop, calls=%fused_computation.2 | loop fusion | flops 5937228 | bytes 25907904 | tf_op jit(solution)/shard_map/min | solution.py:46
  152.3 5.5 %slice_minimum_fusion.48 = f32[520,1032]{1,0:T(8,128)S(1)} fusion(f32[528,1040]{1,0:T(8,128)S(1)} %get-tuple-element.10, f32[522,1034]{1,0:T(8,128)S(1)} %slice_minimum_fusion, f32[528,1040]{1,0:T(8,128)S(1)} %get-tuple-element.9), kind=kLoop, calls=%fused_computation.71 | loop fusion | flops 5903040 | bytes 25758720 | tf_op jit(solution)/shard_map/min | solution.py:46
  157.8 5.2 %slice_minimum_fusion.40 = f32[518,1030]{1,0:T(8,128)S(1)} fusion(f32[528,1040]{1,0:T(8,128)S(1)} %get-tuple-element.10, f32[520,1032]{1,0:T(8,128)S(1)} %slice_minimum_fusion.48, f32[528,1040]{1,0:T(8,128)S(1)} %get-tuple-element.9), kind=kLoop, calls=%fused_computation.60 | loop fusion | flops 5868940 | bytes 25609920 | tf_op jit(solution)/shard_map/min | solution.py:46
  163.0 5.2 %slice_minimum_fusion.32 = f32[516,1028]{1,0:T(8,128)S(1)} fusion(f32[528,1040]{1,0:T(8,128)S(1)} %get-tuple-element.10, f32[518,1030]{1,0:T(8,128)S(1)} %slice_minimum_fusion.40, f32[528,1040]{1,0:T(8,128)S(1)} %get-tuple-element.9), kind=kLoop, calls=%fused_computation.49 | loop fusion | flops 5834928 | bytes 25461504 | tf_op jit(solution)/shard_map/min | solution.py:46
  168.3 5.2 %slice_minimum_fusion.24 = f32[514,1026]{1,0:T(8,128)S(1)} fusion(f32[528,1040]{1,0:T(8,128)S(1)} %get-tuple-element.10, f32[516,1028]{1,0:T(8,128)S(1)} %slice_minimum_fusion.32, f32[528,1040]{1,0:T(8,128)S(1)} %get-tuple-element.9), kind=kLoop, calls=%fused_computation.38 | loop fusion | flops 5801004 | bytes 25313472 | tf_op jit(solution)/shard_map/min | solution.py:46
  173.5 5.5 %slice_minimum_fusion.56 = f32[512,1024]{1,0:T(8,128)} fusion(f32[528,1040]{1,0:T(8,128)S(1)} %get-tuple-element.10, f32[514,1026]{1,0:T(8,128)S(1)} %slice_minimum_fusion.24, f32[528,1040]{1,0:T(8,128)S(1)} %get-tuple-element.9), kind=kLoop, calls=%fused_computation.82 | loop fusion | flops 5767168 | bytes 25165824 | tf_op jit(solution)/shard_map/min | solution.py:46
  (44 shorter events, 2.1 us)
Async XLA Ops:
  24.1 13.0 %collective-permute-start = (f32[1,64]{1,0:T(1,128)S(1)}, f32[1,64]{1,0:T(1,128)S(1)}, u32[]{:S(2)}, u32[]{:S(2)}) collective-permute-start(f32[1,64]{1,0:T(1,128)S(1)} %get-tuple-element.30), channel_id=1, source_target_pairs={{0,8},{8,16},{16,24},{24,0},{1,9},{9,17},{17,25},{25,1},{2,10},{10... | collective-permute-start | bytes 776 | tf_op jit(solution)/shard_map/ppermute | solution.py:22
  27.1 10.0 %collective-permute-start.1 = (f32[1,64]{1,0:T(1,128)S(1)}, f32[1,64]{1,0:T(1,128)S(1)}, u32[]{:S(2)}, u32[]{:S(2)}) collective-permute-start(f32[1,64]{1,0:T(1,128)S(1)} %get-tuple-element.31), channel_id=1, source_target_pairs={{8,0},{16,8},{24,16},{0,24},{9,1},{17,9},{25,17},{1,25},{10,2},{18... | collective-permute-start | bytes 776 | tf_op jit(solution)/shard_map/ppermute | solution.py:25
  37.2 10.6 %collective-permute-start.2 = (f32[34,1]{1,0:T(8,128)S(1)}, f32[34,1]{1,0:T(8,128)S(1)}, u32[]{:S(2)}, u32[]{:S(2)}) collective-permute-start(f32[34,1]{1,0:T(8,128)S(1)} %get-tuple-element.22), channel_id=1, source_target_pairs={{0,1},{1,2},{2,3},{3,4},{4,5},{5,6},{6,7},{7,0},{8,9},{9,10},{10,1... | collective-permute-start | bytes 416 | tf_op jit(solution)/shard_map/ppermute | solution.py:22
  37.2 10.6 %collective-permute-start.3 = (f32[34,1]{1,0:T(8,128)S(1)}, f32[34,1]{1,0:T(8,128)S(1)}, u32[]{:S(2)}, u32[]{:S(2)}) collective-permute-start(f32[34,1]{1,0:T(8,128)S(1)} %get-tuple-element.23), channel_id=1, source_target_pairs={{1,0},{2,1},{3,2},{4,3},{5,4},{6,5},{7,6},{0,7},{9,8},{10,9},{11,1... | collective-permute-start | bytes 416 | tf_op jit(solution)/shard_map/ppermute | solution.py:25
  48.0 4.5 %collective-permute-start.4 = (f32[1,64]{1,0:T(1,128)S(1)}, f32[1,64]{1,0:T(1,128)S(1)}, u32[]{:S(2)}, u32[]{:S(2)}) collective-permute-start(f32[1,64]{1,0:T(1,128)S(1)} %get-tuple-element.28), channel_id=1, source_target_pairs={{0,8},{8,16},{16,24},{24,0},{1,9},{9,17},{17,25},{25,1},{2,10},{10... | collective-permute-start | bytes 776 | tf_op jit(solution)/shard_map/ppermute | solution.py:22
  49.1 3.9 %collective-permute-start.5 = (f32[1,64]{1,0:T(1,128)S(1)}, f32[1,64]{1,0:T(1,128)S(1)}, u32[]{:S(2)}, u32[]{:S(2)}) collective-permute-start(f32[1,64]{1,0:T(1,128)S(1)} %get-tuple-element.29), channel_id=1, source_target_pairs={{8,0},{16,8},{24,16},{0,24},{9,1},{17,9},{25,17},{1,25},{10,2},{18... | collective-permute-start | bytes 776 | tf_op jit(solution)/shard_map/ppermute | solution.py:25
  53.1 5.0 %collective-permute-start.6 = (f32[34,1]{1,0:T(8,128)S(1)}, f32[34,1]{1,0:T(8,128)S(1)}, u32[]{:S(2)}, u32[]{:S(2)}) collective-permute-start(f32[34,1]{1,0:T(8,128)S(1)} %get-tuple-element.20), channel_id=1, source_target_pairs={{0,1},{1,2},{2,3},{3,4},{4,5},{5,6},{6,7},{7,0},{8,9},{9,10},{10,1... | collective-permute-start | bytes 416 | tf_op jit(solution)/shard_map/ppermute | solution.py:22
  53.1 5.0 %collective-permute-start.7 = (f32[34,1]{1,0:T(8,128)S(1)}, f32[34,1]{1,0:T(8,128)S(1)}, u32[]{:S(2)}, u32[]{:S(2)}) collective-permute-start(f32[34,1]{1,0:T(8,128)S(1)} %get-tuple-element.21), channel_id=1, source_target_pairs={{1,0},{2,1},{3,2},{4,3},{5,4},{6,5},{7,6},{0,7},{9,8},{10,9},{11,1... | collective-permute-start | bytes 416 | tf_op jit(solution)/shard_map/ppermute | solution.py:25
  58.3 4.5 %collective-permute-start.8 = (f32[1,64]{1,0:T(1,128)S(1)}, f32[1,64]{1,0:T(1,128)S(1)}, u32[]{:S(2)}, u32[]{:S(2)}) collective-permute-start(f32[1,64]{1,0:T(1,128)S(1)} %get-tuple-element.26), channel_id=1, source_target_pairs={{0,8},{8,16},{16,24},{24,0},{1,9},{9,17},{17,25},{25,1},{2,10},{10... | collective-permute-start | bytes 776 | tf_op jit(solution)/shard_map/ppermute | solution.py:22
  61.3 3.5 %collective-permute-start.9 = (f32[1,64]{1,0:T(1,128)S(1)}, f32[1,64]{1,0:T(1,128)S(1)}, u32[]{:S(2)}, u32[]{:S(2)}) collective-permute-start(f32[1,64]{1,0:T(1,128)S(1)} %get-tuple-element.27), channel_id=1, source_target_pairs={{8,0},{16,8},{24,16},{0,24},{9,1},{17,9},{25,17},{1,25},{10,2},{18... | collective-permute-start | bytes 776 | tf_op jit(solution)/shard_map/ppermute | solution.py:25
  64.9 5.0 %collective-permute-start.10 = (f32[34,1]{1,0:T(8,128)S(1)}, f32[34,1]{1,0:T(8,128)S(1)}, u32[]{:S(2)}, u32[]{:S(2)}) collective-permute-start(f32[34,1]{1,0:T(8,128)S(1)} %get-tuple-element.18), channel_id=1, source_target_pairs={{0,1},{1,2},{2,3},{3,4},{4,5},{5,6},{6,7},{7,0},{8,9},{9,10},{10,1... | collective-permute-start | bytes 416 | tf_op jit(solution)/shard_map/ppermute | solution.py:22
  64.9 5.0 %collective-permute-start.11 = (f32[34,1]{1,0:T(8,128)S(1)}, f32[34,1]{1,0:T(8,128)S(1)}, u32[]{:S(2)}, u32[]{:S(2)}) collective-permute-start(f32[34,1]{1,0:T(8,128)S(1)} %get-tuple-element.19), channel_id=1, source_target_pairs={{1,0},{2,1},{3,2},{4,3},{5,4},{6,5},{7,6},{0,7},{9,8},{10,9},{11,1... | collective-permute-start | bytes 416 | tf_op jit(solution)/shard_map/ppermute | solution.py:25
  70.1 4.5 %collective-permute-start.12 = (f32[1,64]{1,0:T(1,128)S(1)}, f32[1,64]{1,0:T(1,128)S(1)}, u32[]{:S(2)}, u32[]{:S(2)}) collective-permute-start(f32[1,64]{1,0:T(1,128)S(1)} %get-tuple-element.24), channel_id=1, source_target_pairs={{0,8},{8,16},{16,24},{24,0},{1,9},{9,17},{17,25},{25,1},{2,10},{10... | collective-permute-start | bytes 776 | tf_op jit(solution)/shard_map/ppermute | solution.py:22
  71.2 3.5 %collective-permute-start.13 = (f32[1,64]{1,0:T(1,128)S(1)}, f32[1,64]{1,0:T(1,128)S(1)}, u32[]{:S(2)}, u32[]{:S(2)}) collective-permute-start(f32[1,64]{1,0:T(1,128)S(1)} %get-tuple-element.25), channel_id=1, source_target_pairs={{8,0},{16,8},{24,16},{0,24},{9,1},{17,9},{25,17},{1,25},{10,2},{18... | collective-permute-start | bytes 776 | tf_op jit(solution)/shard_map/ppermute | solution.py:25
  74.8 5.0 %collective-permute-start.14 = (f32[34,1]{1,0:T(8,128)S(1)}, f32[34,1]{1,0:T(8,128)S(1)}, u32[]{:S(2)}, u32[]{:S(2)}) collective-permute-start(f32[34,1]{1,0:T(8,128)S(1)} %get-tuple-element.16), channel_id=1, source_target_pairs={{0,1},{1,2},{2,3},{3,4},{4,5},{5,6},{6,7},{7,0},{8,9},{9,10},{10,1... | collective-permute-start | bytes 416 | tf_op jit(solution)/shard_map/ppermute | solution.py:22
  74.8 5.0 %collective-permute-start.15 = (f32[34,1]{1,0:T(8,128)S(1)}, f32[34,1]{1,0:T(8,128)S(1)}, u32[]{:S(2)}, u32[]{:S(2)}) collective-permute-start(f32[34,1]{1,0:T(8,128)S(1)} %get-tuple-element.17), channel_id=1, source_target_pairs={{1,0},{2,1},{3,2},{4,3},{5,4},{6,5},{7,6},{0,7},{9,8},{10,9},{11,1... | collective-permute-start | bytes 416 | tf_op jit(solution)/shard_map/ppermute | solution.py:25
  103.2 3.0 %copy-start = (f32[512,1024]{1,0:T(8,128)S(1)}, f32[512,1024]{1,0:T(8,128)}, u32[]{:S(2)}) copy-start(f32[512,1024]{1,0:T(8,128)} %get-tuple-element.8) | copy-start | bytes 6291460
  106.2 5.6 %collective-permute-start.16 = (f32[3,8,1024]{2,1,0:T(8,128)S(1)}, f32[3,8,1024]{2,1,0:T(8,128)S(1)}, u32[]{:S(2)}, u32[]{:S(2)}) collective-permute-start(f32[3,8,1024]{2,1,0:T(8,128)S(1)} %get-tuple-element.14), channel_id=1, source_target_pairs={{0,8},{8,16},{16,24},{24,0},{1,9},{9,17},{17,25},{25,1},{2,10},{10... | collective-permute-start | bytes 294920 | tf_op jit(solution)/shard_map/ppermute | solution.py:22
  107.8 4.6 %collective-permute-start.17 = (f32[3,8,1024]{2,1,0:T(8,128)S(1)}, f32[3,8,1024]{2,1,0:T(8,128)S(1)}, u32[]{:S(2)}, u32[]{:S(2)}) collective-permute-start(f32[3,8,1024]{2,1,0:T(8,128)S(1)} %get-tuple-element.15), channel_id=1, source_target_pairs={{8,0},{16,8},{24,16},{0,24},{9,1},{17,9},{25,17},{1,25},{10,2},{18... | collective-permute-start | bytes 294920 | tf_op jit(solution)/shard_map/ppermute | solution.py:25
  113.5 2.8 %copy-start.1 = (f32[3,528,1024]{2,1,0:T(8,128)}, f32[3,528,1024]{2,1,0:T(8,128)S(1)}, u32[]{:S(2)}) copy-start(f32[3,528,1024]{2,1,0:T(8,128)S(1)} %pad_maximum_fusion) | copy-start | bytes 19464196
  117.1 5.7 %collective-permute-start.18 = (f32[3,528,8]{1,2,0:T(8,128)S(1)}, f32[3,528,8]{1,2,0:T(8,128)S(1)}, u32[]{:S(2)}, u32[]{:S(2)}) collective-permute-start(f32[3,528,8]{1,2,0:T(8,128)S(1)} %copy.4), channel_id=1, source_target_pairs={{0,1},{1,2},{2,3},{3,4},{4,5},{5,6},{6,7},{7,0},{8,9},{9,10},{10,1... | collective-permute-start | bytes 152072 | tf_op jit(solution)/shard_map/ppermute | solution.py:22
  117.2 5.4 %collective-permute-start.19 = (f32[3,528,8]{1,2,0:T(8,128)S(1)}, f32[3,528,8]{1,2,0:T(8,128)S(1)}, u32[]{:S(2)}, u32[]{:S(2)}) collective-permute-start(f32[3,528,8]{1,2,0:T(8,128)S(1)} %copy.5), channel_id=1, source_target_pairs={{1,0},{2,1},{3,2},{4,3},{5,4},{6,5},{7,6},{0,7},{9,8},{10,9},{11,1... | collective-permute-start | bytes 152072 | tf_op jit(solution)/shard_map/ppermute | solution.py:25
where the time goes:
time: 180 us; the launch traced here: 179 us
  other arithmetic  71.7 us (40%)
  local copies, waits for them, and re-layouts  56.7 us (32%)
  starting transfers between devices  33.8 us (19%)
  waiting for transfers between devices  16.4 us (9%)
    min x12, other arithmetic, update(): return jnp.minimum(jnp.maximum(ground, lowered), lock)  42.7 us
    ppermute x10, starting transfers between devices, extended_2(): lax.ppermute(lax.slice_in_dim(block, 0, width, axis=dim), axis, backward)  24.2 us
    reshape x1, local copies, waits for them, and re-layouts, shards(): jnp.broadcast_to(coarse[:, None, :, None], shape_blocks)  15.2 us
    ppermute x10, waiting for transfers between devices, extended_2(): lax.ppermute(lax.slice_in_dim(block, block.shape[dim] - width, None, axis...  11.3 us
    reshape x1, local copies, waits for them, and re-layouts, shards(): ground_c = ground.reshape(shape_blocks).min(axis=(1, 3))  10.4 us
    ppermute x10, starting transfers between devices, extended_2(): lax.ppermute(lax.slice_in_dim(block, block.shape[dim] - width, None, axis...  9.62 us
    concatenate x1, local copies, waits for them, and re-layouts, extended_2(): block = jnp.concatenate([low, block, high], axis=dim)  9.15 us
    reshape x1, local copies, waits for them, and re-layouts, shards(): lock_c = lock.reshape(shape_blocks).min(axis=(1, 3))  9.01 us
  transfers between devices with their start and end apart: 20, of which 12 were waited for; matrix products, arithmetic and copies ran while one was open for 9% of the time, Pallas kernels for 0%

commit v1 on v0

v1 whole, which is shorter than its diff:
```python
import functools

import jax
import jax.numpy as jnp
from jax import lax
from jax.experimental import pallas as pl
from jax.experimental.pallas import tpu as pltpu
from jax.sharding import PartitionSpec as P

BLK = 16
COARSE = 4
FINE = 8
LANES = 128
SUB = 8
HALO_C = 8
UNROLL = 22

huge_level = 1e30
fine_step = 2.0 ** (-10)
coarse_step = 2.0 ** (-6)
MIB = 2**20


def roll(x, shift, axis):
    return pltpu.roll(x, shift % x.shape[axis], axis)


def lane_iota(shape=(SUB, LANES)):
    return lax.broadcasted_iota(jnp.int32, shape, 1)


def gather_lanes(x, index):
    return jnp.take_along_axis(x, index, axis=1, mode="promise_in_bounds")


def prepare_kernel(elev, ocean, outlet, ground, lock, stats, north, south):
    step = pl.program_id(0)
    tiles = pl.num_programs(0)
    rows = elev.shape[0]
    blocks = rows // BLK
    lane = lane_iota()
    spread = (lane % 8) * BLK
    mine = lane // 8 == step

    @pl.when(step == 0)
    def _():
        stats[...] = jnp.zeros(stats.shape, jnp.float32)
        north[...] = jnp.zeros(north.shape, jnp.float32)
        south[...] = jnp.zeros(south.shape, jnp.float32)

    is_ocean = ocean[...] == 1
    g = jnp.where(is_ocean, jnp.float32(0.0), elev[...])
    k = jnp.where(is_ocean | (outlet[...] == 1), g, jnp.float32(huge_level))
    ground[0] = g
    lock[0] = k
    north[step, 0:FINE, :] = g[0:FINE]
    north[step, FINE:, :] = k[0:FINE]
    south[step, 0:FINE, :] = g[rows - FINE :]
    south[step, FINE:, :] = k[rows - FINE :]
    for q in range(blocks // SUB):
        for which, (source, pick) in enumerate(
            ((g, jnp.minimum), (k, jnp.minimum), (g, jnp.maximum))
        ):
            part = source[q * SUB * BLK : (q + 1) * SUB * BLK].reshape(SUB, BLK, LANES)
            reduce = jnp.max if which == 2 else jnp.min
            acc = reduce(part, axis=1)
            for shift in (1, 2, 4, 8):
                acc = pick(acc, roll(acc, -shift, 1))
            compact = gather_lanes(acc, spread)
            at = pl.ds(which * blocks + q * SUB, SUB)
            stats[at, :] = jnp.where(mine, compact, stats[at, :])

    @pl.when(step == tiles - 1)
    def _():
        for which in range(3):
            slot = tiles + which // 2
            at = (which % 2) * HALO_C
            first = which * blocks
            north[slot, at : at + HALO_C, :] = stats[first : first + HALO_C, :]
            south[slot, at : at + HALO_C, :] = stats[first + blocks - HALO_C : first + blocks, :]


def prepare(elevation, ocean, outlet):
    rows, cols = elevation.shape
    tiles = cols // LANES
    tile = pl.BlockSpec((rows, LANES), lambda j: (0, j))
    out_tile = pl.BlockSpec((1, rows, LANES), lambda j: (j, 0, 0))
    f32 = jnp.float32
    whole = lambda *shape: pl.BlockSpec(shape, lambda j: (0,) * len(shape))
    band = (tiles + 2, 2 * FINE, LANES)
    stats = (3 * rows // BLK, LANES)
    return pl.pallas_call(
        prepare_kernel,
        grid=(tiles,),
        in_specs=[tile, tile, tile],
        out_specs=[out_tile, out_tile, whole(*stats), whole(*band), whole(*band)],
        out_shape=[
            jax.ShapeDtypeStruct((tiles, rows, LANES), f32),
            jax.ShapeDtypeStruct((tiles, rows, LANES), f32),
            jax.ShapeDtypeStruct(stats, f32),
            jax.ShapeDtypeStruct(band, f32),
            jax.ShapeDtypeStruct(band, f32),
        ],
        compiler_params=pltpu.CompilerParams(vmem_limit_bytes=12 * MIB),
        name="prepare",
    )(elevation, ocean, outlet)


def sealed(value, is_edge):
    return jnp.where(is_edge, jnp.float32(huge_level), value)


def edges():
    pos = lax.axis_index("row")
    return pos == 0, pos == lax.axis_size("row") - 1


def coarse_fields(stats, from_north, from_south):
    tiles = from_north.shape[0] - 2
    blocks = stats.shape[0] // 3
    at_north, at_south = edges()
    fields = []
    for which in range(3):
        slot = tiles + which // 2
        at = (which % 2) * HALO_C
        top = sealed(from_north[slot, at : at + HALO_C, :], at_north)
        low = sealed(from_south[slot, at : at + HALO_C, :], at_south)
        mid = stats[which * blocks : (which + 1) * blocks, :]
        fields.append(jnp.concatenate([top, mid, low], axis=0))
    return fields


def coarse_sweeps(ground_c, lock_c, value):
    for _ in range(COARSE):
        across = jnp.minimum(value, jnp.minimum(roll(value, 1, 1), roll(value, -1, 1)))
        around = jnp.minimum(across, jnp.minimum(roll(across, 1, 0), roll(across, -1, 0)))
        lowered = jnp.minimum(value, around + coarse_step)
        value = jnp.minimum(jnp.maximum(ground_c, lowered), lock_c)
    return value


def start_tile(g, k, c):
    return jnp.minimum(jnp.maximum(g, c), k), jnp.minimum(g, k)


def across_min(tiles, lane, joined):
    count = len(tiles)
    left = [roll(v, 1, 1) for v in tiles]
    right = [roll(v, -1, 1) for v in tiles]
    out = []
    for j in range(count):
        west, east = left[j], right[j]
        if joined:
            west = jnp.where(lane == 0, left[j - 1], west)
            east = jnp.where(lane == LANES - 1, right[(j + 1) % count], east)
        out.append(jnp.minimum(tiles[j], jnp.minimum(west, east)))
    return out


def fine_sweep(src, dst, floor, stride, joined):
    count = src.shape[0]
    lane = lane_iota()

    def load(t):
        return [src[j, pl.ds(t, SUB, stride=stride), :] for j in range(count)]

    first = load(0)
    h_first = across_min(first, lane, joined)
    h_before = [roll(h, 1, 0) for h in across_min(load(stride - 1), lane, joined)]

    def advance(t, carry, after=None):
        h_up, h_here, here = carry
        if after is None:
            below = load(t + 1)
            h_down = across_min(below, lane, joined)
        else:
            below, h_down = here, after
        for j in range(count):
            low = jnp.minimum(jnp.minimum(h_up[j], h_down[j]), h_here[j])
            at = pl.ds(t, SUB, stride=stride)
            dst[j, at, :] = jnp.maximum(floor[j, at, :], jnp.minimum(here[j], low + fine_step))
        return h_here, h_down, below

    def body(q, carry):
        for u in range(UNROLL):
            carry = advance(q * UNROLL + u, carry)
        return carry

    loops = (stride - 1) // UNROLL
    carry = lax.fori_loop(0, loops, body, (h_before, h_first, first))
    for t in range(loops * UNROLL, stride - 1):
        carry = advance(t, carry)
    advance(stride - 1, carry, [roll(h, -1, 0) for h in h_first])


def all_sweeps(va, vb, floor, joined):
    stride = va.shape[1] // SUB

    def pair(i, carry):
        fine_sweep(va, vb, floor, stride, joined)
        fine_sweep(vb, va, floor, stride, joined)
        return carry

    lax.fori_loop(0, FINE // 2, pair, 0)


def padded_rows(rows):
    stride = -(-(rows + 2 * FINE) // SUB)
    return SUB * (stride + 1 - stride % 2)


def main_kernel(ground, lock, stats, from_north, from_south, out, va, vb, floor, lifted, sems):
    tiles, rows, _ = ground.shape
    blocks = rows // BLK
    at_north, at_south = edges()
    coarse = coarse_sweeps(*coarse_fields(stats, from_north, from_south))
    lane = lane_iota(coarse.shape)
    for j in range(tiles):
        lifted[j] = gather_lanes(coarse, lane // BLK + 8 * j)

    def put(j, at, size, g, k, c):
        v, low = start_tile(g, k, c)
        va[j, pl.ds(at, size), :] = v
        floor[j, pl.ds(at, size), :] = low

    for j in range(tiles):
        for band, is_edge, at, c_row in (
            (from_north, at_north, 0, HALO_C - 1),
            (from_south, at_south, FINE + rows, HALO_C + blocks),
        ):
            g = sealed(band[j, 0:FINE, :], is_edge)
            k = sealed(band[j, FINE:, :], is_edge)
            put(j, at, FINE, g, k, lifted[j, c_row : c_row + 1, :])
        rest = va.shape[1] - rows - 2 * FINE
        if rest:
            fill = jnp.full((rest, LANES), huge_level, jnp.float32)
            put(j, rows + 2 * FINE, rest, fill, fill, fill)

    def body(b, carry):
        for j in range(tiles):
            at = pl.ds(pl.multiple_of(b * BLK, BLK), BLK)
            c = lifted[j, pl.ds(HALO_C + b, 1), :]
            put(j, pl.multiple_of(FINE + b * BLK, SUB), BLK, ground[j, at, :], lock[j, at, :], c)
        return carry

    lax.fori_loop(0, blocks, body, 0, unroll=4)
    all_sweeps(va, vb, floor, True)
    copies = [
        pltpu.make_async_copy(
            va.at[j, pl.ds(FINE, rows), :], out.at[:, pl.ds(j * LANES, LANES)], sems.at[j]
        )
        for j in range(tiles)
    ]
    for copy in copies:
        copy.start()
    for copy in copies:
        copy.wait()


def main_part(ground, lock, stats, from_north, from_south):
    tiles, rows, _ = ground.shape
    blocks = rows // BLK
    vmem = pl.BlockSpec(memory_space=pltpu.VMEM)
    tall = (tiles, padded_rows(rows), LANES)
    return pl.pallas_call(
        main_kernel,
        in_specs=[vmem] * 5,
        out_specs=pl.BlockSpec(memory_space=pl.ANY),
        out_shape=jax.ShapeDtypeStruct((rows, tiles * LANES), jnp.float32),
        scratch_shapes=[
            pltpu.VMEM(tall, jnp.float32),
            pltpu.VMEM(tall, jnp.float32),
            pltpu.VMEM(tall, jnp.float32),
            pltpu.VMEM((tiles, blocks + 2 * HALO_C, LANES), jnp.float32),
            pltpu.SemaphoreType.DMA((tiles,)),
        ],
        compiler_params=pltpu.CompilerParams(vmem_limit_bytes=24 * MIB),
        cost_estimate=pl.CostEstimate(flops=100_000_000, bytes_accessed=40_000_000, transcendentals=0),
        name="middle",
    )(ground, lock, stats, from_north, from_south)


def column_sources(rows, blocks):
    fine = (rows + 2 * FINE) // SUB
    coarse = (blocks + 2 * HALO_C) // SUB
    return fine, coarse, -(-(2 * fine + 3 * coarse) // 16)


def pack_kernel(g_first, k_first, g_last, k_last, stats, from_north, from_south, west, east):
    rows = g_first.shape[1]
    blocks = rows // BLK
    tiles = from_north.shape[0] - 2
    at_north, at_south = edges()
    group = lane_iota() // 8
    fields = coarse_fields(stats, from_north, from_south)
    fine, coarse, slots = column_sources(rows, blocks)
    coarse_cols = tiles * LANES // BLK
    for dst, g_ref, k_ref, j, lane_at, lane_at_c in (
        (west, g_first, k_first, 0, 0, 0),
        (east, g_last, k_last, tiles - 1, LANES - 8, coarse_cols - 8),
    ):
        sources = []
        for half, ref in ((0, g_ref), (1, k_ref)):
            at = half * FINE
            sources.append((sealed(from_north[j, at : at + FINE, :], at_north), lane_at))
            for i in range(rows // SUB):
                sources.append((ref[0, i * SUB : (i + 1) * SUB, :], lane_at))
            sources.append((sealed(from_south[j, at : at + FINE, :], at_south), lane_at))
        for field in fields:
            for i in range(coarse):
                sources.append((field[i * SUB : (i + 1) * SUB], lane_at_c))
        for slot in range(slots):
            packed = jnp.zeros((SUB, LANES), jnp.float32)
            for n, (value, at) in enumerate(sources[slot * 16 : slot * 16 + 16]):
                packed = jnp.where(group == n, roll(value, 8 * n - at, 1), packed)
            dst[slot * SUB : (slot + 1) * SUB, :] = packed


def pack_columns(ground, lock, stats, from_north, from_south):
    tiles, rows, _ = ground.shape
    blocks = rows // BLK
    slots = column_sources(rows, blocks)[2]
    first = pl.BlockSpec((1, rows, LANES), lambda i: (0, 0, 0))
    last = pl.BlockSpec((1, rows, LANES), lambda i: (tiles - 1, 0, 0))
    whole = lambda x: pl.BlockSpec(x.shape, lambda i: (0,) * x.ndim)
    out = jax.ShapeDtypeStruct((slots * SUB, LANES), jnp.float32)
    return pl.pallas_call(
        pack_kernel,
        grid=(1,),
        in_specs=[first, first, last, last, whole(stats), whole(from_north), whole(from_south)],
        out_specs=[whole(out), whole(out)],
        out_shape=[out, out],
        compiler_params=pltpu.CompilerParams(vmem_limit_bytes=8 * MIB),
        name="pack",
    )(ground, lock, ground, lock, stats, from_north, from_south)


def strip_kernel(
    g_first, k_first, g_last, k_last, stats, from_north, from_south, from_west, from_east, partial,
    out, va, vb, floor, lifted, edge, in_sems, out_sems,
):
    rows = g_first.shape[1]
    blocks = rows // BLK
    tiles = from_north.shape[0] - 2
    coarse_cols = tiles * LANES // BLK
    at_north, at_south = edges()
    lane = lane_iota()
    fine, coarse, slots = column_sources(rows, blocks)
    edge_cols = [pl.ds(0, LANES), pl.ds((tiles - 1) * LANES, LANES)]
    loads = [
        pltpu.make_async_copy(partial.at[:, edge_cols[j]], edge.at[j], in_sems.at[j])
        for j in range(2)
    ]
    for copy in loads:
        copy.start()

    def piece(ref, n, to):
        value = ref[(n // 16) * SUB : (n // 16 + 1) * SUB, :]
        return roll(value, to - 8 * (n % 16), 1)

    fields = []
    for which, field in enumerate(coarse_fields(stats, from_north, from_south)):
        parts = []
        for i in range(coarse):
            n = 2 * fine + which * coarse + i
            here = field[i * SUB : (i + 1) * SUB]
            here = jnp.where(lane // 8 == coarse_cols // 8, piece(from_east, n, coarse_cols), here)
            here = jnp.where(lane // 8 == 15, piece(from_west, n, LANES - 8), here)
            parts.append(here)
        fields.append(jnp.concatenate(parts, axis=0))
    value = coarse_sweeps(*fields)
    wide = lane_iota(value.shape)
    lifted[0] = gather_lanes(value, ((wide - 8) >> 4) & (LANES - 1))
    lifted[1] = gather_lanes(value, coarse_cols - 8 + ((wide + 8) >> 4))

    for strip, (g_ref, k_ref, j, source) in enumerate(
        ((g_first, k_first, 0, from_west), (g_last, k_last, tiles - 1, from_east))
    ):
        outer = lane // 8 == (0 if strip == 0 else 15)
        shift = 8 if strip == 0 else -8
        to = 0 if strip == 0 else LANES - 8
        for i in range(fine):
            if i == 0:
                here = [sealed(from_north[j, h * FINE : (h + 1) * FINE, :], at_north) for h in range(2)]
            elif i == fine - 1:
                here = [sealed(from_south[j, h * FINE : (h + 1) * FINE, :], at_south) for h in range(2)]
            else:
                here = [ref[0, (i - 1) * SUB : i * SUB, :] for ref in (g_ref, k_ref)]
            both = [
                jnp.where(outer, piece(source, h * fine + i, to), roll(here[h], shift, 1))
                for h in range(2)
            ]
            c_row = (i + 2 * HALO_C - 1) // 2
            v, low = start_tile(both[0], both[1], lifted[strip, c_row : c_row + 1, :])
            va[strip, i * SUB : (i + 1) * SUB, :] = v
            floor[strip, i * SUB : (i + 1) * SUB, :] = low
        rest = va.shape[1] - fine * SUB
        if rest:
            fill = jnp.full((rest, LANES), huge_level, jnp.float32)
            va[strip, fine * SUB :, :] = fill
            floor[strip, fine * SUB :, :] = fill

    all_sweeps(va, vb, floor, False)
    for copy in loads:
        copy.wait()
    stores = []
    for strip in range(2):
        inner = (lane < LANES - 16) if strip == 0 else (lane >= 16)
        for i in range(rows // SUB):
            at = slice(i * SUB, (i + 1) * SUB)
            moved = roll(va[strip, FINE + i * SUB : FINE + (i + 1) * SUB, :], -8 if strip == 0 else 8, 1)
            edge[strip, at, :] = jnp.where(inner, moved, edge[strip, at, :])
        stores.append(
            pltpu.make_async_copy(edge.at[strip], out.at[:, edge_cols[strip]], out_sems.at[strip])
        )
        stores[-1].start()
    for copy in stores:
        copy.wait()


def strips(ground, lock, stats, from_north, from_south, from_west, from_east, partial):
    tiles, rows, _ = ground.shape
    blocks = rows // BLK
    first = pl.BlockSpec((1, rows, LANES), lambda i: (0, 0, 0))
    last = pl.BlockSpec((1, rows, LANES), lambda i: (tiles - 1, 0, 0))
    whole = lambda x: pl.BlockSpec(x.shape, lambda i: (0,) * x.ndim)
    hbm = pl.BlockSpec(memory_space=pl.ANY)
    tall = (2, padded_rows(rows), LANES)
    small = [stats, from_north, from_south, from_west, from_east]
    return pl.pallas_call(
        strip_kernel,
        grid=(1,),
        in_specs=[first, first, last, last] + [whole(x) for x in small] + [hbm],
        out_specs=hbm,
        out_shape=jax.ShapeDtypeStruct(partial.shape, jnp.float32),
        input_output_aliases={9: 0},
        scratch_shapes=[
            pltpu.VMEM(tall, jnp.float32),
            pltpu.VMEM(tall, jnp.float32),
            pltpu.VMEM(tall, jnp.float32),
            pltpu.VMEM((2, blocks + 2 * HALO_C, LANES), jnp.float32),
            pltpu.VMEM((2, rows, LANES), jnp.float32),
            pltpu.SemaphoreType.DMA((2,)),
            pltpu.SemaphoreType.DMA((2,)),
        ],
        compiler_params=pltpu.CompilerParams(vmem_limit_bytes=12 * MIB),
        name="strips",
    )(ground, lock, ground, lock, *small, partial)


def ring(value, axis, shift):
    count = lax.axis_size(axis)
    return lax.ppermute(value, axis, [(i, (i + shift) % count) for i in range(count)])


def shards(elevation, ocean, outlet):
    ground, lock, stats, north, south = prepare(elevation, ocean, outlet)
    from_south = ring(north, "row", -1)
    from_north = ring(south, "row", 1)
    rows_args = (ground, lock, stats, from_north, from_south)
    west, east = pack_columns(*rows_args)
    from_east = ring(west, "col", -1)
    from_west = ring(east, "col", 1)
    partial = main_part(*rows_args)
    return strips(*rows_args, from_west, from_east, partial)


def solution(mesh):
    return jax.shard_map(
        shards,
        mesh=mesh,
        in_specs=(P("row", "col"), P("row", "col"), P("row", "col")),
        out_specs=P("row", "col"),
        check_vma=False,
    )
```

time: 180 us -> 42.7 us (0.24)
  other arithmetic: 71.7 us -> 0 us
  local copies, waits for them, and re-layouts: 56.7 us -> 4.77 us
  starting transfers between devices: 33.8 us -> 7.59 us
  Pallas kernels: 0 us -> 25.7 us
  waiting for transfers between devices: 16.4 us -> 4.39 us
    min x12 -> x0, other arithmetic: 42.7 us -> none  [update(): return jnp.minimum(jnp.maximum(ground, lowered), lock)]
    reshape x3 -> x0, local copies, waits for them, and re-layouts: 34.6 us -> none  [the longest x1 15.2 us: shards(): jnp.broadcast_to(coarse[:, None, :, None], shape_blocks)]
    ppermute x20 -> x4, starting transfers between devices: 33.8 us -> 7.59 us  [ring(): lax.ppermute(value, axis, [(i, (i + shift) % count) for i in range(count)])]
    pallas_call x0 -> x4, Pallas kernels: none -> 25.7 us  [the longest x1 13.9 us: main_part(): pl.pallas_call(main_kernel, in_specs=[vmem] * 5, out_specs=pl.BlockSpec(m...]
    ppermute x20 -> x4, waiting for transfers between devices: 16.4 us -> 4.39 us  [ring(): lax.ppermute(value, axis, [(i, (i + shift) % count) for i in range(count)])]
    select_n x6 -> x0, other arithmetic: 9.55 us -> none  [the longest x1 5.37 us: shards(): lock = jnp.where(drains, ground, jnp.float32(huge_level))]
    concatenate x1 -> x0, local copies, waits for them, and re-layouts: 9.15 us -> none  [extended_2(): block = jnp.concatenate([low, block, high], axis=dim)]
    reduce_max x1 -> x0, other arithmetic: 8.33 us -> none  [shards(): coarse = ground.reshape(shape_blocks).max(axis=(1, 3))]
  transfers between devices with their start and end apart: 20 -> 4, of which waited for: 12 -> 2; matrix products, arithmetic and copies ran while one was open for 9% -> 0% of each run, Pallas kernels for 0% -> 33%
where the time goes in v1:
time: 42.7 us; the launch traced here: 42.5 us
  Pallas kernels  25.7 us (60%)
  starting transfers between devices  7.59 us (18%)
  local copies, waits for them, and re-layouts  4.77 us (11%)
  waiting for transfers between devices  4.39 us (10%)
    pallas_call x1, Pallas kernels, main_part(): pl.pallas_call(main_kernel, in_specs=[vmem] * 5, out_specs=pl.BlockSpec(m...  13.9 us
    ppermute x4, starting transfers between devices, ring(): lax.ppermute(value, axis, [(i, (i + shift) % count) for i in range(count)])  7.59 us
    pallas_call x1, Pallas kernels, strips(): pl.pallas_call(strip_kernel, grid=(1,), in_specs=[first, first, last, las...  6.44 us
    pallas_call x1, Pallas kernels, prepare(): pl.pallas_call(prepare_kernel, grid=(tiles,), in_specs=[tile, tile, tile]...  4.98 us
    unnamed x6, local copies, waits for them, and re-layouts  4.77 us
    ppermute x4, waiting for transfers between devices, ring(): lax.ppermute(value, axis, [(i, (i + shift) % count) for i in range(count)])  4.39 us
  transfers between devices with their start and end apart: 4, of which 2 were waited for; matrix products, arithmetic and copies ran while one was open for 0% of the time, Pallas kernels for 33%

profile of v1, /device:TPU:0, one launch (start us, length us, event | category | flops | bytes accessed | tf_op | source)
XLA Modules:
  0.0 42.5 jit_solution(9688515727437353106)
XLA Ops:
  0.0 0.0 copy-start
  0.0 1.6 %copy-done = f32[512,1024]{1,0:T(8,128)S(1)} copy-done((f32[512,1024]{1,0:T(8,128)S(1)}, f32[512,1024]{1,0:T(8,128)}, u32[]{:S(2)}) %copy-start) | copy-done | bytes 2097176
  1.6 0.0 copy-start.1
  1.6 1.6 %copy-done.1 = s32[512,1024]{1,0:T(8,128)S(1)} copy-done((s32[512,1024]{1,0:T(8,128)S(1)}, s32[512,1024]{1,0:T(8,128)}, u32[]{:S(2)}) %copy-start.1) | copy-done | bytes 2097176
  3.2 0.0 copy-start.2
  3.2 1.6 %copy-done.2 = s32[512,1024]{1,0:T(8,128)S(1)} copy-done((s32[512,1024]{1,0:T(8,128)S(1)}, s32[512,1024]{1,0:T(8,128)}, u32[]{:S(2)}) %copy-start.2) | copy-done | bytes 2097176
  4.8 5.0 %prepare.1 = (f32[8,512,128]{2,1,0:T(8,128)S(1)}, f32[8,512,128]{2,1,0:T(8,128)S(1)}, f32[96,128]{1,0:T(8,128)S(1)}, f32[10,16,128]{2,1,0:T(8,128)S(1)}, f32[10,16,128]{2,1,0:T(8,128)S(1)}) custom-call(f32[512,1024]{1,0:T(8,128)S(1)} %copy-done, s32[512,1024]{1,0:T(8,128)S(1)} %copy-done.1, s32[512,1024]{1,0:T(8,128)S(1)} %copy-done.2), custom_call_target="tpu_custom_call" | custom-call | tf_op jit(solution)/shard_map/prepare/pallas_call | solution.py:92
  9.8 3.0 %collective-permute-start = (f32[10,16,128]{2,1,0:T(8,128)S(1)}, f32[10,16,128]{2,1,0:T(8,128)S(1)}, u32[]{:S(2)}, u32[]{:S(2)}) collective-permute-start(f32[10,16,128]{2,1,0:T(8,128)S(1)} %get-tuple-element.15), channel_id=1, source_target_pairs={{0,8},{8,16},{16,24},{24,0},{1,9},{9,17},{17,25},{25,1},{2,10},{10... | collective-permute-start | bytes 245768 | tf_op jit(solution)/shard_map/ppermute | solution.py:453
  12.7 1.0 %collective-permute-start.1 = (f32[10,16,128]{2,1,0:T(8,128)S(1)}, f32[10,16,128]{2,1,0:T(8,128)S(1)}, u32[]{:S(2)}, u32[]{:S(2)}) collective-permute-start(f32[10,16,128]{2,1,0:T(8,128)S(1)} %get-tuple-element.16), channel_id=1, source_target_pairs={{0,24},{8,0},{16,8},{24,16},{1,25},{9,1},{17,9},{25,17},{2,26},{10... | collective-permute-start | bytes 245768 | tf_op jit(solution)/shard_map/ppermute | solution.py:453
  13.8 2.7 %collective-permute-done.from_north = f32[10,16,128]{2,1,0:T(8,128)S(1)} collective-permute-done((f32[10,16,128]{2,1,0:T(8,128)S(1)}, f32[10,16,128]{2,1,0:T(8,128)S(1)}, u32[]{:S(2)}, u32[]{:S(2)}) %collective-permute-start) | collective-permute-done | bytes 81952 | tf_op jit(solution)/shard_map/ppermute | solution.py:453
  16.5 1.7 %collective-permute-done.1.from_south = f32[10,16,128]{2,1,0:T(8,128)S(1)} collective-permute-done((f32[10,16,128]{2,1,0:T(8,128)S(1)}, f32[10,16,128]{2,1,0:T(8,128)S(1)}, u32[]{:S(2)}, u32[]{:S(2)}) %collective-permute-start.1) | collective-permute-done | bytes 81952 | tf_op jit(solution)/shard_map/ppermute | solution.py:453
  18.1 0.4 pack.1
  18.5 0.1 collective-permute-start.2
  18.6 3.5 %collective-permute-start.3 = (f32[80,128]{1,0:T(8,128)S(1)}, f32[80,128]{1,0:T(8,128)S(1)}, u32[]{:S(2)}, u32[]{:S(2)}) collective-permute-start(f32[80,128]{1,0:T(8,128)S(1)} %get-tuple-element.18), channel_id=1, source_target_pairs={{0,7},{1,0},{2,1},{3,2},{4,3},{5,4},{6,5},{7,6},{8,15},{9,8},{10,9... | collective-permute-start | bytes 122888 | tf_op jit(solution)/shard_map/ppermute | solution.py:453
  22.1 13.9 %middle.1.partial = f32[512,1024]{1,0:T(8,128)} custom-call(f32[8,512,128]{2,1,0:T(8,128)S(1)} %get-tuple-element.12.g_first.g_last.ground, f32[8,512,128]{2,1,0:T(8,128)S(1)} %get-tuple-element.13.k_first.k_last.lock, f32[96,128]{1,0:T(8,128)S(1)} %get-tuple-element.14.stats, f32[10,16,128]{2,1,0:T(8,128)S(1)} %collective-permute-done.from_north, ...), custom_call_target="tpu_custom_call" | custom-call | flops 100000000 | bytes 40000000 | tf_op jit(solution)/shard_map/middle/pallas_call | solution.py:265
  36.0 0.0 collective-permute-done.2.from_west
  36.0 0.0 collective-permute-done.3.from_east
  36.0 6.4 %strips.1 = f32[512,1024]{1,0:T(8,128)} custom-call(f32[8,512,128]{2,1,0:T(8,128)S(1)} %get-tuple-element.12.g_first.g_last.ground, f32[8,512,128]{2,1,0:T(8,128)S(1)} %get-tuple-element.13.k_first.k_last.lock, f32[8,512,128]{2,1,0:T(8,128)S(1)} %get-tuple-element.12.g_first.g_last.ground, ...), custom_call_target="tpu_custom_call", output_to_operand_aliasing={{}: (9, {})} | custom-call | tf_op jit(solution)/shard_map/strips/pallas_call | solution.py:430
Async XLA Ops:
  0.0 1.6 %copy-start = (f32[512,1024]{1,0:T(8,128)S(1)}, f32[512,1024]{1,0:T(8,128)}, u32[]{:S(2)}) copy-start(f32[512,1024]{1,0:T(8,128)} %elev.1) | copy-start | bytes 6291460
  1.6 1.6 %copy-start.1 = (s32[512,1024]{1,0:T(8,128)S(1)}, s32[512,1024]{1,0:T(8,128)}, u32[]{:S(2)}) copy-start(s32[512,1024]{1,0:T(8,128)} %ocean.1) | copy-start | bytes 6291460
  3.2 1.6 %copy-start.2 = (s32[512,1024]{1,0:T(8,128)S(1)}, s32[512,1024]{1,0:T(8,128)}, u32[]{:S(2)}) copy-start(s32[512,1024]{1,0:T(8,128)} %outlet.1) | copy-start | bytes 6291460
  9.8 6.7 %collective-permute-start = (f32[10,16,128]{2,1,0:T(8,128)S(1)}, f32[10,16,128]{2,1,0:T(8,128)S(1)}, u32[]{:S(2)}, u32[]{:S(2)}) collective-permute-start(f32[10,16,128]{2,1,0:T(8,128)S(1)} %get-tuple-element.15), channel_id=1, source_target_pairs={{0,8},{8,16},{16,24},{24,0},{1,9},{9,17},{17,25},{25,1},{2,10},{10... | collective-permute-start | bytes 245768 | tf_op jit(solution)/shard_map/ppermute | solution.py:453
  12.7 5.4 %collective-permute-start.1 = (f32[10,16,128]{2,1,0:T(8,128)S(1)}, f32[10,16,128]{2,1,0:T(8,128)S(1)}, u32[]{:S(2)}, u32[]{:S(2)}) collective-permute-start(f32[10,16,128]{2,1,0:T(8,128)S(1)} %get-tuple-element.16), channel_id=1, source_target_pairs={{0,24},{8,0},{16,8},{24,16},{1,25},{9,1},{17,9},{25,17},{2,26},{10... | collective-permute-start | bytes 245768 | tf_op jit(solution)/shard_map/ppermute | solution.py:453
  18.5 17.5 %collective-permute-start.2 = (f32[80,128]{1,0:T(8,128)S(1)}, f32[80,128]{1,0:T(8,128)S(1)}, u32[]{:S(2)}, u32[]{:S(2)}) collective-permute-start(f32[80,128]{1,0:T(8,128)S(1)} %get-tuple-element.17), channel_id=1, source_target_pairs={{0,1},{1,2},{2,3},{3,4},{4,5},{5,6},{6,7},{7,0},{8,9},{9,10},{10,1... | collective-permute-start | bytes 122888 | tf_op jit(solution)/shard_map/ppermute | solution.py:453
  18.6 17.5 %collective-permute-start.3 = (f32[80,128]{1,0:T(8,128)S(1)}, f32[80,128]{1,0:T(8,128)S(1)}, u32[]{:S(2)}, u32[]{:S(2)}) collective-permute-start(f32[80,128]{1,0:T(8,128)S(1)} %get-tuple-element.18), channel_id=1, source_target_pairs={{0,7},{1,0},{2,1},{3,2},{4,3},{5,4},{6,5},{7,6},{8,15},{9,8},{10,9... | collective-permute-start | bytes 122888 | tf_op jit(solution)/shard_map/ppermute | solution.py:453

commit v2 on v1

--- a/solution.py
+++ b/solution.py
@@ -14,6 +14,7 @@
 SUB = 8
 HALO_C = 8
 UNROLL = 22
+UNROLL_T = 15
 
 huge_level = 1e30
 fine_step = 2.0 ** (-10)
@@ -33,77 +34,131 @@
     return jnp.take_along_axis(x, index, axis=1, mode="promise_in_bounds")
 
 
-def prepare_kernel(elev, ocean, outlet, ground, lock, stats, north, south):
-    step = pl.program_id(0)
-    tiles = pl.num_programs(0)
-    rows = elev.shape[0]
+def interior(tiles):
+    margin = COARSE * BLK
+    chunk = (tiles * LANES - 2 * margin) // SUB
+    return margin, chunk
+
+
+def plane_row(col, tiles):
+    margin, chunk = interior(tiles)
+    return col + (col + chunk - margin) // chunk
+
+
+def plane_rows(tiles):
+    return -(-(plane_row(tiles * LANES, tiles) + 1) // SUB) * SUB
+
+
+def prepare_kernel(
+    elev, ocean, outlet, ground, lock, ground_t, lock_t, stats, stats_t, north, south,
+    elev_buf, ocean_buf, outlet_buf, turn, sems,
+):
+    tiles, rows, _ = ground.shape
+    planes = rows // LANES
     blocks = rows // BLK
     lane = lane_iota()
-    spread = (lane % 8) * BLK
-    mine = lane // 8 == step
-
-    @pl.when(step == 0)
-    def _():
-        stats[...] = jnp.zeros(stats.shape, jnp.float32)
-        north[...] = jnp.zeros(north.shape, jnp.float32)
-        south[...] = jnp.zeros(south.shape, jnp.float32)
-
-    is_ocean = ocean[...] == 1
-    g = jnp.where(is_ocean, jnp.float32(0.0), elev[...])
-    k = jnp.where(is_ocean | (outlet[...] == 1), g, jnp.float32(huge_level))
-    ground[0] = g
-    lock[0] = k
-    north[step, 0:FINE, :] = g[0:FINE]
-    north[step, FINE:, :] = k[0:FINE]
-    south[step, 0:FINE, :] = g[rows - FINE :]
-    south[step, FINE:, :] = k[rows - FINE :]
-    for q in range(blocks // SUB):
-        for which, (source, pick) in enumerate(
-            ((g, jnp.minimum), (k, jnp.minimum), (g, jnp.maximum))
-        ):
-            part = source[q * SUB * BLK : (q + 1) * SUB * BLK].reshape(SUB, BLK, LANES)
-            reduce = jnp.max if which == 2 else jnp.min
-            acc = reduce(part, axis=1)
-            for shift in (1, 2, 4, 8):
-                acc = pick(acc, roll(acc, -shift, 1))
-            compact = gather_lanes(acc, spread)
-            at = pl.ds(which * blocks + q * SUB, SUB)
-            stats[at, :] = jnp.where(mine, compact, stats[at, :])
-
-    @pl.when(step == tiles - 1)
-    def _():
+    sub = lax.broadcasted_iota(jnp.int32, (SUB, LANES), 0)
+
+    def copies(j):
+        cols = pl.ds(pl.multiple_of(j * LANES, LANES), LANES)
+        return [
+            pltpu.make_async_copy(src.at[:, cols], dst.at[j], sems.at[n, j])
+            for n, (src, dst) in enumerate(
+                ((elev, elev_buf), (ocean, ocean_buf), (outlet, outlet_buf))
+            )
+        ]
+
+    for j in range(tiles):
+        for copy in copies(j):
+            copy.start()
+    turn[...] = jnp.zeros(turn.shape, jnp.float32)
+    for band in (north, south):
+        band[tiles:, :, :] = jnp.zeros((2, 2 * FINE, LANES), jnp.float32)
+
+    def tile(j, carry):
+        for copy in copies(j):
+            copy.wait()
+        is_ocean = ocean_buf[j] == 1
+        g = jnp.where(is_ocean, jnp.float32(0.0), elev_buf[j])
+        k = jnp.where(is_ocean | (outlet_buf[j] == 1), g, jnp.float32(huge_level))
+        ground[j] = g
+        lock[j] = k
+        north[j, 0:FINE, :] = g[0:FINE]
+        north[j, FINE:, :] = k[0:FINE]
+        south[j, 0:FINE, :] = g[rows - FINE :]
+        south[j, FINE:, :] = k[rows - FINE :]
+        found = [[None] * 8 for _ in range(3)]
+        for c in range(planes):
+            for which, (ref, dst) in enumerate(((ground, ground_t), (lock, lock_t))):
+                parts = [
+                    ref[j, pl.ds(a * SUB * planes + c, SUB, stride=planes), :]
+                    for a in range(LANES // SUB)
+                ]
+                turned = jnp.concatenate(parts, axis=0).T
+                for v in range(LANES // SUB):
+                    value = turned[v * SUB : (v + 1) * SUB]
+                    at = plane_row(j * LANES + v * SUB, tiles)
+                    dst[c, pl.ds(at, SUB), :] = value
+                    b = v // 2
+                    for to, pick in ((which, jnp.minimum), (2, jnp.maximum)):
+                        if to == 2 and which == 1:
+                            continue
+                        old = found[to][b]
+                        found[to][b] = value if old is None else pick(old, value)
         for which in range(3):
-            slot = tiles + which // 2
-            at = (which % 2) * HALO_C
-            first = which * blocks
-            north[slot, at : at + HALO_C, :] = stats[first : first + HALO_C, :]
-            south[slot, at : at + HALO_C, :] = stats[first + blocks - HALO_C : first + blocks, :]
+            pick = jnp.maximum if which == 2 else jnp.minimum
+            total = None
+            for b in range(8):
+                value = found[which][b]
+                for shift in (4, 2, 1):
+                    value = pick(value, roll(value, shift, 0))
+                total = value if b == 0 else jnp.where(sub == b, value, total)
+            for swap in (1, 2):
+                total = pick(total, gather_lanes(total, lane ^ swap))
+            at = pl.ds(pl.multiple_of(j * SUB, SUB), SUB)
+            stats_t[which, at, :] = total
+            turn[which, at, :] = total
+        return carry
+
+    lax.fori_loop(0, tiles, tile, 0)
+    for which in range(3):
+        turn[which] = turn[which].T
+        for q in range(blocks // SUB):
+            stats[which * blocks + q * SUB : which * blocks + (q + 1) * SUB, :] = turn[
+                which, pl.ds(q * SUB * BLK // planes, SUB, stride=BLK // planes), :
+            ]
+        slot = tiles + which // 2
+        at = (which % 2) * HALO_C
+        first = which * blocks
+        north[slot, at : at + HALO_C, :] = stats[first : first + HALO_C, :]
+        south[slot, at : at + HALO_C, :] = stats[first + blocks - HALO_C : first + blocks, :]
 
 
 def prepare(elevation, ocean, outlet):
     rows, cols = elevation.shape
     tiles = cols // LANES
-    tile = pl.BlockSpec((rows, LANES), lambda j: (0, j))
-    out_tile = pl.BlockSpec((1, rows, LANES), lambda j: (j, 0, 0))
     f32 = jnp.float32
-    whole = lambda *shape: pl.BlockSpec(shape, lambda j: (0,) * len(shape))
+    hbm = pl.BlockSpec(memory_space=pltpu.HBM)
+    vmem = pl.BlockSpec(memory_space=pltpu.VMEM)
+    natural = (tiles, rows, LANES)
+    turned = (rows // LANES, plane_rows(tiles), LANES)
     band = (tiles + 2, 2 * FINE, LANES)
-    stats = (3 * rows // BLK, LANES)
+    shapes = [natural, natural, turned, turned, (3 * rows // BLK, LANES), (3, cols // BLK, LANES), band, band]
     return pl.pallas_call(
         prepare_kernel,
-        grid=(tiles,),
-        in_specs=[tile, tile, tile],
-        out_specs=[out_tile, out_tile, whole(*stats), whole(*band), whole(*band)],
-        out_shape=[
-            jax.ShapeDtypeStruct((tiles, rows, LANES), f32),
-            jax.ShapeDtypeStruct((tiles, rows, LANES), f32),
-            jax.ShapeDtypeStruct(stats, f32),
-            jax.ShapeDtypeStruct(band, f32),
-            jax.ShapeDtypeStruct(band, f32),
+        in_specs=[hbm] * 3,
+        out_specs=[vmem] * len(shapes),
+        out_shape=[jax.ShapeDtypeStruct(shape, f32) for shape in shapes],
+        scratch_shapes=[
+            pltpu.VMEM(natural, f32),
+            pltpu.VMEM(natural, jnp.int32),
+            pltpu.VMEM(natural, jnp.int32),
+            pltpu.VMEM((3, LANES, LANES), f32),
+            pltpu.SemaphoreType.DMA((3, tiles)),
         ],
-        compiler_params=pltpu.CompilerParams(vmem_limit_bytes=12 * MIB),
+        compiler_params=pltpu.CompilerParams(vmem_limit_bytes=24 * MIB),
         name="prepare",
-    )(elevation, ocean, outlet)
+    )(*(pltpu.with_memory_space_constraint(x, pltpu.HBM) for x in (elevation, ocean, outlet)))
 
 
 def sealed(value, is_edge):
@@ -209,75 +264,222 @@
     return SUB * (stride + 1 - stride % 2)
 
 
-def main_kernel(ground, lock, stats, from_north, from_south, out, va, vb, floor, lifted, sems):
+def turned_sweep(count, planes, load, store, floor):
+    def across(tiles):
+        up = [roll(tiles[planes - 1], 1, 1)] + tiles[:-1]
+        down = tiles[1:] + [roll(tiles[0], -1, 1)]
+        return [jnp.minimum(jnp.minimum(u, v), d) for u, v, d in zip(up, tiles, down)]
+
+    first = load(0)
+    h_first = across(first)
+    h_before = [roll(h, 1, 0) for h in across(load(count - 1))]
+
+    def advance(t, carry, after=None):
+        h_west, h_here, here = carry
+        if after is None:
+            east = load(t + 1)
+            h_east = across(east)
+        else:
+            east, h_east = here, after
+        for c in range(planes):
+            low = jnp.minimum(jnp.minimum(h_west[c], h_east[c]), h_here[c])
+            store(c, t, jnp.maximum(floor[c, t], jnp.minimum(here[c], low + fine_step)))
+        return h_here, h_east, east
+
+    def body(q, carry):
+        for u in range(UNROLL_T):
+            carry = advance(q * UNROLL_T + u, carry)
+        return carry
+
+    loops = (count - 1) // UNROLL_T
+    carry = lax.fori_loop(0, loops, body, (h_before, h_first, first))
+    for t in range(loops * UNROLL_T, count - 1):
+        carry = advance(t, carry)
+    advance(count - 1, carry, [roll(h, -1, 0) for h in h_first])
+
+
+def main_kernel(ground_t, lock_t, stats_t, out, va, vb, floor, coarse, turned, natural, sems):
+    tiles, rows, _ = natural.shape
+    planes = rows // LANES
+    margin, chunk = interior(tiles)
+    first = plane_row(margin, tiles)
+    pitch = chunk + 1
+    value = stats_t[2]
+    for _ in range(COARSE):
+        across = jnp.minimum(value, jnp.minimum(roll(value, 1, 0), roll(value, -1, 0)))
+        reach = BLK // planes
+        around = jnp.minimum(across, jnp.minimum(roll(across, reach, 1), roll(across, -reach, 1)))
+        lowered = jnp.minimum(value, around + coarse_step)
+        value = jnp.minimum(jnp.maximum(stats_t[0], lowered), stats_t[1])
+    coarse[...] = value
+
+    def start(b, carry):
+        c_value = coarse[pl.ds(margin // BLK + b, SUB, stride=chunk // BLK), :]
+        for u in range(BLK):
+            t = b * BLK + u
+            at = pl.ds(first + t, SUB, stride=pitch)
+            for c in range(planes):
+                va[c, t], floor[c, t] = start_tile(ground_t[c, at, :], lock_t[c, at, :], c_value)
+        return carry
+
+    lax.fori_loop(0, chunk // BLK, start, 0)
+
+    def sweep(src, dst):
+        def store(c, t, value):
+            dst[c, t] = value
+
+        turned_sweep(chunk, planes, lambda t: [src[c, t] for c in range(planes)], store, floor)
+
+    def pair(i, carry):
+        sweep(va, vb)
+        sweep(vb, va)
+        return carry
+
+    lax.fori_loop(0, FINE // 2 - 1, pair, 0)
+    sweep(va, vb)
+
+    def store_last(c, t, value):
+        turned[c, pl.ds(first + t, SUB, stride=pitch), :] = value
+
+    turned_sweep(chunk, planes, lambda t: [vb[c, t] for c in range(planes)], store_last, floor)
+    cols = tiles * LANES
+    for c in range(planes):
+        for col in list(range(0, margin, SUB)) + list(range(cols - margin, cols, SUB)):
+            at = plane_row(col, tiles)
+            turned[c, at : at + SUB, :] = jnp.zeros((SUB, LANES), jnp.float32)
+
+    keep = pl.ds(margin + FINE, rows - 2 * margin - 2 * FINE)
+
+    def copy_out(j):
+        cols_j = pl.ds(pl.multiple_of(j * LANES, LANES), LANES)
+        return pltpu.make_async_copy(natural.at[j, keep, :], out.at[keep, cols_j], sems.at[j])
+
+    def finish(j, carry):
+        for c in range(planes):
+            parts = []
+            for v in range(LANES // SUB):
+                at = plane_row(j * LANES + v * SUB, tiles)
+                parts.append(turned[c, pl.ds(at, SUB), :])
+            back = jnp.concatenate(parts, axis=0).T
+            for a in range(LANES // SUB):
+                natural[j, pl.ds(a * SUB * planes + c, SUB, stride=planes), :] = back[
+                    a * SUB : (a + 1) * SUB
+                ]
+        copy_out(j).start()
+        return carry
+
+    lax.fori_loop(0, tiles, finish, 0)
+    for j in range(tiles):
+        copy_out(j).wait()
+
+
+def main_part(ground_t, lock_t, stats_t):
+    planes, length, _ = ground_t.shape
+    tiles = stats_t.shape[1] * BLK // LANES
+    rows = planes * LANES
+    chunk = interior(tiles)[1]
+    vmem = pl.BlockSpec(memory_space=pltpu.VMEM)
+    tall = (planes, chunk, SUB, LANES)
+    f32 = jnp.float32
+    return pl.pallas_call(
+        main_kernel,
+        in_specs=[vmem] * 3,
+        out_specs=pl.BlockSpec(memory_space=pltpu.HBM),
+        out_shape=jax.ShapeDtypeStruct((rows, tiles * LANES), f32),
+        scratch_shapes=[
+            pltpu.VMEM(tall, f32),
+            pltpu.VMEM(tall, f32),
+            pltpu.VMEM(tall, f32),
+            pltpu.VMEM(stats_t.shape[1:], f32),
+            pltpu.VMEM((planes, length, LANES), f32),
+            pltpu.VMEM((tiles, rows, LANES), f32),
+            pltpu.SemaphoreType.DMA((tiles,)),
+        ],
+        compiler_params=pltpu.CompilerParams(vmem_limit_bytes=24 * MIB),
+        cost_estimate=pl.CostEstimate(flops=100_000_000, bytes_accessed=20_000_000, transcendentals=0),
+        name="middle",
+    )(ground_t, lock_t, stats_t)
+
+
+def bands_kernel(ground, lock, stats, from_north, from_south, partial, out, va, vb, floor, lifted, sems):
     tiles, rows, _ = ground.shape
     blocks = rows // BLK
+    height = va.shape[2]
+    inner = height - FINE
     at_north, at_south = edges()
     coarse = coarse_sweeps(*coarse_fields(stats, from_north, from_south))
     lane = lane_iota(coarse.shape)
     for j in range(tiles):
         lifted[j] = gather_lanes(coarse, lane // BLK + 8 * j)
-
-    def put(j, at, size, g, k, c):
-        v, low = start_tile(g, k, c)
-        va[j, pl.ds(at, size), :] = v
-        floor[j, pl.ds(at, size), :] = low
-
-    for j in range(tiles):
-        for band, is_edge, at, c_row in (
-            (from_north, at_north, 0, HALO_C - 1),
-            (from_south, at_south, FINE + rows, HALO_C + blocks),
-        ):
-            g = sealed(band[j, 0:FINE, :], is_edge)
-            k = sealed(band[j, FINE:, :], is_edge)
-            put(j, at, FINE, g, k, lifted[j, c_row : c_row + 1, :])
-        rest = va.shape[1] - rows - 2 * FINE
-        if rest:
-            fill = jnp.full((rest, LANES), huge_level, jnp.float32)
-            put(j, rows + 2 * FINE, rest, fill, fill, fill)
-
-    def body(b, carry):
+    for side, (band, is_edge, at_band, at_inner, first) in enumerate(
+        ((from_north, at_north, 0, FINE, 0), (from_south, at_south, inner, 0, rows - inner))
+    ):
         for j in range(tiles):
-            at = pl.ds(pl.multiple_of(b * BLK, BLK), BLK)
-            c = lifted[j, pl.ds(HALO_C + b, 1), :]
-            put(j, pl.multiple_of(FINE + b * BLK, SUB), BLK, ground[j, at, :], lock[j, at, :], c)
-        return carry
-
-    lax.fori_loop(0, blocks, body, 0, unroll=4)
-    all_sweeps(va, vb, floor, True)
-    copies = [
-        pltpu.make_async_copy(
-            va.at[j, pl.ds(FINE, rows), :], out.at[:, pl.ds(j * LANES, LANES)], sems.at[j]
-        )
-        for j in range(tiles)
-    ]
-    for copy in copies:
-        copy.start()
+
+            def put(at, g, k, c_row):
+                c = lifted[j, c_row : c_row + 1, :]
+                v, low = start_tile(g, k, c)
+                va[side, j, at : at + SUB, :] = v
+                floor[side, j, at : at + SUB, :] = low
+
+            put(
+                at_band,
+                sealed(band[j, 0:FINE, :], is_edge),
+                sealed(band[j, FINE:, :], is_edge),
+                HALO_C - 1 if side == 0 else HALO_C + blocks,
+            )
+            for i in range(inner // SUB):
+                at = slice(first + i * SUB, first + (i + 1) * SUB)
+                c_row = HALO_C + (first + i * SUB) // BLK
+                put(at_inner + i * SUB, ground[j, at, :], lock[j, at, :], c_row)
+
+    def pair(i, carry):
+        for src, dst in ((va, vb), (vb, va)):
+            for side in range(2):
+                fine_sweep(src.at[side], dst.at[side], floor.at[side], height // SUB, True)
+        return carry
+
+    lax.fori_loop(0, FINE // 2, pair, 0)
+    valid = inner - FINE
+    copies = []
+    for side, (at, to) in enumerate(((FINE, 0), (FINE, rows - valid))):
+        for j in range(tiles):
+            copies.append(
+                pltpu.make_async_copy(
+                    va.at[side, j, pl.ds(at, valid), :],
+                    out.at[pl.ds(to, valid), pl.ds(j * LANES, LANES)],
+                    sems.at[side, j],
+                )
+            )
+            copies[-1].start()
     for copy in copies:
         copy.wait()
 
 
-def main_part(ground, lock, stats, from_north, from_south):
+def bands(ground, lock, stats, from_north, from_south, partial):
     tiles, rows, _ = ground.shape
     blocks = rows // BLK
     vmem = pl.BlockSpec(memory_space=pltpu.VMEM)
-    tall = (tiles, padded_rows(rows), LANES)
+    hbm = pl.BlockSpec(memory_space=pltpu.HBM)
+    tall = (2, tiles, COARSE * BLK + 3 * FINE, LANES)
+    f32 = jnp.float32
     return pl.pallas_call(
-        main_kernel,
-        in_specs=[vmem] * 5,
-        out_specs=pl.BlockSpec(memory_space=pl.ANY),
-        out_shape=jax.ShapeDtypeStruct((rows, tiles * LANES), jnp.float32),
+        bands_kernel,
+        in_specs=[vmem] * 5 + [hbm],
+        out_specs=hbm,
+        out_shape=jax.ShapeDtypeStruct(partial.shape, f32),
+        input_output_aliases={5: 0},
         scratch_shapes=[
-            pltpu.VMEM(tall, jnp.float32),
-            pltpu.VMEM(tall, jnp.float32),
-            pltpu.VMEM(tall, jnp.float32),
-            pltpu.VMEM((tiles, blocks + 2 * HALO_C, LANES), jnp.float32),
-            pltpu.SemaphoreType.DMA((tiles,)),
+            pltpu.VMEM(tall, f32),
+            pltpu.VMEM(tall, f32),
+            pltpu.VMEM(tall, f32),
+            pltpu.VMEM((tiles, blocks + 2 * HALO_C, LANES), f32),
+            pltpu.SemaphoreType.DMA((2, tiles)),
         ],
-        compiler_params=pltpu.CompilerParams(vmem_limit_bytes=24 * MIB),
-        cost_estimate=pl.CostEstimate(flops=100_000_000, bytes_accessed=40_000_000, transcendentals=0),
-        name="middle",
-    )(ground, lock, stats, from_north, from_south)
+        compiler_params=pltpu.CompilerParams(vmem_limit_bytes=16 * MIB),
+        cost_estimate=pl.CostEstimate(flops=60_000_000, bytes_accessed=12_000_000, transcendentals=0),
+        name="bands",
+    )(ground, lock, stats, from_north, from_south, partial)
 
 
 def column_sources(rows, blocks):
@@ -454,14 +656,16 @@
 
 
 def shards(elevation, ocean, outlet):
-    ground, lock, stats, north, south = prepare(elevation, ocean, outlet)
+    ground, lock, ground_t, lock_t, stats, stats_t, north, south = prepare(elevation, ocean, outlet)
     from_south = ring(north, "row", -1)
     from_north = ring(south, "row", 1)
+    partial = main_part(ground_t, lock_t, stats_t)
+    from_north, from_south, partial = lax.optimization_barrier((from_north, from_south, partial))
     rows_args = (ground, lock, stats, from_north, from_south)
     west, east = pack_columns(*rows_args)
     from_east = ring(west, "col", -1)
     from_west = ring(east, "col", 1)
-    partial = main_part(*rows_args)
+    partial = bands(*rows_args, partial)
     return strips(*rows_args, from_west, from_east, partial)
 
 

time: 42.7 us -> 34.4 us (0.81)
  local copies, waits for them, and re-layouts: 4.77 us -> 0 us
  waiting for transfers between devices: 4.39 us -> 0.01 us
  Pallas kernels: 25.7 us -> 26.6 us
    unnamed x6 -> x0, local copies, waits for them, and re-layouts: 4.77 us -> none
    ppermute x4, waiting for transfers between devices: 4.39 us -> 0.01 us  [ring(): lax.ppermute(value, axis, [(i, (i + shift) % count) for i in range(count)])]
    pallas_call x2 -> x3, Pallas kernels: 18.9 us -> 19.8 us  [the longest x1 10.1 us: main_part(): pl.pallas_call(main_kernel, in_specs=[vmem] * 3, out_specs=pl.BlockSpec(m...]
  transfers between devices with their start and end apart: 4 -> 4, of which waited for: 2 -> 0; matrix products, arithmetic and copies ran while one was open for 0% -> 0% of each run, Pallas kernels for 33% -> 44%
where the time goes in v2:
time: 34.4 us; the launch traced here: 34.3 us
  Pallas kernels  26.6 us (77%)
  starting transfers between devices  7.6 us (22%)
    pallas_call x1, Pallas kernels, main_part(): pl.pallas_call(main_kernel, in_specs=[vmem] * 3, out_specs=pl.BlockSpec(m...  10.1 us
    ppermute x4, starting transfers between devices, ring(): lax.ppermute(value, axis, [(i, (i + shift) % count) for i in range(count)])  7.6 us
    pallas_call x1, Pallas kernels, strips(): pl.pallas_call(strip_kernel, grid=(1,), in_specs=[first, first, last, las...  6.44 us
    pallas_call x1, Pallas kernels, bands(): pl.pallas_call(bands_kernel, in_specs=[vmem] * 5 + [hbm], out_specs=hbm,...  5.03 us
    pallas_call x1, Pallas kernels, prepare(): pl.pallas_call(prepare_kernel, in_specs=[hbm] * 3, out_specs=[vmem] * len...  4.73 us
  transfers between devices with their start and end apart: 4, of which 0 were waited for; matrix products, arithmetic and copies ran while one was open for 0% of the time, Pallas kernels for 44%

profile of v2, /device:TPU:0, one launch (start us, length us, event | category | flops | bytes accessed | tf_op | source)
XLA Modules:
  0.0 34.3 jit_solution(3504677762714518260)
XLA Ops:
  0.0 4.7 %prepare.1 = (f32[8,512,128]{2,1,0:T(8,128)S(1)}, f32[8,512,128]{2,1,0:T(8,128)S(1)}, f32[4,1040,128]{2,1,0:T(8,128)S(1)}, f32[4,1040,128]{2,1,0:T(8,128)S(1)}, ...) custom-call(f32[512,1024]{1,0:T(8,128)} %elev.1, ...), custom_call_target="tpu_custom_call" | custom-call | tf_op jit(solution)/shard_map/prepare/pallas_call | solution.py:147
  4.7 3.0 %collective-permute-start = (f32[10,16,128]{2,1,0:T(8,128)S(1)}, f32[10,16,128]{2,1,0:T(8,128)S(1)}, u32[]{:S(2)}, u32[]{:S(2)}) collective-permute-start(f32[10,16,128]{2,1,0:T(8,128)S(1)} %get-tuple-element.21), channel_id=1, source_target_pairs={{0,8},{8,16},{16,24},{24,0},{1,9},{9,17},{17,25},{25,1},{2,10},{10... | collective-permute-start | bytes 245768 | tf_op jit(solution)/shard_map/ppermute | solution.py:655
  7.7 1.0 %collective-permute-start.1 = (f32[10,16,128]{2,1,0:T(8,128)S(1)}, f32[10,16,128]{2,1,0:T(8,128)S(1)}, u32[]{:S(2)}, u32[]{:S(2)}) collective-permute-start(f32[10,16,128]{2,1,0:T(8,128)S(1)} %get-tuple-element.22), channel_id=1, source_target_pairs={{0,24},{8,0},{16,8},{24,16},{1,25},{9,1},{17,9},{25,17},{2,26},{10... | collective-permute-start | bytes 245768 | tf_op jit(solution)/shard_map/ppermute | solution.py:655
  8.7 10.1 %middle.1.partial = f32[512,1024]{1,0:T(8,128)} custom-call(f32[4,1040,128]{2,1,0:T(8,128)S(1)} %get-tuple-element.23.ground_t, f32[4,1040,128]{2,1,0:T(8,128)S(1)} %get-tuple-element.24.lock_t, f32[3,64,128]{2,1,0:T(8,128)S(1)} %get-tuple-element.25.stats_t), custom_call_target="tpu_custom_call" | custom-call | flops 100000000 | bytes 20000000 | tf_op jit(solution)/shard_map/middle/pallas_call | solution.py:384
  18.8 0.0 collective-permute-done.from_north
  18.8 0.0 collective-permute-done.1.from_south
  18.8 0.4 %pack.1 = (f32[80,128]{1,0:T(8,128)S(1)}, f32[80,128]{1,0:T(8,128)S(1)}) custom-call(f32[8,512,128]{2,1,0:T(8,128)S(1)} %get-tuple-element.18.g_first.g_last.ground, f32[8,512,128]{2,1,0:T(8,128)S(1)} %get-tuple-element.19.k_first.k_last.lock, f32[8,512,128]{2,1,0:T(8,128)S(1)} %get-tuple-element.18.g_first.g_last.ground, ...), custom_call_target="tpu_custom_call" | custom-call | tf_op jit(solution)/shard_map/pack/pallas_call | solution.py:529
  19.2 0.1 collective-permute-start.2
  19.3 3.5 %collective-permute-start.3 = (f32[80,128]{1,0:T(8,128)S(1)}, f32[80,128]{1,0:T(8,128)S(1)}, u32[]{:S(2)}, u32[]{:S(2)}) collective-permute-start(f32[80,128]{1,0:T(8,128)S(1)} %get-tuple-element.29), channel_id=1, source_target_pairs={{0,7},{1,0},{2,1},{3,2},{4,3},{5,4},{6,5},{7,6},{8,15},{9,8},{10,9... | collective-permute-start | bytes 122888 | tf_op jit(solution)/shard_map/ppermute | solution.py:655
  22.8 5.0 %bands.1.partial = f32[512,1024]{1,0:T(8,128)} custom-call(f32[8,512,128]{2,1,0:T(8,128)S(1)} %get-tuple-element.18.g_first.g_last.ground, f32[8,512,128]{2,1,0:T(8,128)S(1)} %get-tuple-element.19.k_first.k_last.lock, f32[96,128]{1,0:T(8,128)S(1)} %get-tuple-element.20.stats, ...), custom_call_target="tpu_custom_call", output_to_operand_aliasing={{}: (5, {})} | custom-call | flops 60000000 | bytes 12000000 | tf_op jit(solution)/shard_map/bands/pallas_call | solution.py:466
  27.8 0.0 collective-permute-done.2.from_west
  27.8 0.0 collective-permute-done.3.from_east
  27.9 6.4 %strips.1 = f32[512,1024]{1,0:T(8,128)} custom-call(f32[8,512,128]{2,1,0:T(8,128)S(1)} %get-tuple-element.18.g_first.g_last.ground, f32[8,512,128]{2,1,0:T(8,128)S(1)} %get-tuple-element.19.k_first.k_last.lock, f32[8,512,128]{2,1,0:T(8,128)S(1)} %get-tuple-element.18.g_first.g_last.ground, ...), custom_call_target="tpu_custom_call", output_to_operand_aliasing={{}: (9, {})} | custom-call | tf_op jit(solution)/shard_map/strips/pallas_call | solution.py:632
Async XLA Ops:
  4.7 14.1 %collective-permute-start = (f32[10,16,128]{2,1,0:T(8,128)S(1)}, f32[10,16,128]{2,1,0:T(8,128)S(1)}, u32[]{:S(2)}, u32[]{:S(2)}) collective-permute-start(f32[10,16,128]{2,1,0:T(8,128)S(1)} %get-tuple-element.21), channel_id=1, source_target_pairs={{0,8},{8,16},{16,24},{24,0},{1,9},{9,17},{17,25},{25,1},{2,10},{10... | collective-permute-start | bytes 245768 | tf_op jit(solution)/shard_map/ppermute | solution.py:655
  7.7 11.1 %collective-permute-start.1 = (f32[10,16,128]{2,1,0:T(8,128)S(1)}, f32[10,16,128]{2,1,0:T(8,128)S(1)}, u32[]{:S(2)}, u32[]{:S(2)}) collective-permute-start(f32[10,16,128]{2,1,0:T(8,128)S(1)} %get-tuple-element.22), channel_id=1, source_target_pairs={{0,24},{8,0},{16,8},{24,16},{1,25},{9,1},{17,9},{25,17},{2,26},{10... | collective-permute-start | bytes 245768 | tf_op jit(solution)/shard_map/ppermute | solution.py:655
  19.2 8.6 %collective-permute-start.2 = (f32[80,128]{1,0:T(8,128)S(1)}, f32[80,128]{1,0:T(8,128)S(1)}, u32[]{:S(2)}, u32[]{:S(2)}) collective-permute-start(f32[80,128]{1,0:T(8,128)S(1)} %get-tuple-element.28), channel_id=1, source_target_pairs={{0,1},{1,2},{2,3},{3,4},{4,5},{5,6},{6,7},{7,0},{8,9},{9,10},{10,1... | collective-permute-start | bytes 122888 | tf_op jit(solution)/shard_map/ppermute | solution.py:655
  19.3 8.6 %collective-permute-start.3 = (f32[80,128]{1,0:T(8,128)S(1)}, f32[80,128]{1,0:T(8,128)S(1)}, u32[]{:S(2)}, u32[]{:S(2)}) collective-permute-start(f32[80,128]{1,0:T(8,128)S(1)} %get-tuple-element.29), channel_id=1, source_target_pairs={{0,7},{1,0},{2,1},{3,2},{4,3},{5,4},{6,5},{7,6},{8,15},{9,8},{10,9... | collective-permute-start | bytes 122888 | tf_op jit(solution)/shard_map/ppermute | solution.py:655

commit v3 on v2

v3 whole, which is shorter than its diff:
```python
import functools

import jax
import jax.numpy as jnp
from jax import lax
from jax.experimental import pallas as pl
from jax.experimental.pallas import tpu as pltpu
from jax.sharding import PartitionSpec as P

BLK = 16
COARSE = 4
FINE = 8
LANES = 128
SUB = 8
HALO_C = 8
UNROLL = 22
UNROLL_T = 37

huge_level = 1e30
fine_step = 2.0 ** (-10)
coarse_step = 2.0 ** (-6)
MIB = 2**20


def roll(x, shift, axis):
    return pltpu.roll(x, shift % x.shape[axis], axis)


def lane_iota(shape=(SUB, LANES)):
    return lax.broadcasted_iota(jnp.int32, shape, 1)


def gather_lanes(x, index):
    return jnp.take_along_axis(x, index, axis=1, mode="promise_in_bounds")


def interior(tiles):
    margin = COARSE * BLK
    chunk = (tiles * LANES - 2 * margin) // SUB
    return margin, chunk


def plane_row(col, tiles):
    margin, chunk = interior(tiles)
    return col + (col + chunk - margin) // chunk


def plane_rows(tiles):
    return -(-(plane_row(tiles * LANES, tiles) + 1) // SUB) * SUB


def prepare_kernel(
    elev, ocean, outlet, floor, lock, floor_t, lock_t, stats, stats_t, north, south,
    elev_buf, ocean_buf, outlet_buf, turn, sems,
):
    tiles, rows, _ = floor.shape
    planes = rows // LANES
    blocks = rows // BLK
    lane = lane_iota()
    sub = lax.broadcasted_iota(jnp.int32, (SUB, LANES), 0)

    def copies(j):
        cols = pl.ds(pl.multiple_of(j * LANES, LANES), LANES)
        return [
            pltpu.make_async_copy(src.at[:, cols], dst.at[j], sems.at[n, j])
            for n, (src, dst) in enumerate(
                ((elev, elev_buf), (ocean, ocean_buf), (outlet, outlet_buf))
            )
        ]

    for j in range(tiles):
        for copy in copies(j):
            copy.start()
    turn[...] = jnp.zeros(turn.shape, jnp.float32)
    for band in (north, south):
        band[tiles:, :, :] = jnp.zeros((2, 2 * FINE, LANES), jnp.float32)

    def tile(j, carry):
        for copy in copies(j):
            copy.wait()
        is_ocean = ocean_buf[j] == 1
        g = jnp.where(is_ocean, jnp.float32(0.0), elev_buf[j])
        k = jnp.where(is_ocean | (outlet_buf[j] == 1), g, jnp.float32(huge_level))
        low = jnp.minimum(g, k)
        elev_buf[j] = g
        floor[j] = low
        lock[j] = k
        north[j, 0:FINE, :] = low[0:FINE]
        north[j, FINE:, :] = k[0:FINE]
        south[j, 0:FINE, :] = low[rows - FINE :]
        south[j, FINE:, :] = k[rows - FINE :]
        found = [[None] * 8 for _ in range(3)]
        for c in range(planes):
            turned = [
                jnp.concatenate(
                    [
                        ref[j, pl.ds(a * SUB * planes + c, SUB, stride=planes), :]
                        for a in range(LANES // SUB)
                    ],
                    axis=0,
                ).T
                for ref in (elev_buf, lock)
            ]
            for v in range(LANES // SUB):
                g, k = (x[v * SUB : (v + 1) * SUB] for x in turned)
                at = plane_row(j * LANES + v * SUB, tiles)
                floor_t[c, pl.ds(at, SUB), :] = jnp.minimum(g, k)
                lock_t[c, pl.ds(at, SUB), :] = k
                for to, pick, value in ((0, jnp.minimum, g), (1, jnp.minimum, k), (2, jnp.maximum, g)):
                    old = found[to][v // 2]
                    found[to][v // 2] = value if old is None else pick(old, value)
        for which in range(3):
            pick = jnp.maximum if which == 2 else jnp.minimum
            total = None
            for b in range(8):
                value = found[which][b]
                for shift in (4, 2, 1):
                    value = pick(value, roll(value, shift, 0))
                total = value if b == 0 else jnp.where(sub == b, value, total)
            for swap in (1, 2):
                total = pick(total, gather_lanes(total, lane ^ swap))
            at = pl.ds(pl.multiple_of(j * SUB, SUB), SUB)
            stats_t[which, at, :] = total
            turn[which, at, :] = total
        return carry

    lax.fori_loop(0, tiles, tile, 0)
    for which in range(3):
        turn[which] = turn[which].T
        for q in range(blocks // SUB):
            stats[which * blocks + q * SUB : which * blocks + (q + 1) * SUB, :] = turn[
                which, pl.ds(q * SUB * BLK // planes, SUB, stride=BLK // planes), :
            ]
        slot = tiles + which // 2
        at = (which % 2) * HALO_C
        first = which * blocks
        north[slot, at : at + HALO_C, :] = stats[first : first + HALO_C, :]
        south[slot, at : at + HALO_C, :] = stats[first + blocks - HALO_C : first + blocks, :]


def prepare(elevation, ocean, outlet):
    rows, cols = elevation.shape
    tiles = cols // LANES
    f32 = jnp.float32
    hbm = pl.BlockSpec(memory_space=pltpu.HBM)
    vmem = pl.BlockSpec(memory_space=pltpu.VMEM)
    natural = (tiles, rows, LANES)
    turned = (rows // LANES, plane_rows(tiles), LANES)
    band = (tiles + 2, 2 * FINE, LANES)
    shapes = [natural, natural, turned, turned, (3 * rows // BLK, LANES), (3, cols // BLK, LANES), band, band]
    return pl.pallas_call(
        prepare_kernel,
        in_specs=[hbm] * 3,
        out_specs=[vmem] * len(shapes),
        out_shape=[jax.ShapeDtypeStruct(shape, f32) for shape in shapes],
        scratch_shapes=[
            pltpu.VMEM(natural, f32),
            pltpu.VMEM(natural, jnp.int32),
            pltpu.VMEM(natural, jnp.int32),
            pltpu.VMEM((3, LANES, LANES), f32),
            pltpu.SemaphoreType.DMA((3, tiles)),
        ],
        compiler_params=pltpu.CompilerParams(vmem_limit_bytes=24 * MIB),
        name="prepare",
    )(*(pltpu.with_memory_space_constraint(x, pltpu.HBM) for x in (elevation, ocean, outlet)))


def sealed(value, is_edge):
    return jnp.where(is_edge, jnp.float32(huge_level), value)


def edges():
    pos = lax.axis_index("row")
    return pos == 0, pos == lax.axis_size("row") - 1


def coarse_fields(stats, from_north, from_south):
    tiles = from_north.shape[0] - 2
    blocks = stats.shape[0] // 3
    at_north, at_south = edges()
    fields = []
    for which in range(3):
        slot = tiles + which // 2
        at = (which % 2) * HALO_C
        top = sealed(from_north[slot, at : at + HALO_C, :], at_north)
        low = sealed(from_south[slot, at : at + HALO_C, :], at_south)
        mid = stats[which * blocks : (which + 1) * blocks, :]
        fields.append(jnp.concatenate([top, mid, low], axis=0))
    return fields


def coarse_sweeps(ground_c, lock_c, value):
    for _ in range(COARSE):
        across = jnp.minimum(value, jnp.minimum(roll(value, 1, 1), roll(value, -1, 1)))
        around = jnp.minimum(across, jnp.minimum(roll(across, 1, 0), roll(across, -1, 0)))
        lowered = jnp.minimum(value, around + coarse_step)
        value = jnp.minimum(jnp.maximum(ground_c, lowered), lock_c)
    return value


def start_value(floor, lock, lifted):
    return jnp.maximum(floor, jnp.minimum(lifted, lock))


def across_min(tiles, lane, joined):
    count = len(tiles)
    left = [roll(v, 1, 1) for v in tiles]
    right = [roll(v, -1, 1) for v in tiles]
    out = []
    for j in range(count):
        west, east = left[j], right[j]
        if joined:
            west = jnp.where(lane == 0, left[j - 1], west)
            east = jnp.where(lane == LANES - 1, right[(j + 1) % count], east)
        out.append(jnp.minimum(tiles[j], jnp.minimum(west, east)))
    return out


def fine_sweep(src, dst, floor, stride, joined):
    count = src.shape[0]
    lane = lane_iota()

    def load(t):
        return [src[j, pl.ds(t, SUB, stride=stride), :] for j in range(count)]

    first = load(0)
    h_first = across_min(first, lane, joined)
    h_before = [roll(h, 1, 0) for h in across_min(load(stride - 1), lane, joined)]

    def advance(t, carry, after=None):
        h_up, h_here, here = carry
        if after is None:
            below = load(t + 1)
            h_down = across_min(below, lane, joined)
        else:
            below, h_down = here, after
        for j in range(count):
            low = jnp.minimum(jnp.minimum(h_up[j], h_down[j]), h_here[j])
            at = pl.ds(t, SUB, stride=stride)
            dst[j, at, :] = jnp.maximum(floor[j, at, :], jnp.minimum(here[j], low + fine_step))
        return h_here, h_down, below

    def body(q, carry):
        for u in range(UNROLL):
            carry = advance(q * UNROLL + u, carry)
        return carry

    loops = (stride - 1) // UNROLL
    carry = lax.fori_loop(0, loops, body, (h_before, h_first, first))
    for t in range(loops * UNROLL, stride - 1):
        carry = advance(t, carry)
    advance(stride - 1, carry, [roll(h, -1, 0) for h in h_first])


def turned_sweeps(count, planes, load, store, load_floor):
    def across(tiles):
        up = [roll(tiles[planes - 1], 1, 1)] + tiles[:-1]
        down = tiles[1:] + [roll(tiles[0], -1, 1)]
        return [jnp.minimum(jnp.minimum(u, v), d) for u, v, d in zip(up, tiles, down)]

    def lowered(west, here, east, value, low):
        out = []
        for w, h, e, v, f in zip(west, here, east, value, low):
            around = jnp.minimum(jnp.minimum(w, e), h)
            out.append(jnp.maximum(f, jnp.minimum(v, around + fine_step)))
        return out

    def eastward(tiles):
        return [roll(h, 1, 0) for h in tiles]

    def westward(tiles):
        return [roll(h, -1, 0) for h in tiles]

    value_a, value_b, value_z = load(0), load(1), load(count - 1)
    h_a, h_b, h_z = across(value_a), across(value_b), across(value_z)
    h_y = across(load(count - 2))
    low_a = load_floor(0)
    once_z = lowered(h_y, h_z, westward(h_a), value_z, load_floor(count - 1))
    once_a = lowered(eastward(h_z), h_a, h_b, value_a, low_a)
    g_a = across(once_a)

    def advance(t, carry, h_next=None, g_next=None):
        h_here, h_east, v_east, g_west, g_here, once, low = carry
        if g_next is None:
            v_next = v_east
            if h_next is None:
                v_next = load(t + 2)
                h_next = across(v_next)
            low_east = load_floor(t + 1)
            once_east = lowered(h_here, h_east, h_next, v_east, low_east)
            g_next = across(once_east)
            carry = (h_east, h_next, v_next, g_here, g_next, once_east, low_east)
        for c, value in enumerate(lowered(g_west, g_here, g_next, once, low)):
            store(c, t, value)
        return carry

    def body(q, carry):
        for u in range(UNROLL_T):
            carry = advance(q * UNROLL_T + u, carry)
        return carry

    loops = (count - 2) // UNROLL_T
    carry = (h_a, h_b, value_b, eastward(across(once_z)), g_a, once_a, low_a)
    carry = lax.fori_loop(0, loops, body, carry)
    for t in range(loops * UNROLL_T, count - 2):
        carry = advance(t, carry)
    carry = advance(count - 2, carry, h_next=westward(h_a))
    advance(count - 1, carry, g_next=westward(g_a))


def main_kernel(floor_t, lock_t, stats_t, natural, va, vb, coarse, turned):
    tiles, rows, _ = natural.shape
    planes = rows // LANES
    margin, chunk = interior(tiles)
    first = plane_row(margin, tiles)
    pitch = chunk + 1
    value = stats_t[2]
    for _ in range(COARSE):
        across = jnp.minimum(value, jnp.minimum(roll(value, 1, 0), roll(value, -1, 0)))
        reach = BLK // planes
        around = jnp.minimum(across, jnp.minimum(roll(across, reach, 1), roll(across, -reach, 1)))
        lowered = jnp.minimum(value, around + coarse_step)
        value = jnp.minimum(jnp.maximum(stats_t[0], lowered), stats_t[1])
    coarse[...] = value

    def strided(ref):
        return lambda t: [ref[c, pl.ds(first + t, SUB, stride=pitch), :] for c in range(planes)]

    load_floor, load_lock = strided(floor_t), strided(lock_t)

    def load_start(t):
        lifted = coarse[pl.ds(margin // BLK + t // BLK, SUB, stride=chunk // BLK), :]
        return [start_value(f, k, lifted) for f, k in zip(load_floor(t), load_lock(t))]

    passes = FINE // 2
    src = None
    for n in range(passes):
        dst = (va, vb)[n % 2]

        def load(t):
            return load_start(t) if src is None else [src[c, t] for c in range(planes)]

        def store(c, t, value):
            if n == passes - 1:
                turned[c, pl.ds(first + t, SUB, stride=pitch), :] = value
            else:
                dst[c, t] = value

        turned_sweeps(chunk, planes, load, store, load_floor)
        src = dst

    cols = tiles * LANES
    for c in range(planes):
        for col in list(range(0, margin, SUB)) + list(range(cols - margin, cols, SUB)):
            at = plane_row(col, tiles)
            turned[c, at : at + SUB, :] = jnp.zeros((SUB, LANES), jnp.float32)

    def finish(j, carry):
        for c in range(planes):
            parts = []
            for v in range(LANES // SUB):
                at = plane_row(j * LANES + v * SUB, tiles)
                parts.append(turned[c, pl.ds(at, SUB), :])
            back = jnp.concatenate(parts, axis=0).T
            for a in range(LANES // SUB):
                natural[j, pl.ds(a * SUB * planes + c, SUB, stride=planes), :] = back[
                    a * SUB : (a + 1) * SUB
                ]
        return carry

    lax.fori_loop(0, tiles, finish, 0, unroll=2)


def main_part(floor_t, lock_t, stats_t):
    planes, length, _ = floor_t.shape
    tiles = stats_t.shape[1] * BLK // LANES
    chunk = interior(tiles)[1]
    vmem = pl.BlockSpec(memory_space=pltpu.VMEM)
    tall = (planes, chunk, SUB, LANES)
    f32 = jnp.float32
    return pl.pallas_call(
        main_kernel,
        in_specs=[vmem] * 3,
        out_specs=vmem,
        out_shape=jax.ShapeDtypeStruct((tiles, planes * LANES, LANES), f32),
        scratch_shapes=[
            pltpu.VMEM(tall, f32),
            pltpu.VMEM(tall, f32),
            pltpu.VMEM(stats_t.shape[1:], f32),
            pltpu.VMEM((planes, length, LANES), f32),
        ],
        compiler_params=pltpu.CompilerParams(vmem_limit_bytes=16 * MIB),
        cost_estimate=pl.CostEstimate(flops=100_000_000, bytes_accessed=20_000_000, transcendentals=0),
        name="middle",
    )(floor_t, lock_t, stats_t)


def bands_kernel(floor_in, lock, stats, from_north, from_south, va, vb, floor, lifted):
    tiles, rows, _ = floor_in.shape
    blocks = rows // BLK
    height = va.shape[2]
    inner = height - FINE
    at_north, at_south = edges()
    coarse = coarse_sweeps(*coarse_fields(stats, from_north, from_south))
    lane = lane_iota(coarse.shape)
    for j in range(tiles):
        lifted[j] = gather_lanes(coarse, lane // BLK + 8 * j)
    for side, (band, is_edge, at_band, at_inner, first) in enumerate(
        ((from_north, at_north, 0, FINE, 0), (from_south, at_south, inner, 0, rows - inner))
    ):
        for j in range(tiles):

            def put(at, low, k, c_row):
                floor[side, j, at : at + SUB, :] = low
                va[side, j, at : at + SUB, :] = start_value(low, k, lifted[j, c_row : c_row + 1, :])

            put(
                at_band,
                sealed(band[j, 0:FINE, :], is_edge),
                sealed(band[j, FINE:, :], is_edge),
                HALO_C - 1 if side == 0 else HALO_C + blocks,
            )
            for i in range(inner // SUB):
                at = slice(first + i * SUB, first + (i + 1) * SUB)
                c_row = HALO_C + (first + i * SUB) // BLK
                put(at_inner + i * SUB, floor_in[j, at, :], lock[j, at, :], c_row)

    def pair(i, carry):
        for src, dst in ((va, vb), (vb, va)):
            for side in range(2):
                fine_sweep(src.at[side], dst.at[side], floor.at[side], height // SUB, True)
        return carry

    lax.fori_loop(0, FINE // 2, pair, 0)


def bands(floor, lock, stats, from_north, from_south):
    tiles, rows, _ = floor.shape
    blocks = rows // BLK
    vmem = pl.BlockSpec(memory_space=pltpu.VMEM)
    tall = (2, tiles, COARSE * BLK + 3 * FINE, LANES)
    f32 = jnp.float32
    return pl.pallas_call(
        bands_kernel,
        in_specs=[vmem] * 5,
        out_specs=vmem,
        out_shape=jax.ShapeDtypeStruct(tall, f32),
        scratch_shapes=[
            pltpu.VMEM(tall, f32),
            pltpu.VMEM(tall, f32),
            pltpu.VMEM((tiles, blocks + 2 * HALO_C, LANES), f32),
        ],
        compiler_params=pltpu.CompilerParams(vmem_limit_bytes=12 * MIB),
        cost_estimate=pl.CostEstimate(flops=60_000_000, bytes_accessed=12_000_000, transcendentals=0),
        name="bands",
    )(floor, lock, stats, from_north, from_south)


def strip_planes(rows):
    return -(-(rows + 2 * FINE) // LANES)


def pack_kernel(
    f_first, k_first, f_last, k_last, stats, from_north, from_south, west, east, turned, tall
):
    rows = f_first.shape[1]
    blocks = rows // BLK
    tiles = from_north.shape[0] - 2
    planes = turned.shape[2]
    at_north, at_south = edges()
    group = lane_iota() // 8
    fields = coarse_fields(stats, from_north, from_south)
    coarse = fields[0].shape[0] // SUB
    coarse_cols = tiles * LANES // BLK
    rest = tall.shape[2] - rows - 2 * FINE
    for side, (dst, refs, j, col_at, lane_at) in enumerate(
        (
            (west, (f_first, k_first), 0, 0, 0),
            (east, (f_last, k_last), tiles - 1, LANES - FINE, coarse_cols - 8),
        )
    ):
        for which, ref in enumerate(refs):
            at = slice(which * FINE, (which + 1) * FINE)
            tall[side, which, 0:FINE, :] = sealed(from_north[j, at, :], at_north)
            tall[side, which, FINE : FINE + rows, :] = ref[0]
            tall[side, which, FINE + rows : 2 * FINE + rows, :] = sealed(from_south[j, at, :], at_south)
            tall[side, which, 2 * FINE + rows :, :] = jnp.full((rest, LANES), huge_level, jnp.float32)
            for c in range(planes):
                parts = [
                    tall[side, which, pl.ds(a * SUB * planes + c, SUB, stride=planes), :]
                    for a in range(LANES // SUB)
                ]
                value = jnp.concatenate(parts, axis=0).T
                turned[side, which, c] = value
                slot = which * planes + c
                dst[slot * SUB : (slot + 1) * SUB, :] = value[col_at : col_at + FINE]
        sources = [field[i * SUB : (i + 1) * SUB] for field in fields for i in range(coarse)]
        for n in range(0, len(sources), 16):
            packed = jnp.zeros((SUB, LANES), jnp.float32)
            for m, value in enumerate(sources[n : n + 16]):
                packed = jnp.where(group == m, roll(value, 8 * m - lane_at, 1), packed)
            slot = 2 * planes + n // 16
            dst[slot * SUB : (slot + 1) * SUB, :] = packed


def pack_columns(floor, lock, stats, from_north, from_south):
    tiles, rows, _ = floor.shape
    blocks = rows // BLK
    planes = strip_planes(rows)
    slots = 2 * planes + -(-3 * (blocks + 2 * HALO_C) // SUB // 16)
    first = pl.BlockSpec((1, rows, LANES), lambda i: (0, 0, 0))
    last = pl.BlockSpec((1, rows, LANES), lambda i: (tiles - 1, 0, 0))
    whole = lambda x: pl.BlockSpec(x.shape, lambda i: (0,) * len(x.shape))
    f32 = jnp.float32
    out = jax.ShapeDtypeStruct((slots * SUB, LANES), f32)
    turned = jax.ShapeDtypeStruct((2, 2, planes, LANES, LANES), f32)
    return pl.pallas_call(
        pack_kernel,
        grid=(1,),
        in_specs=[first, first, last, last, whole(stats), whole(from_north), whole(from_south)],
        out_specs=[whole(out), whole(out), whole(turned)],
        out_shape=[out, out, turned],
        scratch_shapes=[pltpu.VMEM((2, 2, planes * LANES, LANES), f32)],
        compiler_params=pltpu.CompilerParams(vmem_limit_bytes=12 * MIB),
        name="pack",
    )(floor, lock, floor, lock, stats, from_north, from_south)


def strip_kernel(
    stats, from_north, from_south, turned, from_west, from_east, natural, banded,
    out, va, vb, floor, lifted, tall, edge, sems, edge_sems,
):
    tiles, rows, _ = natural.shape
    planes = turned.shape[2]
    coarse_cols = tiles * LANES // BLK
    lane = lane_iota()
    width = va.shape[2]
    inner = width - FINE
    valid = inner - FINE
    spans = (
        (pl.ds(0, valid), lambda j: banded.at[0, j, pl.ds(FINE, valid), :]),
        (pl.ds(valid, rows - 2 * valid), lambda j: natural.at[j, pl.ds(valid, rows - 2 * valid), :]),
        (pl.ds(rows - valid, valid), lambda j: banded.at[1, j, pl.ds(FINE, valid), :]),
    )
    copies = [
        pltpu.make_async_copy(part(j), out.at[span, pl.ds(j * LANES, LANES)], sems.at[n, j])
        for j in range(1, tiles - 1)
        for n, (span, part) in enumerate(spans)
    ]
    for copy in copies:
        copy.start()

    def piece(ref, n, to):
        slot = 2 * planes + n // 16
        return roll(ref[slot * SUB : (slot + 1) * SUB, :], to - 8 * (n % 16), 1)

    fields = []
    for which, field in enumerate(coarse_fields(stats, from_north, from_south)):
        parts = []
        count = field.shape[0] // SUB
        for i in range(count):
            n = which * count + i
            here = field[i * SUB : (i + 1) * SUB]
            here = jnp.where(lane // 8 == coarse_cols // 8, piece(from_east, n, coarse_cols), here)
            here = jnp.where(lane // 8 == 15, piece(from_west, n, LANES - 8), here)
            parts.append(here)
        fields.append(jnp.concatenate(parts, axis=0))
    value = coarse_sweeps(*fields)
    value = jnp.concatenate([value, jnp.zeros((LANES - value.shape[0], LANES), jnp.float32)], axis=0).T
    for c in range(planes):
        index = (planes * lane + (c + HALO_C * BLK - FINE)) // BLK
        for side, groups in enumerate(((LANES - 8, 0), (coarse_cols - 8, coarse_cols))):
            for n, at in enumerate(groups):
                lifted[side, c, n * SUB : (n + 1) * SUB, :] = gather_lanes(value[at : at + SUB], index)

    for side, ref in enumerate((from_west, from_east)):
        for c in range(planes):
            for i in range(width // SUB):
                if (side, i) in ((0, 0), (1, width // SUB - 1)):
                    low, k = (ref[(w * planes + c) * SUB : (w * planes + c + 1) * SUB, :] for w in range(2))
                else:
                    col = (i - 1) * SUB if side == 0 else LANES - inner + i * SUB
                    low, k = (turned[side, w, c, col : col + SUB, :] for w in range(2))
                c_row = (i + 15) // 2 if side == 0 else 8 - COARSE - 1 + i // 2
                at = slice(i * SUB, (i + 1) * SUB)
                floor[side, c, at, :] = low
                va[side, c, at, :] = start_value(low, k, lifted[side, c, c_row : c_row + 1, :])

    count = width // SUB

    def strided(ref, side):
        return lambda t: [ref[side, c, pl.ds(t, SUB, stride=count), :] for c in range(planes)]

    def twice(i, carry):
        for src, dst in ((va, vb), (vb, va)):
            for side in range(2):

                def store(c, t, value):
                    dst[side, c, pl.ds(t, SUB, stride=count), :] = value

                turned_sweeps(count, planes, strided(src, side), store, strided(floor, side))
        return carry

    lax.fori_loop(0, FINE // 4, twice, 0)

    stores = []
    for side, j in enumerate((0, tiles - 1)):
        fill = jnp.zeros((LANES - inner, LANES), jnp.float32)
        for c in range(planes):
            parts = [va[side, c, FINE:, :], fill] if side == 0 else [fill, va[side, c, 0:inner, :]]
            back = jnp.concatenate(parts, axis=0).T
            for a in range(LANES // SUB):
                tall[side, pl.ds(a * SUB * planes + c, SUB, stride=planes), :] = back[a * SUB : (a + 1) * SUB]
        mine = (lane < valid) if side == 0 else (lane >= LANES - valid)
        for i in range(rows // SUB):
            at = i * SUB
            if at < valid:
                other = banded[0, j, FINE + at : FINE + at + SUB, :]
            elif at >= rows - valid:
                at_band = FINE + at - (rows - valid)
                other = banded[1, j, at_band : at_band + SUB, :]
            else:
                other = natural[j, at : at + SUB, :]
            edge[side, at : at + SUB, :] = jnp.where(mine, tall[side, FINE + at : FINE + at + SUB, :], other)
        stores.append(
            pltpu.make_async_copy(edge.at[side], out.at[:, pl.ds(j * LANES, LANES)], edge_sems.at[side])
        )
        stores[-1].start()
    for copy in copies + stores:
        copy.wait()


def strips(stats, from_north, from_south, turned, from_west, from_east, natural, banded):
    tiles, rows, _ = natural.shape
    planes = turned.shape[2]
    vmem = pl.BlockSpec(memory_space=pltpu.VMEM)
    wide = (2, planes, COARSE * BLK + 3 * FINE, LANES)
    f32 = jnp.float32
    return pl.pallas_call(
        strip_kernel,
        in_specs=[vmem] * 8,
        out_specs=pl.BlockSpec(memory_space=pltpu.HBM),
        out_shape=jax.ShapeDtypeStruct((rows, tiles * LANES), f32),
        scratch_shapes=[
            pltpu.VMEM(wide, f32),
            pltpu.VMEM(wide, f32),
            pltpu.VMEM(wide, f32),
            pltpu.VMEM((2, planes, 2 * SUB, LANES), f32),
            pltpu.VMEM((2, planes * LANES, LANES), f32),
            pltpu.VMEM((2, rows, LANES), f32),
            pltpu.SemaphoreType.DMA((3, tiles)),
            pltpu.SemaphoreType.DMA((2,)),
        ],
        compiler_params=pltpu.CompilerParams(vmem_limit_bytes=12 * MIB),
        name="strips",
    )(stats, from_north, from_south, turned, from_west, from_east, natural, banded)


def ring(value, axis, shift):
    count = lax.axis_size(axis)
    return lax.ppermute(value, axis, [(i, (i + shift) % count) for i in range(count)])


def shards(elevation, ocean, outlet):
    floor, lock, floor_t, lock_t, stats, stats_t, north, south = prepare(elevation, ocean, outlet)
    from_south = ring(north, "row", -1)
    from_north = ring(south, "row", 1)
    natural = main_part(floor_t, lock_t, stats_t)
    from_north, from_south, natural = lax.optimization_barrier((from_north, from_south, natural))
    halo_args = (stats, from_north, from_south)
    west, east, turned = pack_columns(floor, lock, *halo_args)
    from_east = ring(west, "col", -1)
    from_west = ring(east, "col", 1)
    banded = bands(floor, lock, *halo_args)
    return strips(*halo_args, turned, from_west, from_east, natural, banded)


def solution(mesh):
    return jax.shard_map(
        shards,
        mesh=mesh,
        in_specs=(P("row", "col"), P("row", "col"), P("row", "col")),
        out_specs=P("row", "col"),
        check_vma=False,
    )
```

time: 34.4 us -> 26.3 us (0.76)
  Pallas kernels: 26.6 us -> 18.5 us
    pallas_call x3, Pallas kernels: 21.5 us -> 13.2 us  [the longest x1 6.18 us: main_part(): pl.pallas_call(main_kernel, in_specs=[vmem] * 3, out_specs=vmem, out_shap...]
  transfers between devices with their start and end apart: 4 -> 4, of which waited for: 0 -> 0; matrix products, arithmetic and copies ran while one was open for 0% -> 0% of each run, Pallas kernels for 44% -> 39%
where the time goes in v3:
time: 26.3 us; the launch traced here: 26.1 us
  Pallas kernels  18.5 us (70%)
  starting transfers between devices  7.6 us (29%)
    ppermute x4, starting transfers between devices, ring(): lax.ppermute(value, axis, [(i, (i + shift) % count) for i in range(count)])  7.6 us
    pallas_call x1, Pallas kernels, main_part(): pl.pallas_call(main_kernel, in_specs=[vmem] * 3, out_specs=vmem, out_shap...  6.18 us
    pallas_call x1, Pallas kernels, prepare(): pl.pallas_call(prepare_kernel, in_specs=[hbm] * 3, out_specs=[vmem] * len...  4.77 us
    pallas_call x1, Pallas kernels, bands(): pl.pallas_call(bands_kernel, in_specs=[vmem] * 5, out_specs=vmem, out_sha...  4.09 us
    pallas_call x1, Pallas kernels, strips(): pl.pallas_call(strip_kernel, in_specs=[vmem] * 8, out_specs=pl.BlockSpec(...  2.93 us
  transfers between devices with their start and end apart: 4, of which 0 were waited for; matrix products, arithmetic and copies ran while one was open for 0% of the time, Pallas kernels for 39%

profile of v3, /device:TPU:0, one launch (start us, length us, event | category | flops | bytes accessed | tf_op | source)
XLA Modules:
  0.0 26.1 jit_solution(1725603839646590597)
XLA Ops:
  0.0 4.8 %prepare.1 = (f32[8,512,128]{2,1,0:T(8,128)S(1)}, f32[8,512,128]{2,1,0:T(8,128)S(1)}, f32[4,1040,128]{2,1,0:T(8,128)S(1)}, f32[4,1040,128]{2,1,0:T(8,128)S(1)}, ...) custom-call(f32[512,1024]{1,0:T(8,128)} %elev.1, ...), custom_call_target="tpu_custom_call" | custom-call | tf_op jit(solution)/shard_map/prepare/pallas_call | solution.py:151
  4.8 3.0 %collective-permute-start = (f32[10,16,128]{2,1,0:T(8,128)S(1)}, f32[10,16,128]{2,1,0:T(8,128)S(1)}, u32[]{:S(2)}, u32[]{:S(2)}) collective-permute-start(f32[10,16,128]{2,1,0:T(8,128)S(1)} %get-tuple-element.20), channel_id=1, source_target_pairs={{0,8},{8,16},{16,24},{24,0},{1,9},{9,17},{17,25},{25,1},{2,10},{10... | collective-permute-start | bytes 245768 | tf_op jit(solution)/shard_map/ppermute | solution.py:661
  7.8 1.0 %collective-permute-start.1 = (f32[10,16,128]{2,1,0:T(8,128)S(1)}, f32[10,16,128]{2,1,0:T(8,128)S(1)}, u32[]{:S(2)}, u32[]{:S(2)}) collective-permute-start(f32[10,16,128]{2,1,0:T(8,128)S(1)} %get-tuple-element.21), channel_id=1, source_target_pairs={{0,24},{8,0},{16,8},{24,16},{1,25},{9,1},{17,9},{25,17},{2,26},{10... | collective-permute-start | bytes 245768 | tf_op jit(solution)/shard_map/ppermute | solution.py:661
  8.8 6.2 %middle.1.natural = f32[8,512,128]{2,1,0:T(8,128)S(1)} custom-call(f32[4,1040,128]{2,1,0:T(8,128)S(1)} %get-tuple-element.22.floor_t, f32[4,1040,128]{2,1,0:T(8,128)S(1)} %get-tuple-element.23.lock_t, f32[3,64,128]{2,1,0:T(8,128)S(1)} %get-tuple-element.24.stats_t), custom_call_target="tpu_custom_call" | custom-call | flops 100000000 | bytes 20000000 | tf_op jit(solution)/shard_map/middle/pallas_call | solution.py:381
  15.0 0.0 collective-permute-done.from_north
  15.0 0.0 collective-permute-done.1.from_south
  15.0 0.5 %pack.1 = (f32[96,128]{1,0:T(8,128)S(1)}, f32[96,128]{1,0:T(8,128)S(1)}, f32[2,2,5,128,128]{4,3,2,1,0:T(8,128)S(1)}) custom-call(f32[8,512,128]{2,1,0:T(8,128)S(1)} %get-tuple-element.27.f_first.f_last.floor_in, f32[8,512,128]{2,1,0:T(8,128)S(1)} %get-tuple-element.28.k_first.k_last.lock, f32[8,512,128]{2,1,0:T(8,128)S(1)} %get-tuple-element.27.f_first.f_last.floor_in, ...), custom_call_target="tpu_custom_call" | custom-call | tf_op jit(solution)/shard_map/pack/pallas_call | solution.py:517
  15.5 0.1 collective-permute-start.2
  15.6 3.5 %collective-permute-start.3 = (f32[96,128]{1,0:T(8,128)S(1)}, f32[96,128]{1,0:T(8,128)S(1)}, u32[]{:S(2)}, u32[]{:S(2)}) collective-permute-start(f32[96,128]{1,0:T(8,128)S(1)} %get-tuple-element.31), channel_id=1, source_target_pairs={{0,7},{1,0},{2,1},{3,2},{4,3},{5,4},{6,5},{7,6},{8,15},{9,8},{10,9... | collective-permute-start | bytes 147464 | tf_op jit(solution)/shard_map/ppermute | solution.py:661
  19.1 4.1 %bands.1.banded = f32[2,8,88,128]{3,2,1,0:T(8,128)S(1)} custom-call(f32[8,512,128]{2,1,0:T(8,128)S(1)} %get-tuple-element.27.f_first.f_last.floor_in, f32[8,512,128]{2,1,0:T(8,128)S(1)} %get-tuple-element.28.k_first.k_last.lock, f32[96,128]{1,0:T(8,128)S(1)} %get-tuple-element.19.stats, f32[10,16,128]{2,1,0:T(8,128)S(1)} %collective-permute-done.from_north, ...), custom_call_target="tpu_custom_call" | custom-call | flops 60000000 | bytes 12000000 | tf_op jit(solution)/shard_map/bands/pallas_call | solution.py:443
  23.2 0.0 collective-permute-done.2.from_west
  23.2 0.0 collective-permute-done.3.from_east
  23.2 2.9 %strips.1 = f32[512,1024]{1,0:T(8,128)} custom-call(f32[96,128]{1,0:T(8,128)S(1)} %get-tuple-element.19.stats, f32[10,16,128]{2,1,0:T(8,128)S(1)} %collective-permute-done.from_north, f32[10,16,128]{2,1,0:T(8,128)S(1)} %collective-permute-done.1.from_south, f32[2,2,5,128,128]{4,3,2,1,0:T(8,128)S(1)} %get-tuple-element.29.turned, ...), custom_call_target="tpu_custom_call" | custom-call | tf_op jit(solution)/shard_map/strips/pallas_call | solution.py:639
Async XLA Ops:
  4.8 10.2 %collective-permute-start = (f32[10,16,128]{2,1,0:T(8,128)S(1)}, f32[10,16,128]{2,1,0:T(8,128)S(1)}, u32[]{:S(2)}, u32[]{:S(2)}) collective-permute-start(f32[10,16,128]{2,1,0:T(8,128)S(1)} %get-tuple-element.20), channel_id=1, source_target_pairs={{0,8},{8,16},{16,24},{24,0},{1,9},{9,17},{17,25},{25,1},{2,10},{10... | collective-permute-start | bytes 245768 | tf_op jit(solution)/shard_map/ppermute | solution.py:661
  7.8 7.2 %collective-permute-start.1 = (f32[10,16,128]{2,1,0:T(8,128)S(1)}, f32[10,16,128]{2,1,0:T(8,128)S(1)}, u32[]{:S(2)}, u32[]{:S(2)}) collective-permute-start(f32[10,16,128]{2,1,0:T(8,128)S(1)} %get-tuple-element.21), channel_id=1, source_target_pairs={{0,24},{8,0},{16,8},{24,16},{1,25},{9,1},{17,9},{25,17},{2,26},{10... | collective-permute-start | bytes 245768 | tf_op jit(solution)/shard_map/ppermute | solution.py:661
  15.5 7.7 %collective-permute-start.2 = (f32[96,128]{1,0:T(8,128)S(1)}, f32[96,128]{1,0:T(8,128)S(1)}, u32[]{:S(2)}, u32[]{:S(2)}) collective-permute-start(f32[96,128]{1,0:T(8,128)S(1)} %get-tuple-element.30), channel_id=1, source_target_pairs={{0,1},{1,2},{2,3},{3,4},{4,5},{5,6},{6,7},{7,0},{8,9},{9,10},{10,1... | collective-permute-start | bytes 147464 | tf_op jit(solution)/shard_map/ppermute | solution.py:661
  15.6 7.6 %collective-permute-start.3 = (f32[96,128]{1,0:T(8,128)S(1)}, f32[96,128]{1,0:T(8,128)S(1)}, u32[]{:S(2)}, u32[]{:S(2)}) collective-permute-start(f32[96,128]{1,0:T(8,128)S(1)} %get-tuple-element.31), channel_id=1, source_target_pairs={{0,7},{1,0},{2,1},{3,2},{4,3},{5,4},{6,5},{7,6},{8,15},{9,8},{10,9... | collective-permute-start | bytes 147464 | tf_op jit(solution)/shard_map/ppermute | solution.py:661

commit v4 on v3

v4 whole, which is shorter than its diff:
```python
import functools

import jax
import jax.numpy as jnp
from jax import lax
from jax.experimental import pallas as pl
from jax.experimental.pallas import tpu as pltpu
from jax.sharding import PartitionSpec as P

BLK = 16
COARSE = 4
FINE = 8
LANES = 128
SUB = 8
HALO_C = 8
UNROLL_T = 112

huge_level = 1e30
fine_step = 2.0 ** (-10)
coarse_step = 2.0 ** (-6)
MIB = 2**20


def roll(x, shift, axis):
    return pltpu.roll(x, shift % x.shape[axis], axis)


def lane_iota(shape=(SUB, LANES)):
    return lax.broadcasted_iota(jnp.int32, shape, 1)


def gather_lanes(x, index):
    return jnp.take_along_axis(x, index, axis=1, mode="promise_in_bounds")


def interior(tiles):
    margin = COARSE * BLK
    chunk = (tiles * LANES - 2 * margin) // SUB
    return margin, chunk


def interior_planes(rows):
    return (rows - 2 * COARSE * BLK) // LANES


def plane_row(col, tiles):
    margin, chunk = interior(tiles)
    return col + (col + chunk - margin) // chunk


def plane_rows(tiles):
    return -(-(plane_row(tiles * LANES, tiles) + 1) // SUB) * SUB


def prepare_kernel(
    elev, ocean, outlet, floor, lock, floor_t, lock_t, stats, stats_t, north, south,
    elev_buf, ocean_buf, outlet_buf, turn, sems,
):
    tiles, rows, _ = floor.shape
    planes = floor_t.shape[0]
    margin = interior(tiles)[0]
    blocks = rows // BLK
    lane = lane_iota()
    sub = lax.broadcasted_iota(jnp.int32, (SUB, LANES), 0)
    unused = jnp.zeros((LANES - 3 * blocks, LANES), jnp.float32)

    def copies(j):
        cols = pl.ds(pl.multiple_of(j * LANES, LANES), LANES)
        return [
            pltpu.make_async_copy(src.at[:, cols], dst.at[j], sems.at[n, j])
            for n, (src, dst) in enumerate(
                ((elev, elev_buf), (ocean, ocean_buf), (outlet, outlet_buf))
            )
        ]

    for j in range(tiles):
        for copy in copies(j):
            copy.start()
    turn[...] = jnp.zeros(turn.shape, jnp.float32)
    for band in (north, south):
        band[tiles:, :, :] = jnp.zeros((2, 2 * FINE, LANES), jnp.float32)

    def tile(j, carry):
        for copy in copies(j):
            copy.wait()
        is_ocean = ocean_buf[j] == 1
        g = jnp.where(is_ocean, jnp.float32(0.0), elev_buf[j])
        k = jnp.where(is_ocean | (outlet_buf[j] == 1), g, jnp.float32(huge_level))
        low = jnp.minimum(g, k)
        elev_buf[j] = g
        floor[j] = low
        lock[j] = k
        north[j, 0:FINE, :] = low[0:FINE]
        north[j, FINE:, :] = k[0:FINE]
        south[j, 0:FINE, :] = low[rows - FINE :]
        south[j, FINE:, :] = k[rows - FINE :]
        for c in range(planes):
            turned = [
                jnp.concatenate(
                    [
                        ref[j, pl.ds(margin + a * SUB * planes + c, SUB, stride=planes), :]
                        for a in range(LANES // SUB)
                    ],
                    axis=0,
                ).T
                for ref in (elev_buf, lock)
            ]
            for v in range(LANES // SUB):
                g, k = (x[v * SUB : (v + 1) * SUB] for x in turned)
                at = plane_row(j * LANES + v * SUB, tiles)
                floor_t[c, pl.ds(at, SUB), :] = jnp.minimum(g, k)
                lock_t[c, pl.ds(at, SUB), :] = k
        found = [[], [], []]
        for q in range(blocks // SUB):
            for r in range(BLK):
                g, k = (ref[j, pl.ds(q * SUB * BLK + r, SUB, stride=BLK), :] for ref in (elev_buf, lock))
                low_g = g if r == 0 else jnp.minimum(low_g, g)
                low_k = k if r == 0 else jnp.minimum(low_k, k)
                high_g = g if r == 0 else jnp.maximum(high_g, g)
            for which, value in enumerate((low_g, low_k, -high_g)):
                found[which].append(value)
        turned = jnp.concatenate(found[0] + found[1] + found[2] + [unused], axis=0).T
        total = None
        for b in range(LANES // BLK):
            value = jnp.minimum(
                turned[b * BLK : b * BLK + SUB], turned[b * BLK + SUB : (b + 1) * BLK]
            )
            for shift in (4, 2, 1):
                value = jnp.minimum(value, roll(value, shift, 0))
            total = value if b == 0 else jnp.where(sub == b, value, total)
        total = jnp.where(lane // blocks == 2, -total, total)
        at = pl.ds(pl.multiple_of(j * SUB, SUB), SUB)
        stats_t[at, :] = total
        turn[at, :] = total
        return carry

    lax.fori_loop(0, tiles, tile, 0)
    stats[...] = turn[...].T[: 3 * blocks]
    for which in range(3):
        slot = tiles + which // 2
        at = (which % 2) * HALO_C
        first = which * blocks
        north[slot, at : at + HALO_C, :] = stats[first : first + HALO_C, :]
        south[slot, at : at + HALO_C, :] = stats[first + blocks - HALO_C : first + blocks, :]


def prepare(elevation, ocean, outlet):
    rows, cols = elevation.shape
    tiles = cols // LANES
    f32 = jnp.float32
    hbm = pl.BlockSpec(memory_space=pltpu.HBM)
    vmem = pl.BlockSpec(memory_space=pltpu.VMEM)
    natural = (tiles, rows, LANES)
    turned = (interior_planes(rows), plane_rows(tiles), LANES)
    band = (tiles + 2, 2 * FINE, LANES)
    shapes = [natural, natural, turned, turned, (3 * rows // BLK, LANES), (cols // BLK, LANES), band, band]
    return pl.pallas_call(
        prepare_kernel,
        in_specs=[hbm] * 3,
        out_specs=[vmem] * len(shapes),
        out_shape=[jax.ShapeDtypeStruct(shape, f32) for shape in shapes],
        scratch_shapes=[
            pltpu.VMEM(natural, f32),
            pltpu.VMEM(natural, jnp.int32),
            pltpu.VMEM(natural, jnp.int32),
            pltpu.VMEM((LANES, LANES), f32),
            pltpu.SemaphoreType.DMA((3, tiles)),
        ],
        compiler_params=pltpu.CompilerParams(vmem_limit_bytes=24 * MIB),
        name="prepare",
    )(*(pltpu.with_memory_space_constraint(x, pltpu.HBM) for x in (elevation, ocean, outlet)))


def sealed(value, is_edge):
    return jnp.where(is_edge, jnp.float32(huge_level), value)


def edges():
    pos = lax.axis_index("row")
    return pos == 0, pos == lax.axis_size("row") - 1


def coarse_fields(stats, from_north, from_south):
    tiles = from_north.shape[0] - 2
    blocks = stats.shape[0] // 3
    at_north, at_south = edges()
    fields = []
    for which in range(3):
        slot = tiles + which // 2
        at = (which % 2) * HALO_C
        top = sealed(from_north[slot, at : at + HALO_C, :], at_north)
        low = sealed(from_south[slot, at : at + HALO_C, :], at_south)
        mid = stats[which * blocks : (which + 1) * blocks, :]
        fields.append(jnp.concatenate([top, mid, low], axis=0))
    return fields


def coarse_sweeps(ground_c, lock_c, value):
    for _ in range(COARSE):
        across = jnp.minimum(value, jnp.minimum(roll(value, 1, 1), roll(value, -1, 1)))
        around = jnp.minimum(across, jnp.minimum(roll(across, 1, 0), roll(across, -1, 0)))
        lowered = jnp.minimum(value, around + coarse_step)
        value = jnp.minimum(jnp.maximum(ground_c, lowered), lock_c)
    return value


def start_value(floor, lock, lifted):
    return jnp.maximum(floor, jnp.minimum(lifted, lock))


def edge_rolls(tiles):
    return roll(tiles[-1], 1, 1), roll(tiles[0], -1, 1)


def grouped_sweep(count, load, edges_at, load_floor, store, store_edges, unroll):
    def plane_min(t, groups):
        out = []
        for (above, below), tiles in zip(edges_at(t, groups), groups):
            line = [above] + tiles + [below]
            mins = []
            for c in range(0, len(tiles), 2):
                pair = jnp.minimum(line[c + 1], line[c + 2])
                mins.append(jnp.minimum(line[c], pair))
                if c + 1 < len(tiles):
                    mins.append(jnp.minimum(pair, line[c + 3]))
            out.append(mins)
        return out

    def each(function, *args):
        return [[function(*values) for values in zip(*groups)] for groups in zip(*args)]

    def least(*args):
        return each(lambda *values: functools.reduce(jnp.minimum, values), *args)

    def finish(t, around, value):
        new = each(
            lambda f, v, m: jnp.maximum(f, jnp.minimum(v, m + fine_step)),
            load_floor(t),
            value,
            around,
        )
        store(t, new)
        if store_edges is not None:
            store_edges(t, new)

    first, last = load(0), load(count - 1)
    h_first = plane_min(0, first)
    h_before = each(lambda h: roll(h, 1, 0), plane_min(count - 1, last))
    h_after = each(lambda h: roll(h, -1, 0), h_first)

    def line_at(t):
        if isinstance(t, int) and t == count:
            return None, h_after
        value = load(t)
        return value, plane_min(t, value)

    def span(start, size, carry):
        h_west, h_here, here = carry
        u = 0
        while u < size:
            t = start + u
            value, h_east = line_at(t + 1)
            pair = least(h_here, h_east)
            finish(t, least(h_west, pair), here)
            if u + 1 < size:
                far, h_far = line_at(t + 2)
                finish(t + 1, least(pair, h_far), value)
                h_west, h_here, here = h_east, h_far, far
                u += 2
            else:
                h_west, h_here, here = h_here, h_east, value
                u += 1
        return h_west, h_here, here

    loops = (count - 1) // unroll
    carry = (h_before, h_first, first)
    if loops:
        carry = lax.fori_loop(0, loops, lambda q, c: span(q * unroll, unroll, c), carry)
    span(loops * unroll, count - loops * unroll, carry)


def main_kernel(
    floor_t, lock_t, stats_t, natural, va, vb, edge_a, edge_b, coarse, spread, turned
):
    tiles, rows, _ = natural.shape
    planes = floor_t.shape[0]
    blocks = rows // BLK
    margin, chunk = interior(tiles)
    first = plane_row(margin, tiles)
    pitch = chunk + 1
    ground_c = stats_t[...]
    lock_c = roll(ground_c, -blocks, 1)
    value = roll(ground_c, -2 * blocks, 1)
    for _ in range(COARSE):
        across = jnp.minimum(value, jnp.minimum(roll(value, 1, 0), roll(value, -1, 0)))
        around = jnp.minimum(across, jnp.minimum(roll(across, 1, 1), roll(across, -1, 1)))
        lowered = jnp.minimum(value, around + coarse_step)
        value = jnp.minimum(jnp.maximum(ground_c, lowered), lock_c)
    coarse[...] = value
    lane = lane_iota()
    for b in range(chunk // BLK):
        part = coarse[pl.ds(margin // BLK + b, SUB, stride=chunk // BLK), :]
        for c in range(planes):
            spread[c, b] = gather_lanes(part, (planes * lane + c + margin) // BLK)

    def strided(ref):
        return lambda t: [[ref[c, pl.ds(first + t, SUB, stride=pitch), :] for c in range(planes)]]

    load_floor, load_lock = strided(floor_t), strided(lock_t)

    def keep_edges(edges):
        def store_edges(t, groups):
            edges[0, t], edges[1, t] = edge_rolls(groups[0])

        return store_edges

    def keep(dst):
        def store(t, groups):
            for c, value in enumerate(groups[0]):
                dst[c, t] = value

        return store

    def start(b, carry):
        for u in range(BLK):
            t = b * BLK + u
            both = zip(load_floor(t)[0], load_lock(t)[0])
            tiles = [[start_value(f, k, spread[c, b]) for c, (f, k) in enumerate(both)]]
            keep(va)(t, tiles)
            keep_edges(edge_a)(t, tiles)
        return carry

    lax.fori_loop(0, chunk // BLK, start, 0, unroll=True)

    def sweep(src, edges_in, store, store_edges):
        grouped_sweep(
            chunk,
            lambda t: [[src[c, t] for c in range(planes)]],
            lambda t, _: [(edges_in[0, t], edges_in[1, t])],
            load_floor,
            store,
            store_edges,
            UNROLL_T,
        )

    def twice(i, carry):
        sweep(va, edge_a, keep(vb), keep_edges(edge_b))
        sweep(vb, edge_b, keep(va), keep_edges(edge_a))
        return carry

    lax.fori_loop(0, FINE // 2 - 1, twice, 0)
    sweep(va, edge_a, keep(vb), keep_edges(edge_b))

    def store_last(t, groups):
        for c, value in enumerate(groups[0]):
            turned[c, pl.ds(first + t, SUB, stride=pitch), :] = value

    sweep(vb, edge_b, store_last, None)
    cols = tiles * LANES
    for c in range(planes):
        for col in list(range(0, margin, SUB)) + list(range(cols - margin, cols, SUB)):
            at = plane_row(col, tiles)
            turned[c, at : at + SUB, :] = jnp.zeros((SUB, LANES), jnp.float32)

    def finish(j, carry):
        for c in range(planes):
            parts = []
            for v in range(LANES // SUB):
                at = plane_row(j * LANES + v * SUB, tiles)
                parts.append(turned[c, pl.ds(at, SUB), :])
            back = jnp.concatenate(parts, axis=0).T
            for a in range(LANES // SUB):
                natural[j, pl.ds(margin + a * SUB * planes + c, SUB, stride=planes), :] = back[
                    a * SUB : (a + 1) * SUB
                ]
        return carry

    lax.fori_loop(0, tiles, finish, 0, unroll=True)


def main_part(floor_t, lock_t, stats_t, rows):
    planes, length, _ = floor_t.shape
    tiles = stats_t.shape[0] * BLK // LANES
    chunk = interior(tiles)[1]
    vmem = pl.BlockSpec(memory_space=pltpu.VMEM)
    tall = (planes, chunk, SUB, LANES)
    f32 = jnp.float32
    return pl.pallas_call(
        main_kernel,
        in_specs=[vmem] * 3,
        out_specs=vmem,
        out_shape=jax.ShapeDtypeStruct((tiles, rows, LANES), f32),
        scratch_shapes=[
            pltpu.VMEM(tall, f32),
            pltpu.VMEM(tall, f32),
            pltpu.VMEM((2, chunk, SUB, LANES), f32),
            pltpu.VMEM((2, chunk, SUB, LANES), f32),
            pltpu.VMEM(stats_t.shape, f32),
            pltpu.VMEM((planes, chunk // BLK, SUB, LANES), f32),
            pltpu.VMEM((planes, length, LANES), f32),
        ],
        compiler_params=pltpu.CompilerParams(vmem_limit_bytes=16 * MIB),
        cost_estimate=pl.CostEstimate(flops=100_000_000, bytes_accessed=20_000_000, transcendentals=0),
        name="middle",
    )(floor_t, lock_t, stats_t)


def split_pair(first, second, even_lane):
    even = jnp.where(even_lane, first, roll(second, 1, 1))
    odd = jnp.where(even_lane, roll(first, -1, 1), second)
    return even, odd


def join_pair(even, odd, even_lane):
    first = jnp.where(even_lane, even, roll(odd, 1, 1))
    second = jnp.where(even_lane, roll(even, -1, 1), odd)
    return first, second


def bands_kernel(
    floor_in, lock, stats, from_north, from_south, out, va_n, va_s, vb_n, vb_s, floor_n, floor_s, lifted
):
    tiles, rows, _ = floor_in.shape
    blocks = rows // BLK
    va, vb, floor = (va_n, va_s), (vb_n, vb_s), (floor_n, floor_s)
    height = va_n.shape[1]
    inner = height - FINE
    pairs = tiles // 2
    at_north, at_south = edges()
    lane = lane_iota()
    even_lane = lane % 2 == 0
    coarse = coarse_sweeps(*coarse_fields(stats, from_north, from_south))
    wide = lane_iota(coarse.shape)
    for j in range(tiles):
        lifted[j] = gather_lanes(coarse, wide // BLK + 8 * j)
    for side, (band, is_edge, at_band, at_inner, first) in enumerate(
        ((from_north, at_north, 0, FINE, 0), (from_south, at_south, inner, 0, rows - inner))
    ):

        def put(at, c_row, fields):
            both = []
            for j in range(2):
                low, k, tile = fields[j]
                both.append((start_value(low, k, lifted[tile, c_row : c_row + 1, :]), low))
            q = fields[0][2]
            for dst, pair in zip((va, floor), zip(*both)):
                for n, value in enumerate(split_pair(*pair, even_lane)):
                    dst[side][q + n, at : at + SUB, :] = value

        for q in range(pairs):
            pair = (2 * q, 2 * q + 1)
            put(
                at_band,
                HALO_C - 1 if side == 0 else HALO_C + blocks,
                [
                    (sealed(band[j, 0:FINE, :], is_edge), sealed(band[j, FINE:, :], is_edge), j)
                    for j in pair
                ],
            )
            for i in range(inner // SUB):
                at = slice(first + i * SUB, first + (i + 1) * SUB)
                c_row = HALO_C + (first + i * SUB) // BLK
                put(at_inner + i * SUB, c_row, [(floor_in[j, at, :], lock[j, at, :], j) for j in pair])

    count = height // SUB
    before = jnp.where(lane < 2, LANES - 1 - lane, lane - 2)
    after = jnp.where(lane < LANES - 2, lane + 2, LANES - 1 - lane)

    def strided(ref):
        return lambda t: [
            [ref[2 * q + n, pl.ds(t, SUB, stride=count), :] for n in range(2)]
            for q in range(pairs)
        ]

    def pair_edges(t, groups):
        above = [gather_lanes(odd, before) for _, odd in groups]
        below = [gather_lanes(even, after) for even, _ in groups]
        return [
            (
                jnp.where(lane == 0, above[q - 1], above[q]),
                jnp.where(lane == LANES - 1, below[(q + 1) % pairs], below[q]),
            )
            for q in range(pairs)
        ]

    def keep(dst):
        def store(t, groups):
            for q, pair in enumerate(groups):
                for n, value in enumerate(pair):
                    dst[2 * q + n, pl.ds(t, SUB, stride=count), :] = value

        return store

    def twice(i, carry):
        for src, dst in ((va, vb), (vb, va)):
            for side in range(2):
                grouped_sweep(
                    count,
                    strided(src[side]),
                    pair_edges,
                    strided(floor[side]),
                    keep(dst[side]),
                    None,
                    count,
                )
        return carry

    lax.fori_loop(0, FINE // 2, twice, 0, unroll=True)
    for side in range(2):
        for i in range(out.shape[2] // SUB):
            at = slice(FINE + i * SUB, FINE + (i + 1) * SUB)
            for q in range(pairs):
                pair = join_pair(va[side][2 * q, at, :], va[side][2 * q + 1, at, :], even_lane)
                for n, value in enumerate(pair):
                    out[side, 2 * q + n, i * SUB : (i + 1) * SUB, :] = value


def bands(floor, lock, stats, from_north, from_south):
    tiles, rows, _ = floor.shape
    blocks = rows // BLK
    vmem = pl.BlockSpec(memory_space=pltpu.VMEM)
    height = COARSE * BLK + 3 * FINE
    tall = (tiles, height, LANES)
    f32 = jnp.float32
    return pl.pallas_call(
        bands_kernel,
        in_specs=[vmem] * 5,
        out_specs=vmem,
        out_shape=jax.ShapeDtypeStruct((2, tiles, height - 2 * FINE, LANES), f32),
        scratch_shapes=[
            *[pltpu.VMEM(tall, f32)] * 6,
            pltpu.VMEM((tiles, blocks + 2 * HALO_C, LANES), f32),
        ],
        compiler_params=pltpu.CompilerParams(vmem_limit_bytes=16 * MIB),
        cost_estimate=pl.CostEstimate(flops=60_000_000, bytes_accessed=12_000_000, transcendentals=0),
        name="bands",
    )(floor, lock, stats, from_north, from_south)


def strip_planes(rows):
    return -(-(rows + 2 * FINE) // LANES)


def pack_kernel(
    floor, lock, stats, from_north, from_south, west, east, turned, tall
):
    tiles, rows, _ = floor.shape
    blocks = rows // BLK
    planes = turned.shape[2]
    at_north, at_south = edges()
    group = lane_iota() // 8
    fields = coarse_fields(stats, from_north, from_south)
    coarse = fields[0].shape[0] // SUB
    coarse_cols = tiles * LANES // BLK
    rest = tall.shape[2] - rows - 2 * FINE
    for side, (dst, j, col_at, lane_at) in enumerate(
        ((west, 0, 0, 0), (east, tiles - 1, LANES - FINE, coarse_cols - 8))
    ):
        for which, ref in enumerate((floor, lock)):
            at = slice(which * FINE, (which + 1) * FINE)
            tall[side, which, 0:FINE, :] = sealed(from_north[j, at, :], at_north)
            tall[side, which, FINE : FINE + rows, :] = ref[j]
            tall[side, which, FINE + rows : 2 * FINE + rows, :] = sealed(from_south[j, at, :], at_south)
            tall[side, which, 2 * FINE + rows :, :] = jnp.full((rest, LANES), huge_level, jnp.float32)
            for c in range(planes):
                parts = [
                    tall[side, which, pl.ds(a * SUB * planes + c, SUB, stride=planes), :]
                    for a in range(LANES // SUB)
                ]
                value = jnp.concatenate(parts, axis=0).T
                turned[side, which, c] = value
                slot = which * planes + c
                dst[slot * SUB : (slot + 1) * SUB, :] = value[col_at : col_at + FINE]
        sources = [field[i * SUB : (i + 1) * SUB] for field in fields for i in range(coarse)]
        for n in range(0, len(sources), 16):
            packed = jnp.zeros((SUB, LANES), jnp.float32)
            for m, value in enumerate(sources[n : n + 16]):
                packed = jnp.where(group == m, roll(value, 8 * m - lane_at, 1), packed)
            slot = 2 * planes + n // 16
            dst[slot * SUB : (slot + 1) * SUB, :] = packed


def pack_columns(floor, lock, stats, from_north, from_south):
    tiles, rows, _ = floor.shape
    blocks = rows // BLK
    planes = strip_planes(rows)
    slots = 2 * planes + -(-3 * (blocks + 2 * HALO_C) // SUB // 16)
    vmem = pl.BlockSpec(memory_space=pltpu.VMEM)
    f32 = jnp.float32
    out = jax.ShapeDtypeStruct((slots * SUB, LANES), f32)
    turned = jax.ShapeDtypeStruct((2, 2, planes, LANES, LANES), f32)
    return pl.pallas_call(
        pack_kernel,
        in_specs=[vmem] * 5,
        out_specs=[vmem] * 3,
        out_shape=[out, out, turned],
        scratch_shapes=[pltpu.VMEM((2, 2, planes * LANES, LANES), f32)],
        compiler_params=pltpu.CompilerParams(vmem_limit_bytes=12 * MIB),
        name="pack",
    )(floor, lock, stats, from_north, from_south)


def strip_kernel(
    stats, from_north, from_south, turned, from_west, from_east, natural, banded,
    out, va_w, va_e, vb_w, vb_e, floor_w, floor_e, lifted, tall, edge, sems, edge_sems,
):
    tiles, rows, _ = natural.shape
    planes = turned.shape[2]
    coarse_cols = tiles * LANES // BLK
    lane = lane_iota()
    va, vb, floor = (va_w, va_e), (vb_w, vb_e), (floor_w, floor_e)
    width = va_w.shape[1]
    inner = width - FINE
    valid = inner - FINE
    spans = (
        (pl.ds(0, valid), lambda j: banded.at[0, j]),
        (pl.ds(valid, rows - 2 * valid), lambda j: natural.at[j, pl.ds(valid, rows - 2 * valid), :]),
        (pl.ds(rows - valid, valid), lambda j: banded.at[1, j]),
    )
    copies = [
        pltpu.make_async_copy(part(j), out.at[span, pl.ds(j * LANES, LANES)], sems.at[n, j])
        for j in range(1, tiles - 1)
        for n, (span, part) in enumerate(spans)
    ]
    for copy in copies:
        copy.start()

    def piece(ref, n, to):
        slot = 2 * planes + n // 16
        return roll(ref[slot * SUB : (slot + 1) * SUB, :], to - 8 * (n % 16), 1)

    fields = []
    for which, field in enumerate(coarse_fields(stats, from_north, from_south)):
        parts = []
        count = field.shape[0] // SUB
        for i in range(count):
            n = which * count + i
            here = field[i * SUB : (i + 1) * SUB]
            here = jnp.where(lane // 8 == coarse_cols // 8, piece(from_east, n, coarse_cols), here)
            here = jnp.where(lane // 8 == 15, piece(from_west, n, LANES - 8), here)
            parts.append(here)
        fields.append(jnp.concatenate(parts, axis=0))
    value = coarse_sweeps(*fields)
    value = jnp.concatenate([value, jnp.zeros((LANES - value.shape[0], LANES), jnp.float32)], axis=0).T
    for c in range(planes):
        index = (planes * lane + (c + HALO_C * BLK - FINE)) // BLK
        for side, groups in enumerate(((LANES - 8, 0), (coarse_cols - 8, coarse_cols))):
            for n, at in enumerate(groups):
                lifted[side, c, n * SUB : (n + 1) * SUB, :] = gather_lanes(value[at : at + SUB], index)

    for side, ref in enumerate((from_west, from_east)):
        for c in range(planes):
            for i in range(width // SUB):
                if (side, i) in ((0, 0), (1, width // SUB - 1)):
                    low, k = (ref[(w * planes + c) * SUB : (w * planes + c + 1) * SUB, :] for w in range(2))
                else:
                    col = (i - 1) * SUB if side == 0 else LANES - inner + i * SUB
                    low, k = (turned[side, w, c, col : col + SUB, :] for w in range(2))
                c_row = (i + 15) // 2 if side == 0 else 8 - COARSE - 1 + i // 2
                at = slice(i * SUB, (i + 1) * SUB)
                floor[side][c, at, :] = low
                va[side][c, at, :] = start_value(low, k, lifted[side, c, c_row : c_row + 1, :])

    count = width // SUB

    def strided(ref):
        return lambda t: [[ref[c, pl.ds(t, SUB, stride=count), :] for c in range(planes)]]

    def keep(dst):
        def store(t, groups):
            for c, value in enumerate(groups[0]):
                dst[c, pl.ds(t, SUB, stride=count), :] = value

        return store

    def twice(i, carry):
        for src, dst in ((va, vb), (vb, va)):
            for side in range(2):
                grouped_sweep(
                    count,
                    strided(src[side]),
                    lambda t, groups: [edge_rolls(groups[0])],
                    strided(floor[side]),
                    keep(dst[side]),
                    None,
                    count,
                )
        return carry

    lax.fori_loop(0, FINE // 2, twice, 0)

    stores = []
    for side, j in enumerate((0, tiles - 1)):
        fill = jnp.zeros((LANES - inner, LANES), jnp.float32)
        for c in range(planes):
            parts = [va[side][c, FINE:, :], fill] if side == 0 else [fill, va[side][c, 0:inner, :]]
            back = jnp.concatenate(parts, axis=0).T
            for a in range(LANES // SUB):
                tall[side, pl.ds(a * SUB * planes + c, SUB, stride=planes), :] = back[a * SUB : (a + 1) * SUB]
        mine = (lane < valid) if side == 0 else (lane >= LANES - valid)
        for i in range(rows // SUB):
            at = i * SUB
            if at < valid:
                other = banded[0, j, at : at + SUB, :]
            elif at >= rows - valid:
                at_band = at - (rows - valid)
                other = banded[1, j, at_band : at_band + SUB, :]
            else:
                other = natural[j, at : at + SUB, :]
            edge[side, at : at + SUB, :] = jnp.where(mine, tall[side, FINE + at : FINE + at + SUB, :], other)
        stores.append(
            pltpu.make_async_copy(edge.at[side], out.at[:, pl.ds(j * LANES, LANES)], edge_sems.at[side])
        )
        stores[-1].start()
    for copy in copies + stores:
        copy.wait()


def strips(stats, from_north, from_south, turned, from_west, from_east, natural, banded):
    tiles, rows, _ = natural.shape
    planes = turned.shape[2]
    vmem = pl.BlockSpec(memory_space=pltpu.VMEM)
    wide = (planes, COARSE * BLK + 3 * FINE, LANES)
    f32 = jnp.float32
    return pl.pallas_call(
        strip_kernel,
        in_specs=[vmem] * 8,
        out_specs=pl.BlockSpec(memory_space=pltpu.HBM),
        out_shape=jax.ShapeDtypeStruct((rows, tiles * LANES), f32),
        scratch_shapes=[
            *[pltpu.VMEM(wide, f32)] * 6,
            pltpu.VMEM((2, planes, 2 * SUB, LANES), f32),
            pltpu.VMEM((2, planes * LANES, LANES), f32),
            pltpu.VMEM((2, rows, LANES), f32),
            pltpu.SemaphoreType.DMA((3, tiles)),
            pltpu.SemaphoreType.DMA((2,)),
        ],
        compiler_params=pltpu.CompilerParams(vmem_limit_bytes=12 * MIB),
        name="strips",
    )(stats, from_north, from_south, turned, from_west, from_east, natural, banded)


def ring(value, axis, shift):
    count = lax.axis_size(axis)
    return lax.ppermute(value, axis, [(i, (i + shift) % count) for i in range(count)])


def shards(elevation, ocean, outlet):
    floor, lock, floor_t, lock_t, stats, stats_t, north, south = prepare(elevation, ocean, outlet)
    from_south = ring(north, "row", -1)
    from_north = ring(south, "row", 1)
    natural = main_part(floor_t, lock_t, stats_t, elevation.shape[0])
    from_north, from_south, natural = lax.optimization_barrier((from_north, from_south, natural))
    halo_args = (stats, from_north, from_south)
    west, east, turned = pack_columns(floor, lock, *halo_args)
    from_east = ring(west, "col", -1)
    from_west = ring(east, "col", 1)
    banded = bands(floor, lock, *halo_args)
    return strips(*halo_args, turned, from_west, from_east, natural, banded)


def solution(mesh):
    return jax.shard_map(
        shards,
        mesh=mesh,
        in_specs=(P("row", "col"), P("row", "col"), P("row", "col")),
        out_specs=P("row", "col"),
        check_vma=False,
    )
```

time: 26.3 us -> 23.8 us (0.905)
  Pallas kernels: 18.5 us -> 15.8 us
    pallas_call x1, Pallas kernels: 6.18 us -> 4.15 us  [main_part(): pl.pallas_call(main_kernel, in_specs=[vmem] * 3, out_specs=vmem, out_shap...]
    pallas_call x1, Pallas kernels: 4.77 us -> 4.38 us  [prepare(): pl.pallas_call(prepare_kernel, in_specs=[hbm] * 3, out_specs=[vmem] * len...]
    pallas_call x1, Pallas kernels: 4.09 us -> 3.77 us  [bands(): pl.pallas_call(bands_kernel, in_specs=[vmem] * 5, out_specs=vmem, out_sha...]
  transfers between devices with their start and end apart: 4 -> 4, of which waited for: 0 -> 1; matrix products, arithmetic and copies ran while one was open for 0% -> 0% of each run, Pallas kernels for 39% -> 33%
where the time goes in v4:
time: 23.8 us; the launch traced here: 23.7 us
  Pallas kernels  15.8 us (66%)
  starting transfers between devices  7.6 us (32%)
    ppermute x4, starting transfers between devices, ring(): lax.ppermute(value, axis, [(i, (i + shift) % count) for i in range(count)])  7.6 us
    pallas_call x1, Pallas kernels, prepare(): pl.pallas_call(prepare_kernel, in_specs=[hbm] * 3, out_specs=[vmem] * len...  4.38 us
    pallas_call x1, Pallas kernels, main_part(): pl.pallas_call(main_kernel, in_specs=[vmem] * 3, out_specs=vmem, out_shap...  4.15 us
    pallas_call x1, Pallas kernels, bands(): pl.pallas_call(bands_kernel, in_specs=[vmem] * 5, out_specs=vmem, out_sha...  3.77 us
    pallas_call x1, Pallas kernels, strips(): pl.pallas_call(strip_kernel, in_specs=[vmem] * 8, out_specs=pl.BlockSpec(...  2.98 us
    pallas_call x1, Pallas kernels, pack_columns(): pl.pallas_call(pack_kernel, in_specs=[vmem] * 5, out_specs=[vmem] * 3, ou...  0.49 us
  transfers between devices with their start and end apart: 4, of which 1 were waited for; matrix products, arithmetic and copies ran while one was open for 0% of the time, Pallas kernels for 33%

profile of v4, /device:TPU:0, one launch (start us, length us, event | category | flops | bytes accessed | tf_op | source)
XLA Modules:
  0.0 23.7 jit_solution(6356880344285912817)
XLA Ops:
  0.0 4.4 %prepare.1 = (f32[8,512,128]{2,1,0:T(8,128)S(1)}, f32[8,512,128]{2,1,0:T(8,128)S(1)}, f32[3,1040,128]{2,1,0:T(8,128)S(1)}, f32[3,1040,128]{2,1,0:T(8,128)S(1)}, ...) custom-call(f32[512,1024]{1,0:T(8,128)} %elev.1, ...), custom_call_target="tpu_custom_call" | custom-call | tf_op jit(solution)/shard_map/prepare/pallas_call | solution.py:157
  4.4 3.0 %collective-permute-start = (f32[10,16,128]{2,1,0:T(8,128)S(1)}, f32[10,16,128]{2,1,0:T(8,128)S(1)}, u32[]{:S(2)}, u32[]{:S(2)}) collective-permute-start(f32[10,16,128]{2,1,0:T(8,128)S(1)} %get-tuple-element.20), channel_id=1, source_target_pairs={{0,8},{8,16},{16,24},{24,0},{1,9},{9,17},{17,25},{25,1},{2,10},{10... | collective-permute-start | bytes 245768 | tf_op jit(solution)/shard_map/ppermute | solution.py:745
  7.4 1.0 %collective-permute-start.1 = (f32[10,16,128]{2,1,0:T(8,128)S(1)}, f32[10,16,128]{2,1,0:T(8,128)S(1)}, u32[]{:S(2)}, u32[]{:S(2)}) collective-permute-start(f32[10,16,128]{2,1,0:T(8,128)S(1)} %get-tuple-element.21), channel_id=1, source_target_pairs={{0,24},{8,0},{16,8},{24,16},{1,25},{9,1},{17,9},{25,17},{2,26},{10... | collective-permute-start | bytes 245768 | tf_op jit(solution)/shard_map/ppermute | solution.py:745
  8.4 4.1 %middle.1.natural = f32[8,512,128]{2,1,0:T(8,128)S(1)} custom-call(f32[3,1040,128]{2,1,0:T(8,128)S(1)} %get-tuple-element.22.floor_t, f32[3,1040,128]{2,1,0:T(8,128)S(1)} %get-tuple-element.23.lock_t, f32[64,128]{1,0:T(8,128)S(1)} %get-tuple-element.24.stats_t), custom_call_target="tpu_custom_call" | custom-call | flops 100000000 | bytes 20000000 | tf_op jit(solution)/shard_map/middle/pallas_call | solution.py:388
  12.6 0.0 collective-permute-done.from_north
  12.6 0.2 collective-permute-done.1.from_south
  12.8 0.5 %pack.1 = (f32[96,128]{1,0:T(8,128)S(1)}, f32[96,128]{1,0:T(8,128)S(1)}, f32[2,2,5,128,128]{4,3,2,1,0:T(8,128)S(1)}) custom-call(f32[8,512,128]{2,1,0:T(8,128)S(1)} %get-tuple-element.27.floor.floor_in, f32[8,512,128]{2,1,0:T(8,128)S(1)} %get-tuple-element.28.lock, f32[96,128]{1,0:T(8,128)S(1)} %get-tuple-element.19.stats, ...), custom_call_target="tpu_custom_call" | custom-call | tf_op jit(solution)/shard_map/pack/pallas_call | solution.py:592
  13.3 0.1 collective-permute-start.2
  13.4 3.5 %collective-permute-start.3 = (f32[96,128]{1,0:T(8,128)S(1)}, f32[96,128]{1,0:T(8,128)S(1)}, u32[]{:S(2)}, u32[]{:S(2)}) collective-permute-start(f32[96,128]{1,0:T(8,128)S(1)} %get-tuple-element.31), channel_id=1, source_target_pairs={{0,7},{1,0},{2,1},{3,2},{4,3},{5,4},{6,5},{7,6},{8,15},{9,8},{10,9... | collective-permute-start | bytes 147464 | tf_op jit(solution)/shard_map/ppermute | solution.py:745
  16.9 3.8 %bands.1.banded = f32[2,8,72,128]{3,2,1,0:T(8,128)S(1)} custom-call(f32[8,512,128]{2,1,0:T(8,128)S(1)} %get-tuple-element.27.floor.floor_in, f32[8,512,128]{2,1,0:T(8,128)S(1)} %get-tuple-element.28.lock, f32[96,128]{1,0:T(8,128)S(1)} %get-tuple-element.19.stats, f32[10,16,128]{2,1,0:T(8,128)S(1)} %collective-permute-done.from_north, ...), custom_call_target="tpu_custom_call" | custom-call | flops 60000000 | bytes 12000000 | tf_op jit(solution)/shard_map/bands/pallas_call | solution.py:525
  20.7 0.0 collective-permute-done.2.from_west
  20.7 0.0 collective-permute-done.3.from_east
  20.7 3.0 %strips.1 = f32[512,1024]{1,0:T(8,128)} custom-call(f32[96,128]{1,0:T(8,128)S(1)} %get-tuple-element.19.stats, f32[10,16,128]{2,1,0:T(8,128)S(1)} %collective-permute-done.from_north, f32[10,16,128]{2,1,0:T(8,128)S(1)} %collective-permute-done.1.from_south, f32[2,2,5,128,128]{4,3,2,1,0:T(8,128)S(1)} %get-tuple-element.29.turned, ...), custom_call_target="tpu_custom_call" | custom-call | tf_op jit(solution)/shard_map/strips/pallas_call | solution.py:725
Async XLA Ops:
  4.4 8.2 %collective-permute-start = (f32[10,16,128]{2,1,0:T(8,128)S(1)}, f32[10,16,128]{2,1,0:T(8,128)S(1)}, u32[]{:S(2)}, u32[]{:S(2)}) collective-permute-start(f32[10,16,128]{2,1,0:T(8,128)S(1)} %get-tuple-element.20), channel_id=1, source_target_pairs={{0,8},{8,16},{16,24},{24,0},{1,9},{9,17},{17,25},{25,1},{2,10},{10... | collective-permute-start | bytes 245768 | tf_op jit(solution)/shard_map/ppermute | solution.py:745
  7.4 5.4 %collective-permute-start.1 = (f32[10,16,128]{2,1,0:T(8,128)S(1)}, f32[10,16,128]{2,1,0:T(8,128)S(1)}, u32[]{:S(2)}, u32[]{:S(2)}) collective-permute-start(f32[10,16,128]{2,1,0:T(8,128)S(1)} %get-tuple-element.21), channel_id=1, source_target_pairs={{0,24},{8,0},{16,8},{24,16},{1,25},{9,1},{17,9},{25,17},{2,26},{10... | collective-permute-start | bytes 245768 | tf_op jit(solution)/shard_map/ppermute | solution.py:745
  13.3 7.4 %collective-permute-start.2 = (f32[96,128]{1,0:T(8,128)S(1)}, f32[96,128]{1,0:T(8,128)S(1)}, u32[]{:S(2)}, u32[]{:S(2)}) collective-permute-start(f32[96,128]{1,0:T(8,128)S(1)} %get-tuple-element.30), channel_id=1, source_target_pairs={{0,1},{1,2},{2,3},{3,4},{4,5},{5,6},{6,7},{7,0},{8,9},{9,10},{10,1... | collective-permute-start | bytes 147464 | tf_op jit(solution)/shard_map/ppermute | solution.py:745
  13.4 7.3 %collective-permute-start.3 = (f32[96,128]{1,0:T(8,128)S(1)}, f32[96,128]{1,0:T(8,128)S(1)}, u32[]{:S(2)}, u32[]{:S(2)}) collective-permute-start(f32[96,128]{1,0:T(8,128)S(1)} %get-tuple-element.31), channel_id=1, source_target_pairs={{0,7},{1,0},{2,1},{3,2},{4,3},{5,4},{6,5},{7,6},{8,15},{9,8},{10,9... | collective-permute-start | bytes 147464 | tf_op jit(solution)/shard_map/ppermute | solution.py:745

commit v5 on v4

--- a/solution.py
+++ b/solution.py
@@ -14,6 +14,7 @@
 SUB = 8
 HALO_C = 8
 UNROLL_T = 112
+PITCH = SUB + 1
 
 huge_level = 1e30
 fine_step = 2.0 ** (-10)
@@ -54,7 +55,7 @@
 
 def prepare_kernel(
     elev, ocean, outlet, floor, lock, floor_t, lock_t, stats, stats_t, north, south,
-    elev_buf, ocean_buf, outlet_buf, turn, sems,
+    elev_buf, ocean_buf, outlet_buf, paired, turn, sems,
 ):
     tiles, rows, _ = floor.shape
     planes = floor_t.shape[0]
@@ -94,6 +95,13 @@
         north[j, FINE:, :] = k[0:FINE]
         south[j, 0:FINE, :] = low[rows - FINE :]
         south[j, FINE:, :] = k[rows - FINE :]
+        for b in range(blocks):
+            at = slice(b * BLK, b * BLK + SUB)
+            also = slice(b * BLK + SUB, (b + 1) * BLK)
+            to = slice(b * PITCH, b * PITCH + SUB)
+            paired[0, to, :] = jnp.minimum(g[at], g[also])
+            paired[1, to, :] = jnp.minimum(k[at], k[also])
+            paired[2, to, :] = -jnp.maximum(g[at], g[also])
         for c in range(planes):
             turned = [
                 jnp.concatenate(
@@ -112,13 +120,11 @@
                 lock_t[c, pl.ds(at, SUB), :] = k
         found = [[], [], []]
         for q in range(blocks // SUB):
-            for r in range(BLK):
-                g, k = (ref[j, pl.ds(q * SUB * BLK + r, SUB, stride=BLK), :] for ref in (elev_buf, lock))
-                low_g = g if r == 0 else jnp.minimum(low_g, g)
-                low_k = k if r == 0 else jnp.minimum(low_k, k)
-                high_g = g if r == 0 else jnp.maximum(high_g, g)
-            for which, value in enumerate((low_g, low_k, -high_g)):
-                found[which].append(value)
+            for which in range(3):
+                for r in range(SUB):
+                    value = paired[which, pl.ds(q * SUB * PITCH + r, SUB, stride=PITCH), :]
+                    low = value if r == 0 else jnp.minimum(low, value)
+                found[which].append(low)
         turned = jnp.concatenate(found[0] + found[1] + found[2] + [unused], axis=0).T
         total = None
         for b in range(LANES // BLK):
@@ -163,6 +169,7 @@
             pltpu.VMEM(natural, f32),
             pltpu.VMEM(natural, jnp.int32),
             pltpu.VMEM(natural, jnp.int32),
+            pltpu.VMEM((3, rows // BLK * PITCH, LANES), f32),
             pltpu.VMEM((LANES, LANES), f32),
             pltpu.SemaphoreType.DMA((3, tiles)),
         ],
@@ -212,7 +219,7 @@
     return roll(tiles[-1], 1, 1), roll(tiles[0], -1, 1)
 
 
-def grouped_sweep(count, load, edges_at, load_floor, store, store_edges, unroll):
+def grouped_sweep(count, load, edges_at, load_floor, store, unroll):
     def plane_min(t, groups):
         out = []
         for (above, below), tiles in zip(edges_at(t, groups), groups):
@@ -240,8 +247,6 @@
             around,
         )
         store(t, new)
-        if store_edges is not None:
-            store_edges(t, new)
 
     first, last = load(0), load(count - 1)
     h_first = plane_min(0, first)
@@ -280,7 +285,7 @@
 
 
 def main_kernel(
-    floor_t, lock_t, stats_t, natural, va, vb, edge_a, edge_b, coarse, spread, turned
+    floor_t, lock_t, stats_t, natural, va, vb, coarse, spread, turned
 ):
     tiles, rows, _ = natural.shape
     planes = floor_t.shape[0]
@@ -308,12 +313,6 @@
 
     load_floor, load_lock = strided(floor_t), strided(lock_t)
 
-    def keep_edges(edges):
-        def store_edges(t, groups):
-            edges[0, t], edges[1, t] = edge_rolls(groups[0])
-
-        return store_edges
-
     def keep(dst):
         def store(t, groups):
             for c, value in enumerate(groups[0]):
@@ -327,35 +326,33 @@
             both = zip(load_floor(t)[0], load_lock(t)[0])
             tiles = [[start_value(f, k, spread[c, b]) for c, (f, k) in enumerate(both)]]
             keep(va)(t, tiles)
-            keep_edges(edge_a)(t, tiles)
         return carry
 
     lax.fori_loop(0, chunk // BLK, start, 0, unroll=True)
 
-    def sweep(src, edges_in, store, store_edges):
+    def sweep(src, store):
         grouped_sweep(
             chunk,
             lambda t: [[src[c, t] for c in range(planes)]],
-            lambda t, _: [(edges_in[0, t], edges_in[1, t])],
+            lambda t, groups: [edge_rolls(groups[0])],
             load_floor,
             store,
-            store_edges,
             UNROLL_T,
         )
 
     def twice(i, carry):
-        sweep(va, edge_a, keep(vb), keep_edges(edge_b))
-        sweep(vb, edge_b, keep(va), keep_edges(edge_a))
+        sweep(va, keep(vb))
+        sweep(vb, keep(va))
         return carry
 
     lax.fori_loop(0, FINE // 2 - 1, twice, 0)
-    sweep(va, edge_a, keep(vb), keep_edges(edge_b))
+    sweep(va, keep(vb))
 
     def store_last(t, groups):
         for c, value in enumerate(groups[0]):
             turned[c, pl.ds(first + t, SUB, stride=pitch), :] = value
 
-    sweep(vb, edge_b, store_last, None)
+    sweep(vb, store_last)
     cols = tiles * LANES
     for c in range(planes):
         for col in list(range(0, margin, SUB)) + list(range(cols - margin, cols, SUB)):
@@ -393,8 +390,6 @@
         scratch_shapes=[
             pltpu.VMEM(tall, f32),
             pltpu.VMEM(tall, f32),
-            pltpu.VMEM((2, chunk, SUB, LANES), f32),
-            pltpu.VMEM((2, chunk, SUB, LANES), f32),
             pltpu.VMEM(stats_t.shape, f32),
             pltpu.VMEM((planes, chunk // BLK, SUB, LANES), f32),
             pltpu.VMEM((planes, length, LANES), f32),
@@ -500,7 +495,6 @@
                     pair_edges,
                     strided(floor[side]),
                     keep(dst[side]),
-                    None,
                     count,
                 )
         return carry
@@ -682,7 +676,6 @@
                     lambda t, groups: [edge_rolls(groups[0])],
                     strided(floor[side]),
                     keep(dst[side]),
-                    None,
                     count,
                 )
         return carry

time: 23.8 us -> 23.1 us (0.971)
  Pallas kernels: 15.8 us -> 14.8 us
  waiting for transfers between devices: 0.22 us -> 0.46 us
    pallas_call x1, Pallas kernels: 4.38 us -> 3.67 us  [prepare(): pl.pallas_call(prepare_kernel, in_specs=[hbm] * 3, out_specs=[vmem] * len...]
    ppermute x4, waiting for transfers between devices: 0.22 us -> 0.46 us  [ring(): lax.ppermute(value, axis, [(i, (i + shift) % count) for i in range(count)])]
where the time goes in v5:
time: 23.1 us; the launch traced here: 23 us
  Pallas kernels  14.8 us (64%)
  starting transfers between devices  7.6 us (33%)
  waiting for transfers between devices  0.46 us (2%)
    ppermute x4, starting transfers between devices, ring(): lax.ppermute(value, axis, [(i, (i + shift) % count) for i in range(count)])  7.6 us
    pallas_call x1, Pallas kernels, main_part(): pl.pallas_call(main_kernel, in_specs=[vmem] * 3, out_specs=vmem, out_shap...  3.92 us
    pallas_call x1, Pallas kernels, bands(): pl.pallas_call(bands_kernel, in_specs=[vmem] * 5, out_specs=vmem, out_sha...  3.77 us
    pallas_call x1, Pallas kernels, prepare(): pl.pallas_call(prepare_kernel, in_specs=[hbm] * 3, out_specs=[vmem] * len...  3.67 us
    pallas_call x1, Pallas kernels, strips(): pl.pallas_call(strip_kernel, in_specs=[vmem] * 8, out_specs=pl.BlockSpec(...  2.98 us
    pallas_call x1, Pallas kernels, pack_columns(): pl.pallas_call(pack_kernel, in_specs=[vmem] * 5, out_specs=[vmem] * 3, ou...  0.49 us
    ppermute x4, waiting for transfers between devices, ring(): lax.ppermute(value, axis, [(i, (i + shift) % count) for i in range(count)])  0.46 us
  transfers between devices with their start and end apart: 4, of which 1 were waited for; matrix products, arithmetic and copies ran while one was open for 0% of the time, Pallas kernels for 33%

profile of v5, /device:TPU:0, one launch (start us, length us, event | category | flops | bytes accessed | tf_op | source)
XLA Modules:
  0.0 23.0 jit_solution(2297477411412419177)
XLA Ops:
  0.0 3.7 %prepare.1 = (f32[8,512,128]{2,1,0:T(8,128)S(1)}, f32[8,512,128]{2,1,0:T(8,128)S(1)}, f32[3,1040,128]{2,1,0:T(8,128)S(1)}, f32[3,1040,128]{2,1,0:T(8,128)S(1)}, ...) custom-call(f32[512,1024]{1,0:T(8,128)} %elev.1, ...), custom_call_target="tpu_custom_call" | custom-call | tf_op jit(solution)/shard_map/prepare/pallas_call | solution.py:163
  3.7 3.0 %collective-permute-start = (f32[10,16,128]{2,1,0:T(8,128)S(1)}, f32[10,16,128]{2,1,0:T(8,128)S(1)}, u32[]{:S(2)}, u32[]{:S(2)}) collective-permute-start(f32[10,16,128]{2,1,0:T(8,128)S(1)} %get-tuple-element.20), channel_id=1, source_target_pairs={{0,8},{8,16},{16,24},{24,0},{1,9},{9,17},{17,25},{25,1},{2,10},{10... | collective-permute-start | bytes 245768 | tf_op jit(solution)/shard_map/ppermute | solution.py:738
  6.7 1.0 %collective-permute-start.1 = (f32[10,16,128]{2,1,0:T(8,128)S(1)}, f32[10,16,128]{2,1,0:T(8,128)S(1)}, u32[]{:S(2)}, u32[]{:S(2)}) collective-permute-start(f32[10,16,128]{2,1,0:T(8,128)S(1)} %get-tuple-element.21), channel_id=1, source_target_pairs={{0,24},{8,0},{16,8},{24,16},{1,25},{9,1},{17,9},{25,17},{2,26},{10... | collective-permute-start | bytes 245768 | tf_op jit(solution)/shard_map/ppermute | solution.py:738
  7.7 3.9 %middle.1.natural = f32[8,512,128]{2,1,0:T(8,128)S(1)} custom-call(f32[3,1040,128]{2,1,0:T(8,128)S(1)} %get-tuple-element.22.floor_t, f32[3,1040,128]{2,1,0:T(8,128)S(1)} %get-tuple-element.23.lock_t, f32[64,128]{1,0:T(8,128)S(1)} %get-tuple-element.24.stats_t), custom_call_target="tpu_custom_call" | custom-call | flops 100000000 | bytes 20000000 | tf_op jit(solution)/shard_map/middle/pallas_call | solution.py:385
  11.6 0.0 collective-permute-done.from_north
  11.6 0.5 %collective-permute-done.1.from_south = f32[10,16,128]{2,1,0:T(8,128)S(1)} collective-permute-done((f32[10,16,128]{2,1,0:T(8,128)S(1)}, f32[10,16,128]{2,1,0:T(8,128)S(1)}, u32[]{:S(2)}, u32[]{:S(2)}) %collective-permute-start.1) | collective-permute-done | bytes 81952 | tf_op jit(solution)/shard_map/ppermute | solution.py:738
  12.1 0.5 %pack.1 = (f32[96,128]{1,0:T(8,128)S(1)}, f32[96,128]{1,0:T(8,128)S(1)}, f32[2,2,5,128,128]{4,3,2,1,0:T(8,128)S(1)}) custom-call(f32[8,512,128]{2,1,0:T(8,128)S(1)} %get-tuple-element.27.floor.floor_in, f32[8,512,128]{2,1,0:T(8,128)S(1)} %get-tuple-element.28.lock, f32[96,128]{1,0:T(8,128)S(1)} %get-tuple-element.19.stats, ...), custom_call_target="tpu_custom_call" | custom-call | tf_op jit(solution)/shard_map/pack/pallas_call | solution.py:586
  12.6 0.1 collective-permute-start.2
  12.6 3.5 %collective-permute-start.3 = (f32[96,128]{1,0:T(8,128)S(1)}, f32[96,128]{1,0:T(8,128)S(1)}, u32[]{:S(2)}, u32[]{:S(2)}) collective-permute-start(f32[96,128]{1,0:T(8,128)S(1)} %get-tuple-element.31), channel_id=1, source_target_pairs={{0,7},{1,0},{2,1},{3,2},{4,3},{5,4},{6,5},{7,6},{8,15},{9,8},{10,9... | collective-permute-start | bytes 147464 | tf_op jit(solution)/shard_map/ppermute | solution.py:738
  16.2 3.8 %bands.1.banded = f32[2,8,72,128]{3,2,1,0:T(8,128)S(1)} custom-call(f32[8,512,128]{2,1,0:T(8,128)S(1)} %get-tuple-element.27.floor.floor_in, f32[8,512,128]{2,1,0:T(8,128)S(1)} %get-tuple-element.28.lock, f32[96,128]{1,0:T(8,128)S(1)} %get-tuple-element.19.stats, f32[10,16,128]{2,1,0:T(8,128)S(1)} %collective-permute-done.from_north, ...), custom_call_target="tpu_custom_call" | custom-call | flops 60000000 | bytes 12000000 | tf_op jit(solution)/shard_map/bands/pallas_call | solution.py:519
  20.0 0.0 collective-permute-done.2.from_west
  20.0 0.0 collective-permute-done.3.from_east
  20.0 3.0 %strips.1 = f32[512,1024]{1,0:T(8,128)} custom-call(f32[96,128]{1,0:T(8,128)S(1)} %get-tuple-element.19.stats, f32[10,16,128]{2,1,0:T(8,128)S(1)} %collective-permute-done.from_north, f32[10,16,128]{2,1,0:T(8,128)S(1)} %collective-permute-done.1.from_south, f32[2,2,5,128,128]{4,3,2,1,0:T(8,128)S(1)} %get-tuple-element.29.turned, ...), custom_call_target="tpu_custom_call" | custom-call | tf_op jit(solution)/shard_map/strips/pallas_call | solution.py:718
Async XLA Ops:
  3.7 7.9 %collective-permute-start = (f32[10,16,128]{2,1,0:T(8,128)S(1)}, f32[10,16,128]{2,1,0:T(8,128)S(1)}, u32[]{:S(2)}, u32[]{:S(2)}) collective-permute-start(f32[10,16,128]{2,1,0:T(8,128)S(1)} %get-tuple-element.20), channel_id=1, source_target_pairs={{0,8},{8,16},{16,24},{24,0},{1,9},{9,17},{17,25},{25,1},{2,10},{10... | collective-permute-start | bytes 245768 | tf_op jit(solution)/shard_map/ppermute | solution.py:738
  6.7 5.4 %collective-permute-start.1 = (f32[10,16,128]{2,1,0:T(8,128)S(1)}, f32[10,16,128]{2,1,0:T(8,128)S(1)}, u32[]{:S(2)}, u32[]{:S(2)}) collective-permute-start(f32[10,16,128]{2,1,0:T(8,128)S(1)} %get-tuple-element.21), channel_id=1, source_target_pairs={{0,24},{8,0},{16,8},{24,16},{1,25},{9,1},{17,9},{25,17},{2,26},{10... | collective-permute-start | bytes 245768 | tf_op jit(solution)/shard_map/ppermute | solution.py:738
  12.6 7.4 %collective-permute-start.2 = (f32[96,128]{1,0:T(8,128)S(1)}, f32[96,128]{1,0:T(8,128)S(1)}, u32[]{:S(2)}, u32[]{:S(2)}) collective-permute-start(f32[96,128]{1,0:T(8,128)S(1)} %get-tuple-element.30), channel_id=1, source_target_pairs={{0,1},{1,2},{2,3},{3,4},{4,5},{5,6},{6,7},{7,0},{8,9},{9,10},{10,1... | collective-permute-start | bytes 147464 | tf_op jit(solution)/shard_map/ppermute | solution.py:738
  12.6 7.3 %collective-permute-start.3 = (f32[96,128]{1,0:T(8,128)S(1)}, f32[96,128]{1,0:T(8,128)S(1)}, u32[]{:S(2)}, u32[]{:S(2)}) collective-permute-start(f32[96,128]{1,0:T(8,128)S(1)} %get-tuple-element.31), channel_id=1, source_target_pairs={{0,7},{1,0},{2,1},{3,2},{4,3},{5,4},{6,5},{7,6},{8,15},{9,8},{10,9... | collective-permute-start | bytes 147464 | tf_op jit(solution)/shard_map/ppermute | solution.py:738

commit v6 on v5

--- a/solution.py
+++ b/solution.py
@@ -219,45 +219,48 @@
     return roll(tiles[-1], 1, 1), roll(tiles[0], -1, 1)
 
 
+def plane_min(edges, groups):
+    out = []
+    for (above, below), tiles in zip(edges, groups):
+        line = [above] + tiles + [below]
+        mins = []
+        for c in range(0, len(tiles), 2):
+            pair = jnp.minimum(line[c + 1], line[c + 2])
+            mins.append(jnp.minimum(line[c], pair))
+            if c + 1 < len(tiles):
+                mins.append(jnp.minimum(pair, line[c + 3]))
+        out.append(mins)
+    return out
+
+
+def each(function, *args):
+    return [[function(*values) for values in zip(*groups)] for groups in zip(*args)]
+
+
+def least(*args):
+    return each(lambda *values: functools.reduce(jnp.minimum, values), *args)
+
+
+def lowered(floor, value, around):
+    return each(
+        lambda f, v, m: jnp.maximum(f, jnp.minimum(v, m + fine_step)), floor, value, around
+    )
+
+
 def grouped_sweep(count, load, edges_at, load_floor, store, unroll):
-    def plane_min(t, groups):
-        out = []
-        for (above, below), tiles in zip(edges_at(t, groups), groups):
-            line = [above] + tiles + [below]
-            mins = []
-            for c in range(0, len(tiles), 2):
-                pair = jnp.minimum(line[c + 1], line[c + 2])
-                mins.append(jnp.minimum(line[c], pair))
-                if c + 1 < len(tiles):
-                    mins.append(jnp.minimum(pair, line[c + 3]))
-            out.append(mins)
-        return out
-
-    def each(function, *args):
-        return [[function(*values) for values in zip(*groups)] for groups in zip(*args)]
-
-    def least(*args):
-        return each(lambda *values: functools.reduce(jnp.minimum, values), *args)
-
     def finish(t, around, value):
-        new = each(
-            lambda f, v, m: jnp.maximum(f, jnp.minimum(v, m + fine_step)),
-            load_floor(t),
-            value,
-            around,
-        )
-        store(t, new)
+        store(t, lowered(load_floor(t), value, around))
 
     first, last = load(0), load(count - 1)
-    h_first = plane_min(0, first)
-    h_before = each(lambda h: roll(h, 1, 0), plane_min(count - 1, last))
+    h_first = plane_min(edges_at(0, first), first)
+    h_before = each(lambda h: roll(h, 1, 0), plane_min(edges_at(count - 1, last), last))
     h_after = each(lambda h: roll(h, -1, 0), h_first)
 
     def line_at(t):
         if isinstance(t, int) and t == count:
             return None, h_after
         value = load(t)
-        return value, plane_min(t, value)
+        return value, plane_min(edges_at(t, value), value)
 
     def span(start, size, carry):
         h_west, h_here, here = carry
@@ -279,6 +282,42 @@
 
     loops = (count - 1) // unroll
     carry = (h_before, h_first, first)
+    if loops:
+        carry = lax.fori_loop(0, loops, lambda q, c: span(q * unroll, unroll, c), carry)
+    span(loops * unroll, count - loops * unroll, carry)
+
+
+def lines_first_sweep(count, load, edges_at, load_floor, store, unroll):
+    def finish(t, lines, value):
+        store(t, lowered(load_floor(t), value, plane_min(edges_at(t, lines), lines)))
+
+    first = load(0)
+    before = each(lambda v: roll(v, 1, 0), load(count - 1))
+    after = each(lambda v: roll(v, -1, 0), first)
+
+    def line_at(t):
+        return after if isinstance(t, int) and t == count else load(t)
+
+    def span(start, size, carry):
+        west, here = carry
+        u = 0
+        while u < size:
+            t = start + u
+            east = line_at(t + 1)
+            pair = least(here, east)
+            finish(t, least(west, pair), here)
+            if u + 1 < size:
+                far = line_at(t + 2)
+                finish(t + 1, least(pair, far), east)
+                west, here = east, far
+                u += 2
+            else:
+                west, here = here, east
+                u += 1
+        return west, here
+
+    loops = (count - 1) // unroll
+    carry = (before, first)
     if loops:
         carry = lax.fori_loop(0, loops, lambda q, c: span(q * unroll, unroll, c), carry)
     span(loops * unroll, count - loops * unroll, carry)
@@ -489,7 +528,7 @@
     def twice(i, carry):
         for src, dst in ((va, vb), (vb, va)):
             for side in range(2):
-                grouped_sweep(
+                lines_first_sweep(
                     count,
                     strided(src[side]),
                     pair_edges,

time: 23.1 us -> 22.9 us (level)
  no operation moved by 1% of the time
where the time goes in v6:
time: 22.9 us; the launch traced here: 22.7 us
  Pallas kernels  14.6 us (64%)
  starting transfers between devices  7.6 us (33%)
  waiting for transfers between devices  0.46 us (2%)
    ppermute x4, starting transfers between devices, ring(): lax.ppermute(value, axis, [(i, (i + shift) % count) for i in range(count)])  7.6 us
    pallas_call x1, Pallas kernels, main_part(): pl.pallas_call(main_kernel, in_specs=[vmem] * 3, out_specs=vmem, out_shap...  3.92 us
    pallas_call x1, Pallas kernels, prepare(): pl.pallas_call(prepare_kernel, in_specs=[hbm] * 3, out_specs=[vmem] * len...  3.67 us
    pallas_call x1, Pallas kernels, bands(): pl.pallas_call(bands_kernel, in_specs=[vmem] * 5, out_specs=vmem, out_sha...  3.55 us
    pallas_call x1, Pallas kernels, strips(): pl.pallas_call(strip_kernel, in_specs=[vmem] * 8, out_specs=pl.BlockSpec(...  2.98 us
    pallas_call x1, Pallas kernels, pack_columns(): pl.pallas_call(pack_kernel, in_specs=[vmem] * 5, out_specs=[vmem] * 3, ou...  0.49 us
    ppermute x4, waiting for transfers between devices, ring(): lax.ppermute(value, axis, [(i, (i + shift) % count) for i in range(count)])  0.46 us
  transfers between devices with their start and end apart: 4, of which 1 were waited for; matrix products, arithmetic and copies ran while one was open for 0% of the time, Pallas kernels for 33%

profile of v6, /device:TPU:0, one launch (start us, length us, event | category | flops | bytes accessed | tf_op | source)
XLA Modules:
  0.0 22.7 jit_solution(14141450900380027504)
XLA Ops:
  0.0 3.7 %prepare.1 = (f32[8,512,128]{2,1,0:T(8,128)S(1)}, f32[8,512,128]{2,1,0:T(8,128)S(1)}, f32[3,1040,128]{2,1,0:T(8,128)S(1)}, f32[3,1040,128]{2,1,0:T(8,128)S(1)}, ...) custom-call(f32[512,1024]{1,0:T(8,128)} %elev.1, ...), custom_call_target="tpu_custom_call" | custom-call | tf_op jit(solution)/shard_map/prepare/pallas_call | solution.py:163
  3.7 3.0 %collective-permute-start = (f32[10,16,128]{2,1,0:T(8,128)S(1)}, f32[10,16,128]{2,1,0:T(8,128)S(1)}, u32[]{:S(2)}, u32[]{:S(2)}) collective-permute-start(f32[10,16,128]{2,1,0:T(8,128)S(1)} %get-tuple-element.20), channel_id=1, source_target_pairs={{0,8},{8,16},{16,24},{24,0},{1,9},{9,17},{17,25},{25,1},{2,10},{10... | collective-permute-start | bytes 245768 | tf_op jit(solution)/shard_map/ppermute | solution.py:777
  6.7 1.0 %collective-permute-start.1 = (f32[10,16,128]{2,1,0:T(8,128)S(1)}, f32[10,16,128]{2,1,0:T(8,128)S(1)}, u32[]{:S(2)}, u32[]{:S(2)}) collective-permute-start(f32[10,16,128]{2,1,0:T(8,128)S(1)} %get-tuple-element.21), channel_id=1, source_target_pairs={{0,24},{8,0},{16,8},{24,16},{1,25},{9,1},{17,9},{25,17},{2,26},{10... | collective-permute-start | bytes 245768 | tf_op jit(solution)/shard_map/ppermute | solution.py:777
  7.7 3.9 %middle.1.natural = f32[8,512,128]{2,1,0:T(8,128)S(1)} custom-call(f32[3,1040,128]{2,1,0:T(8,128)S(1)} %get-tuple-element.22.floor_t, f32[3,1040,128]{2,1,0:T(8,128)S(1)} %get-tuple-element.23.lock_t, f32[64,128]{1,0:T(8,128)S(1)} %get-tuple-element.24.stats_t), custom_call_target="tpu_custom_call" | custom-call | flops 100000000 | bytes 20000000 | tf_op jit(solution)/shard_map/middle/pallas_call | solution.py:424
  11.6 0.0 collective-permute-done.from_north
  11.6 0.5 %collective-permute-done.1.from_south = f32[10,16,128]{2,1,0:T(8,128)S(1)} collective-permute-done((f32[10,16,128]{2,1,0:T(8,128)S(1)}, f32[10,16,128]{2,1,0:T(8,128)S(1)}, u32[]{:S(2)}, u32[]{:S(2)}) %collective-permute-start.1) | collective-permute-done | bytes 81952 | tf_op jit(solution)/shard_map/ppermute | solution.py:777
  12.1 0.5 %pack.1 = (f32[96,128]{1,0:T(8,128)S(1)}, f32[96,128]{1,0:T(8,128)S(1)}, f32[2,2,5,128,128]{4,3,2,1,0:T(8,128)S(1)}) custom-call(f32[8,512,128]{2,1,0:T(8,128)S(1)} %get-tuple-element.27.floor.floor_in, f32[8,512,128]{2,1,0:T(8,128)S(1)} %get-tuple-element.28.lock, f32[96,128]{1,0:T(8,128)S(1)} %get-tuple-element.19.stats, ...), custom_call_target="tpu_custom_call" | custom-call | tf_op jit(solution)/shard_map/pack/pallas_call | solution.py:625
  12.6 0.1 collective-permute-start.2
  12.6 3.5 %collective-permute-start.3 = (f32[96,128]{1,0:T(8,128)S(1)}, f32[96,128]{1,0:T(8,128)S(1)}, u32[]{:S(2)}, u32[]{:S(2)}) collective-permute-start(f32[96,128]{1,0:T(8,128)S(1)} %get-tuple-element.31), channel_id=1, source_target_pairs={{0,7},{1,0},{2,1},{3,2},{4,3},{5,4},{6,5},{7,6},{8,15},{9,8},{10,9... | collective-permute-start | bytes 147464 | tf_op jit(solution)/shard_map/ppermute | solution.py:777
  16.2 3.5 %bands.1.banded = f32[2,8,72,128]{3,2,1,0:T(8,128)S(1)} custom-call(f32[8,512,128]{2,1,0:T(8,128)S(1)} %get-tuple-element.27.floor.floor_in, f32[8,512,128]{2,1,0:T(8,128)S(1)} %get-tuple-element.28.lock, f32[96,128]{1,0:T(8,128)S(1)} %get-tuple-element.19.stats, f32[10,16,128]{2,1,0:T(8,128)S(1)} %collective-permute-done.from_north, ...), custom_call_target="tpu_custom_call" | custom-call | flops 60000000 | bytes 12000000 | tf_op jit(solution)/shard_map/bands/pallas_call | solution.py:558
  19.7 0.0 collective-permute-done.2.from_west
  19.7 0.0 collective-permute-done.3.from_east
  19.7 3.0 %strips.1 = f32[512,1024]{1,0:T(8,128)} custom-call(f32[96,128]{1,0:T(8,128)S(1)} %get-tuple-element.19.stats, f32[10,16,128]{2,1,0:T(8,128)S(1)} %collective-permute-done.from_north, f32[10,16,128]{2,1,0:T(8,128)S(1)} %collective-permute-done.1.from_south, f32[2,2,5,128,128]{4,3,2,1,0:T(8,128)S(1)} %get-tuple-element.29.turned, ...), custom_call_target="tpu_custom_call" | custom-call | tf_op jit(solution)/shard_map/strips/pallas_call | solution.py:757
Async XLA Ops:
  3.7 7.9 %collective-permute-start = (f32[10,16,128]{2,1,0:T(8,128)S(1)}, f32[10,16,128]{2,1,0:T(8,128)S(1)}, u32[]{:S(2)}, u32[]{:S(2)}) collective-permute-start(f32[10,16,128]{2,1,0:T(8,128)S(1)} %get-tuple-element.20), channel_id=1, source_target_pairs={{0,8},{8,16},{16,24},{24,0},{1,9},{9,17},{17,25},{25,1},{2,10},{10... | collective-permute-start | bytes 245768 | tf_op jit(solution)/shard_map/ppermute | solution.py:777
  6.7 5.4 %collective-permute-start.1 = (f32[10,16,128]{2,1,0:T(8,128)S(1)}, f32[10,16,128]{2,1,0:T(8,128)S(1)}, u32[]{:S(2)}, u32[]{:S(2)}) collective-permute-start(f32[10,16,128]{2,1,0:T(8,128)S(1)} %get-tuple-element.21), channel_id=1, source_target_pairs={{0,24},{8,0},{16,8},{24,16},{1,25},{9,1},{17,9},{25,17},{2,26},{10... | collective-permute-start | bytes 245768 | tf_op jit(solution)/shard_map/ppermute | solution.py:777
  12.6 7.2 %collective-permute-start.2 = (f32[96,128]{1,0:T(8,128)S(1)}, f32[96,128]{1,0:T(8,128)S(1)}, u32[]{:S(2)}, u32[]{:S(2)}) collective-permute-start(f32[96,128]{1,0:T(8,128)S(1)} %get-tuple-element.30), channel_id=1, source_target_pairs={{0,1},{1,2},{2,3},{3,4},{4,5},{5,6},{6,7},{7,0},{8,9},{9,10},{10,1... | collective-permute-start | bytes 147464 | tf_op jit(solution)/shard_map/ppermute | solution.py:777
  12.6 7.1 %collective-permute-start.3 = (f32[96,128]{1,0:T(8,128)S(1)}, f32[96,128]{1,0:T(8,128)S(1)}, u32[]{:S(2)}, u32[]{:S(2)}) collective-permute-start(f32[96,128]{1,0:T(8,128)S(1)} %get-tuple-element.31), channel_id=1, source_target_pairs={{0,7},{1,0},{2,1},{3,2},{4,3},{5,4},{6,5},{7,6},{8,15},{9,8},{10,9... | collective-permute-start | bytes 147464 | tf_op jit(solution)/shard_map/ppermute | solution.py:777

commit v7 on v6

--- a/solution.py
+++ b/solution.py
@@ -586,20 +586,31 @@
     coarse = fields[0].shape[0] // SUB
     coarse_cols = tiles * LANES // BLK
     rest = tall.shape[2] - rows - 2 * FINE
+    span = SUB * planes
+    inside = [a * span >= FINE and (a + 1) * span - FINE <= rows for a in range(LANES // SUB)]
+    head = inside.index(True) * span - FINE
+    foot = (LANES // SUB - inside[::-1].index(True)) * span - FINE
     for side, (dst, j, col_at, lane_at) in enumerate(
         ((west, 0, 0, 0), (east, tiles - 1, LANES - FINE, coarse_cols - 8))
     ):
         for which, ref in enumerate((floor, lock)):
             at = slice(which * FINE, (which + 1) * FINE)
             tall[side, which, 0:FINE, :] = sealed(from_north[j, at, :], at_north)
-            tall[side, which, FINE : FINE + rows, :] = ref[j]
+            for at_local in range(0, rows, SUB):
+                if at_local < head or at_local + SUB > foot:
+                    to = FINE + at_local
+                    tall[side, which, to : to + SUB, :] = ref[j, at_local : at_local + SUB, :]
             tall[side, which, FINE + rows : 2 * FINE + rows, :] = sealed(from_south[j, at, :], at_south)
             tall[side, which, 2 * FINE + rows :, :] = jnp.full((rest, LANES), huge_level, jnp.float32)
             for c in range(planes):
-                parts = [
-                    tall[side, which, pl.ds(a * SUB * planes + c, SUB, stride=planes), :]
-                    for a in range(LANES // SUB)
-                ]
+                parts = []
+                for a in range(LANES // SUB):
+                    at = a * span + c
+                    if inside[a]:
+                        part = ref[j, pl.ds(at - FINE, SUB, stride=planes), :]
+                    else:
+                        part = tall[side, which, pl.ds(at, SUB, stride=planes), :]
+                    parts.append(part)
                 value = jnp.concatenate(parts, axis=0).T
                 turned[side, which, c] = value
                 slot = which * planes + c
@@ -779,14 +790,14 @@
 
 def shards(elevation, ocean, outlet):
     floor, lock, floor_t, lock_t, stats, stats_t, north, south = prepare(elevation, ocean, outlet)
+    from_north = ring(south, "row", 1)
     from_south = ring(north, "row", -1)
-    from_north = ring(south, "row", 1)
     natural = main_part(floor_t, lock_t, stats_t, elevation.shape[0])
     from_north, from_south, natural = lax.optimization_barrier((from_north, from_south, natural))
     halo_args = (stats, from_north, from_south)
     west, east, turned = pack_columns(floor, lock, *halo_args)
+    from_west = ring(east, "col", 1)
     from_east = ring(west, "col", -1)
-    from_west = ring(east, "col", 1)
     banded = bands(floor, lock, *halo_args)
     return strips(*halo_args, turned, from_west, from_east, natural, banded)
 

time: 22.9 us -> 22.8 us (level)
  no operation moved by 1% of the time
where the time goes in v7:
time: 22.8 us; the launch traced here: 22.7 us
  Pallas kernels  14.6 us (64%)
  starting transfers between devices  7.6 us (33%)
  waiting for transfers between devices  0.46 us (2%)
    ppermute x4, starting transfers between devices, ring(): lax.ppermute(value, axis, [(i, (i + shift) % count) for i in range(count)])  7.6 us
    pallas_call x1, Pallas kernels, main_part(): pl.pallas_call(main_kernel, in_specs=[vmem] * 3, out_specs=vmem, out_shap...  3.92 us
    pallas_call x1, Pallas kernels, prepare(): pl.pallas_call(prepare_kernel, in_specs=[hbm] * 3, out_specs=[vmem] * len...  3.67 us
    pallas_call x1, Pallas kernels, bands(): pl.pallas_call(bands_kernel, in_specs=[vmem] * 5, out_specs=vmem, out_sha...  3.55 us
    pallas_call x1, Pallas kernels, strips(): pl.pallas_call(strip_kernel, in_specs=[vmem] * 8, out_specs=pl.BlockSpec(...  2.98 us
    pallas_call x1, Pallas kernels, pack_columns(): pl.pallas_call(pack_kernel, in_specs=[vmem] * 5, out_specs=[vmem] * 3, ou...  0.47 us
    ppermute x4, waiting for transfers between devices, ring(): lax.ppermute(value, axis, [(i, (i + shift) % count) for i in range(count)])  0.46 us
  transfers between devices with their start and end apart: 4, of which 1 were waited for; matrix products, arithmetic and copies ran while one was open for 0% of the time, Pallas kernels for 33%

profile of v7, /device:TPU:0, one launch (start us, length us, event | category | flops | bytes accessed | tf_op | source)
XLA Modules:
  0.0 22.7 jit_solution(5183303628489665321)
XLA Ops:
  0.0 3.7 %prepare.1 = (f32[8,512,128]{2,1,0:T(8,128)S(1)}, f32[8,512,128]{2,1,0:T(8,128)S(1)}, f32[3,1040,128]{2,1,0:T(8,128)S(1)}, f32[3,1040,128]{2,1,0:T(8,128)S(1)}, ...) custom-call(f32[512,1024]{1,0:T(8,128)} %elev.1, ...), custom_call_target="tpu_custom_call" | custom-call | tf_op jit(solution)/shard_map/prepare/pallas_call | solution.py:163
  3.7 3.0 %collective-permute-start = (f32[10,16,128]{2,1,0:T(8,128)S(1)}, f32[10,16,128]{2,1,0:T(8,128)S(1)}, u32[]{:S(2)}, u32[]{:S(2)}) collective-permute-start(f32[10,16,128]{2,1,0:T(8,128)S(1)} %get-tuple-element.20), channel_id=1, source_target_pairs={{0,8},{8,16},{16,24},{24,0},{1,9},{9,17},{17,25},{25,1},{2,10},{10... | collective-permute-start | bytes 245768 | tf_op jit(solution)/shard_map/ppermute | solution.py:788
  6.7 1.0 %collective-permute-start.1 = (f32[10,16,128]{2,1,0:T(8,128)S(1)}, f32[10,16,128]{2,1,0:T(8,128)S(1)}, u32[]{:S(2)}, u32[]{:S(2)}) collective-permute-start(f32[10,16,128]{2,1,0:T(8,128)S(1)} %get-tuple-element.21), channel_id=1, source_target_pairs={{0,24},{8,0},{16,8},{24,16},{1,25},{9,1},{17,9},{25,17},{2,26},{10... | collective-permute-start | bytes 245768 | tf_op jit(solution)/shard_map/ppermute | solution.py:788
  7.7 3.9 %middle.1.natural = f32[8,512,128]{2,1,0:T(8,128)S(1)} custom-call(f32[3,1040,128]{2,1,0:T(8,128)S(1)} %get-tuple-element.22.floor_t, f32[3,1040,128]{2,1,0:T(8,128)S(1)} %get-tuple-element.23.lock_t, f32[64,128]{1,0:T(8,128)S(1)} %get-tuple-element.24.stats_t), custom_call_target="tpu_custom_call" | custom-call | flops 100000000 | bytes 20000000 | tf_op jit(solution)/shard_map/middle/pallas_call | solution.py:424
  11.6 0.0 collective-permute-done.from_north
  11.6 0.5 %collective-permute-done.1.from_south = f32[10,16,128]{2,1,0:T(8,128)S(1)} collective-permute-done((f32[10,16,128]{2,1,0:T(8,128)S(1)}, f32[10,16,128]{2,1,0:T(8,128)S(1)}, u32[]{:S(2)}, u32[]{:S(2)}) %collective-permute-start.1) | collective-permute-done | bytes 81952 | tf_op jit(solution)/shard_map/ppermute | solution.py:788
  12.1 0.5 %pack.1 = (f32[96,128]{1,0:T(8,128)S(1)}, f32[96,128]{1,0:T(8,128)S(1)}, f32[2,2,5,128,128]{4,3,2,1,0:T(8,128)S(1)}) custom-call(f32[8,512,128]{2,1,0:T(8,128)S(1)} %get-tuple-element.27.floor.floor_in, f32[8,512,128]{2,1,0:T(8,128)S(1)} %get-tuple-element.28.lock, f32[96,128]{1,0:T(8,128)S(1)} %get-tuple-element.19.stats, ...), custom_call_target="tpu_custom_call" | custom-call | tf_op jit(solution)/shard_map/pack/pallas_call | solution.py:636
  12.6 0.1 collective-permute-start.2
  12.6 3.5 %collective-permute-start.3 = (f32[96,128]{1,0:T(8,128)S(1)}, f32[96,128]{1,0:T(8,128)S(1)}, u32[]{:S(2)}, u32[]{:S(2)}) collective-permute-start(f32[96,128]{1,0:T(8,128)S(1)} %get-tuple-element.31), channel_id=1, source_target_pairs={{0,7},{1,0},{2,1},{3,2},{4,3},{5,4},{6,5},{7,6},{8,15},{9,8},{10,9... | collective-permute-start | bytes 147464 | tf_op jit(solution)/shard_map/ppermute | solution.py:788
  16.2 3.5 %bands.1.banded = f32[2,8,72,128]{3,2,1,0:T(8,128)S(1)} custom-call(f32[8,512,128]{2,1,0:T(8,128)S(1)} %get-tuple-element.27.floor.floor_in, f32[8,512,128]{2,1,0:T(8,128)S(1)} %get-tuple-element.28.lock, f32[96,128]{1,0:T(8,128)S(1)} %get-tuple-element.19.stats, f32[10,16,128]{2,1,0:T(8,128)S(1)} %collective-permute-done.from_north, ...), custom_call_target="tpu_custom_call" | custom-call | flops 60000000 | bytes 12000000 | tf_op jit(solution)/shard_map/bands/pallas_call | solution.py:558
  19.7 0.0 collective-permute-done.2.from_west
  19.7 0.0 collective-permute-done.3.from_east
  19.7 3.0 %strips.1 = f32[512,1024]{1,0:T(8,128)} custom-call(f32[96,128]{1,0:T(8,128)S(1)} %get-tuple-element.19.stats, f32[10,16,128]{2,1,0:T(8,128)S(1)} %collective-permute-done.from_north, f32[10,16,128]{2,1,0:T(8,128)S(1)} %collective-permute-done.1.from_south, f32[2,2,5,128,128]{4,3,2,1,0:T(8,128)S(1)} %get-tuple-element.29.turned, ...), custom_call_target="tpu_custom_call" | custom-call | tf_op jit(solution)/shard_map/strips/pallas_call | solution.py:768
Async XLA Ops:
  3.7 7.9 %collective-permute-start = (f32[10,16,128]{2,1,0:T(8,128)S(1)}, f32[10,16,128]{2,1,0:T(8,128)S(1)}, u32[]{:S(2)}, u32[]{:S(2)}) collective-permute-start(f32[10,16,128]{2,1,0:T(8,128)S(1)} %get-tuple-element.20), channel_id=1, source_target_pairs={{0,8},{8,16},{16,24},{24,0},{1,9},{9,17},{17,25},{25,1},{2,10},{10... | collective-permute-start | bytes 245768 | tf_op jit(solution)/shard_map/ppermute | solution.py:788
  6.7 5.4 %collective-permute-start.1 = (f32[10,16,128]{2,1,0:T(8,128)S(1)}, f32[10,16,128]{2,1,0:T(8,128)S(1)}, u32[]{:S(2)}, u32[]{:S(2)}) collective-permute-start(f32[10,16,128]{2,1,0:T(8,128)S(1)} %get-tuple-element.21), channel_id=1, source_target_pairs={{0,24},{8,0},{16,8},{24,16},{1,25},{9,1},{17,9},{25,17},{2,26},{10... | collective-permute-start | bytes 245768 | tf_op jit(solution)/shard_map/ppermute | solution.py:788
  12.6 7.2 %collective-permute-start.2 = (f32[96,128]{1,0:T(8,128)S(1)}, f32[96,128]{1,0:T(8,128)S(1)}, u32[]{:S(2)}, u32[]{:S(2)}) collective-permute-start(f32[96,128]{1,0:T(8,128)S(1)} %get-tuple-element.30), channel_id=1, source_target_pairs={{0,1},{1,2},{2,3},{3,4},{4,5},{5,6},{6,7},{7,0},{8,9},{9,10},{10,1... | collective-permute-start | bytes 147464 | tf_op jit(solution)/shard_map/ppermute | solution.py:788
  12.6 7.1 %collective-permute-start.3 = (f32[96,128]{1,0:T(8,128)S(1)}, f32[96,128]{1,0:T(8,128)S(1)}, u32[]{:S(2)}, u32[]{:S(2)}) collective-permute-start(f32[96,128]{1,0:T(8,128)S(1)} %get-tuple-element.31), channel_id=1, source_target_pairs={{0,7},{1,0},{2,1},{3,2},{4,3},{5,4},{6,5},{7,6},{8,15},{9,8},{10,9... | collective-permute-start | bytes 147464 | tf_op jit(solution)/shard_map/ppermute | solution.py:788

commit v8 on v7

--- a/solution.py
+++ b/solution.py
@@ -466,7 +466,8 @@
     coarse = coarse_sweeps(*coarse_fields(stats, from_north, from_south))
     wide = lane_iota(coarse.shape)
     for j in range(tiles):
-        lifted[j] = gather_lanes(coarse, wide // BLK + 8 * j)
+        for part in (slice(0, 2 * SUB), slice(coarse.shape[0] - 2 * SUB, coarse.shape[0])):
+            lifted[j, part, :] = gather_lanes(coarse[part], wide[part] // BLK + 8 * j)
     for side, (band, is_edge, at_band, at_inner, first) in enumerate(
         ((from_north, at_north, 0, FINE, 0), (from_south, at_south, inner, 0, rows - inner))
     ):
@@ -612,7 +613,8 @@
                         part = tall[side, which, pl.ds(at, SUB, stride=planes), :]
                     parts.append(part)
                 value = jnp.concatenate(parts, axis=0).T
-                turned[side, which, c] = value
+                used = slice(0, COARSE * BLK + 2 * FINE) if side == 0 else slice(LANES - COARSE * BLK - 2 * FINE, LANES)
+                turned[side, which, c, used, :] = value[used]
                 slot = which * planes + c
                 dst[slot * SUB : (slot + 1) * SUB, :] = value[col_at : col_at + FINE]
         sources = [field[i * SUB : (i + 1) * SUB] for field in fields for i in range(coarse)]

time: 22.8 us -> 22.8 us (level)
  no operation moved by 1% of the time
where the time goes in v8:
time: 22.8 us; the launch traced here: 22.7 us
  Pallas kernels  14.6 us (64%)
  starting transfers between devices  7.6 us (33%)
  waiting for transfers between devices  0.46 us (2%)
    ppermute x4, starting transfers between devices, ring(): lax.ppermute(value, axis, [(i, (i + shift) % count) for i in range(count)])  7.6 us
    pallas_call x1, Pallas kernels, main_part(): pl.pallas_call(main_kernel, in_specs=[vmem] * 3, out_specs=vmem, out_shap...  3.92 us
    pallas_call x1, Pallas kernels, prepare(): pl.pallas_call(prepare_kernel, in_specs=[hbm] * 3, out_specs=[vmem] * len...  3.67 us
    pallas_call x1, Pallas kernels, bands(): pl.pallas_call(bands_kernel, in_specs=[vmem] * 5, out_specs=vmem, out_sha...  3.53 us
    pallas_call x1, Pallas kernels, strips(): pl.pallas_call(strip_kernel, in_specs=[vmem] * 8, out_specs=pl.BlockSpec(...  2.98 us
    pallas_call x1, Pallas kernels, pack_columns(): pl.pallas_call(pack_kernel, in_specs=[vmem] * 5, out_specs=[vmem] * 3, ou...  0.47 us
    ppermute x4, waiting for transfers between devices, ring(): lax.ppermute(value, axis, [(i, (i + shift) % count) for i in range(count)])  0.46 us
  transfers between devices with their start and end apart: 4, of which 1 were waited for; matrix products, arithmetic and copies ran while one was open for 0% of the time, Pallas kernels for 33%

profile of v8, /device:TPU:0, one launch (start us, length us, event | category | flops | bytes accessed | tf_op | source)
XLA Modules:
  0.0 22.7 jit_solution(2953316181568024371)
XLA Ops:
  0.0 3.7 %prepare.1 = (f32[8,512,128]{2,1,0:T(8,128)S(1)}, f32[8,512,128]{2,1,0:T(8,128)S(1)}, f32[3,1040,128]{2,1,0:T(8,128)S(1)}, f32[3,1040,128]{2,1,0:T(8,128)S(1)}, ...) custom-call(f32[512,1024]{1,0:T(8,128)} %elev.1, ...), custom_call_target="tpu_custom_call" | custom-call | tf_op jit(solution)/shard_map/prepare/pallas_call | solution.py:163
  3.7 3.0 %collective-permute-start = (f32[10,16,128]{2,1,0:T(8,128)S(1)}, f32[10,16,128]{2,1,0:T(8,128)S(1)}, u32[]{:S(2)}, u32[]{:S(2)}) collective-permute-start(f32[10,16,128]{2,1,0:T(8,128)S(1)} %get-tuple-element.20), channel_id=1, source_target_pairs={{0,8},{8,16},{16,24},{24,0},{1,9},{9,17},{17,25},{25,1},{2,10},{10... | collective-permute-start | bytes 245768 | tf_op jit(solution)/shard_map/ppermute | solution.py:790
  6.7 1.0 %collective-permute-start.1 = (f32[10,16,128]{2,1,0:T(8,128)S(1)}, f32[10,16,128]{2,1,0:T(8,128)S(1)}, u32[]{:S(2)}, u32[]{:S(2)}) collective-permute-start(f32[10,16,128]{2,1,0:T(8,128)S(1)} %get-tuple-element.21), channel_id=1, source_target_pairs={{0,24},{8,0},{16,8},{24,16},{1,25},{9,1},{17,9},{25,17},{2,26},{10... | collective-permute-start | bytes 245768 | tf_op jit(solution)/shard_map/ppermute | solution.py:790
  7.7 3.9 %middle.1.natural = f32[8,512,128]{2,1,0:T(8,128)S(1)} custom-call(f32[3,1040,128]{2,1,0:T(8,128)S(1)} %get-tuple-element.22.floor_t, f32[3,1040,128]{2,1,0:T(8,128)S(1)} %get-tuple-element.23.lock_t, f32[64,128]{1,0:T(8,128)S(1)} %get-tuple-element.24.stats_t), custom_call_target="tpu_custom_call" | custom-call | flops 100000000 | bytes 20000000 | tf_op jit(solution)/shard_map/middle/pallas_call | solution.py:424
  11.6 0.0 collective-permute-done.from_north
  11.6 0.5 %collective-permute-done.1.from_south = f32[10,16,128]{2,1,0:T(8,128)S(1)} collective-permute-done((f32[10,16,128]{2,1,0:T(8,128)S(1)}, f32[10,16,128]{2,1,0:T(8,128)S(1)}, u32[]{:S(2)}, u32[]{:S(2)}) %collective-permute-start.1) | collective-permute-done | bytes 81952 | tf_op jit(solution)/shard_map/ppermute | solution.py:790
  12.1 0.5 %pack.1 = (f32[96,128]{1,0:T(8,128)S(1)}, f32[96,128]{1,0:T(8,128)S(1)}, f32[2,2,5,128,128]{4,3,2,1,0:T(8,128)S(1)}) custom-call(f32[8,512,128]{2,1,0:T(8,128)S(1)} %get-tuple-element.27.floor.floor_in, f32[8,512,128]{2,1,0:T(8,128)S(1)} %get-tuple-element.28.lock, f32[96,128]{1,0:T(8,128)S(1)} %get-tuple-element.19.stats, ...), custom_call_target="tpu_custom_call" | custom-call | tf_op jit(solution)/shard_map/pack/pallas_call | solution.py:638
  12.6 0.1 collective-permute-start.2
  12.6 3.5 %collective-permute-start.3 = (f32[96,128]{1,0:T(8,128)S(1)}, f32[96,128]{1,0:T(8,128)S(1)}, u32[]{:S(2)}, u32[]{:S(2)}) collective-permute-start(f32[96,128]{1,0:T(8,128)S(1)} %get-tuple-element.31), channel_id=1, source_target_pairs={{0,7},{1,0},{2,1},{3,2},{4,3},{5,4},{6,5},{7,6},{8,15},{9,8},{10,9... | collective-permute-start | bytes 147464 | tf_op jit(solution)/shard_map/ppermute | solution.py:790
  16.2 3.5 %bands.1.banded = f32[2,8,72,128]{3,2,1,0:T(8,128)S(1)} custom-call(f32[8,512,128]{2,1,0:T(8,128)S(1)} %get-tuple-element.27.floor.floor_in, f32[8,512,128]{2,1,0:T(8,128)S(1)} %get-tuple-element.28.lock, f32[96,128]{1,0:T(8,128)S(1)} %get-tuple-element.19.stats, f32[10,16,128]{2,1,0:T(8,128)S(1)} %collective-permute-done.from_north, ...), custom_call_target="tpu_custom_call" | custom-call | flops 60000000 | bytes 12000000 | tf_op jit(solution)/shard_map/bands/pallas_call | solution.py:559
  19.7 0.0 collective-permute-done.2.from_west
  19.7 0.0 collective-permute-done.3.from_east
  19.7 3.0 %strips.1 = f32[512,1024]{1,0:T(8,128)} custom-call(f32[96,128]{1,0:T(8,128)S(1)} %get-tuple-element.19.stats, f32[10,16,128]{2,1,0:T(8,128)S(1)} %collective-permute-done.from_north, f32[10,16,128]{2,1,0:T(8,128)S(1)} %collective-permute-done.1.from_south, f32[2,2,5,128,128]{4,3,2,1,0:T(8,128)S(1)} %get-tuple-element.29.turned, ...), custom_call_target="tpu_custom_call" | custom-call | tf_op jit(solution)/shard_map/strips/pallas_call | solution.py:770
Async XLA Ops:
  3.7 7.9 %collective-permute-start = (f32[10,16,128]{2,1,0:T(8,128)S(1)}, f32[10,16,128]{2,1,0:T(8,128)S(1)}, u32[]{:S(2)}, u32[]{:S(2)}) collective-permute-start(f32[10,16,128]{2,1,0:T(8,128)S(1)} %get-tuple-element.20), channel_id=1, source_target_pairs={{0,8},{8,16},{16,24},{24,0},{1,9},{9,17},{17,25},{25,1},{2,10},{10... | collective-permute-start | bytes 245768 | tf_op jit(solution)/shard_map/ppermute | solution.py:790
  6.7 5.4 %collective-permute-start.1 = (f32[10,16,128]{2,1,0:T(8,128)S(1)}, f32[10,16,128]{2,1,0:T(8,128)S(1)}, u32[]{:S(2)}, u32[]{:S(2)}) collective-permute-start(f32[10,16,128]{2,1,0:T(8,128)S(1)} %get-tuple-element.21), channel_id=1, source_target_pairs={{0,24},{8,0},{16,8},{24,16},{1,25},{9,1},{17,9},{25,17},{2,26},{10... | collective-permute-start | bytes 245768 | tf_op jit(solution)/shard_map/ppermute | solution.py:790
  12.6 7.1 %collective-permute-start.2 = (f32[96,128]{1,0:T(8,128)S(1)}, f32[96,128]{1,0:T(8,128)S(1)}, u32[]{:S(2)}, u32[]{:S(2)}) collective-permute-start(f32[96,128]{1,0:T(8,128)S(1)} %get-tuple-element.30), channel_id=1, source_target_pairs={{0,1},{1,2},{2,3},{3,4},{4,5},{5,6},{6,7},{7,0},{8,9},{9,10},{10,1... | collective-permute-start | bytes 147464 | tf_op jit(solution)/shard_map/ppermute | solution.py:790
  12.6 7.1 %collective-permute-start.3 = (f32[96,128]{1,0:T(8,128)S(1)}, f32[96,128]{1,0:T(8,128)S(1)}, u32[]{:S(2)}, u32[]{:S(2)}) collective-permute-start(f32[96,128]{1,0:T(8,128)S(1)} %get-tuple-element.31), channel_id=1, source_target_pairs={{0,7},{1,0},{2,1},{3,2},{4,3},{5,4},{6,5},{7,6},{8,15},{9,8},{10,9... | collective-permute-start | bytes 147464 | tf_op jit(solution)/shard_map/ppermute | solution.py:790
